TPU v7x, 32 devices: a whole 2x2x4 slice. The times are simulated.
32 devices in a mesh: dp: 8 (over z, x), tensor: 4 (over y, core).
Axes of the slice: x: 2, y: 2, z: 4, core: 2. Of those that a mesh axis runs over, the one named last changes fastest.
Arguments:
- tokens: bfloat16 [4096, 768], P('dp'), may hold values from -6 to 6
- segment_ids: int32 [8, 512], P('dp'), may hold values from 0 to 5, never falling along the last dimension, each value on 1 to 256 neighbouring positions
- cotangent: bfloat16 [4096, 768], P('dp'), may hold values from -6 to 6
- w_qkv: float32 [3, 768, 768], P(None, 'dp', 'tensor'), may hold values from -0.21875 to 0.21875
- w_out: float32 [768, 768], P('tensor', 'dp'), may hold values from -1.75 to 1.75
- w_in: float32 [2, 768, 1152], P(None, 'dp', 'tensor'), may hold values from -0.21875 to 0.21875
- w_down: float32 [1152, 768], P('tensor', 'dp'), may hold values from -0.1875 to 0.1875
- gains: float32 [2, 768], P(None, 'dp'), may hold values from 0.5 to 1.5
- first_qkv: float32 [3, 768, 768], P(None, 'dp', 'tensor'), may hold values from -23.04 to 23.04
- first_out: float32 [768, 768], P('tensor', 'dp'), may hold values from -3.84 to 3.84
- first_in: float32 [2, 768, 1152], P(None, 'dp', 'tensor'), may hold values from -23.04 to 23.04
- first_down: float32 [1152, 768], P('tensor', 'dp'), may hold values from -23.04 to 23.04
- first_gains: float32 [2, 768], P(None, 'dp'), may hold values from -23.04 to 23.04
- second_qkv: float32 [3, 768, 768], P(None, 'dp', 'tensor'), may hold values from 409.6 to 1638.4
- second_out: float32 [768, 768], P('tensor', 'dp'), may hold values from 20.48 to 81.92
- second_in: float32 [2, 768, 1152], P(None, 'dp', 'tensor'), may hold values from 81.92 to 327.68
- second_down: float32 [1152, 768], P('tensor', 'dp'), may hold values from 307.2 to 1228.8
- second_gains: float32 [2, 768], P(None, 'dp'), may hold values from 614.4 to 2457.6
Outputs:
- out_tokens: float32 [4096, 768], P('dp')
- grad_tokens: float32 [4096, 768], P('dp')
- grad_qkv: float32 [3, 768, 768], P(None, 'dp', 'tensor')
- grad_out: float32 [768, 768], P('tensor', 'dp')
- grad_in: float32 [2, 768, 1152], P(None, 'dp', 'tensor')
- grad_down: float32 [1152, 768], P('tensor', 'dp')
- grad_gains: float32 [2, 768], P(None, 'dp')
- delta_qkv: float32 [3, 768, 768], P(None, 'dp', 'tensor')
- delta_out: float32 [768, 768], P('tensor', 'dp')
- delta_in: float32 [2, 768, 1152], P(None, 'dp', 'tensor')
- delta_down: float32 [1152, 768], P('tensor', 'dp')
- delta_gains: float32 [2, 768], P(None, 'dp')
- new_first_qkv: float32 [3, 768, 768], P(None, 'dp', 'tensor')
- new_first_out: float32 [768, 768], P('tensor', 'dp')
- new_first_in: float32 [2, 768, 1152], P(None, 'dp', 'tensor')
- new_first_down: float32 [1152, 768], P('tensor', 'dp')
- new_first_gains: float32 [2, 768], P(None, 'dp')
- new_second_qkv: float32 [3, 768, 768], P(None, 'dp', 'tensor')
- new_second_out: float32 [768, 768], P('tensor', 'dp')
- new_second_in: float32 [2, 768, 1152], P(None, 'dp', 'tensor')
- new_second_down: float32 [1152, 768], P('tensor', 'dp')
- new_second_gains: float32 [2, 768], P(None, 'dp')
Inputs may be any that keep to these rules, and one draw needn't show every extreme that they name: `segment_ids`: along each of the 8 sequences the ids never fall; each document holds 1 to 256 tokens, and one holds exactly 256.
All inputs are finite; a program needn't handle non-finite values.
Results may differ from a plain program's by a relative error of at most 0.018.
Values may be sent and summed in bfloat16 or wider, within the bound.
No kernel may reach another device: no remote copies, remote signals or barrier semaphores. Data moves between devices by JAX's collectives and lax.ppermute only.
A program may use at most 128 MiB of HBM per device.

v0:
```python
import jax
import jax.numpy as jnp
from jax import lax
from jax.sharding import PartitionSpec as P

HEAD_DIM = 64
STEP = 3


norm_eps = 1e-05
rope_base = 160000.0
learn_rate = 0.01
beta_one = 0.9
beta_two = 0.98
adam_eps = 1e-08
decay_rate = 0.01
big_negative = -1e30


def rope_tables(count, head_width):
    half_dim = head_width // 2
    frequency = rope_base ** (-(jnp.arange(half_dim, dtype=jnp.float32) * 2.0 / head_width))
    angles = jnp.arange(count, dtype=jnp.float32)[:, None] * frequency[None, :]
    cosine_table = jnp.concatenate([jnp.cos(angles), jnp.cos(angles)], axis=1)
    sine_values = jnp.concatenate([jnp.sin(angles), jnp.sin(angles)], axis=1)
    return (cosine_table, sine_values)


def rotate_fwd(values, cosine_table, sine_values):
    half_dim = values.shape[-1] // 2
    turned = jnp.concatenate([-values[..., half_dim:], values[..., :half_dim]], axis=-1)
    return values * cosine_table + turned * sine_values


def inverse_rotation(gradient, cosine_table, sine_values):
    half_dim = gradient.shape[-1] // 2
    scaled = gradient * sine_values
    turned = jnp.concatenate([scaled[..., half_dim:], -scaled[..., :half_dim]], axis=-1)
    return gradient * cosine_table + turned


def gelu_parts(inputs):
    normal_cdf = 0.5 * (1.0 + lax.erf(inputs * 0.7071067811865476))
    density = jnp.exp(-0.5 * inputs * inputs) * 0.3989422804014327
    return (inputs * normal_cdf, normal_cdf + inputs * density)


def norm_fwd(values, gain_vec):
    center = values - jnp.mean(values, axis=-1, keepdims=True)
    inverse = lax.rsqrt(jnp.mean(center * center, axis=-1, keepdims=True) + norm_eps)
    normed = center * inverse
    return (normed * gain_vec, normed, inverse)


def norm_back(grad_norm, gain_vec, normed, inverse):
    scaled = grad_norm * gain_vec
    grad_input = (
        scaled
        - jnp.mean(scaled, axis=-1, keepdims=True)
        - normed * jnp.mean(scaled * normed, axis=-1, keepdims=True)
    ) * inverse
    grad_gain = jnp.sum(grad_norm * normed, axis=0)
    return (grad_input, grad_gain)


def adamw(weight, gradient, first_mom, second, decay_now):
    first_new = beta_one * first_mom + (1.0 - beta_one) * gradient
    second_new = beta_two * second + (1.0 - beta_two) * gradient * gradient
    corr_one = 1.0 - beta_one**STEP
    corr_two = 1.0 - beta_two**STEP
    update = (
        first_new / corr_one / (jnp.sqrt(second_new / corr_two) + adam_eps) + decay_now * weight
    )
    return (-learn_rate * update, first_new, second_new)


def local(
    tokens,
    segment_ids,
    cotangent,
    w_qkv,
    w_out,
    w_in,
    w_down,
    gains,
    first_qkv,
    first_out,
    first_in,
    first_down,
    first_gains,
    second_qkv,
    second_out,
    second_in,
    second_down,
    second_gains,
):
    full_qkv, full_out, full_in, full_down, full_gains = (
        lax.all_gather(w_qkv.astype(jnp.bfloat16), "dp", axis=1, tiled=True),
        lax.all_gather(w_out.astype(jnp.bfloat16), "dp", axis=1, tiled=True),
        lax.all_gather(w_in.astype(jnp.bfloat16), "dp", axis=1, tiled=True),
        lax.all_gather(w_down.astype(jnp.bfloat16), "dp", axis=1, tiled=True),
        lax.all_gather(gains.astype(jnp.bfloat16), "dp", axis=1, tiled=True),
    )
    gain_one = full_gains[0].astype(jnp.float32)
    gain_two = full_gains[1].astype(jnp.float32)
    segments = segment_ids[0]
    length = tokens.shape[0]
    head_count = full_qkv.shape[2] // HEAD_DIM
    logit_scale = HEAD_DIM ** (-0.5)
    cosine_table, sine_values = rope_tables(length, HEAD_DIM)
    allowed = (segments[:, None] == segments[None, :])[None]
    stream = tokens.astype(jnp.float32)
    normed_one, hat_one, inv_one = norm_fwd(stream, gain_one)
    in_one = normed_one.astype(jnp.bfloat16)
    projected = jnp.einsum("ld,sde->sle", in_one, full_qkv, preferred_element_type=jnp.float32)
    split_heads = projected.reshape(3, length, head_count, HEAD_DIM).transpose(0, 2, 1, 3)
    query_per_head = rotate_fwd(split_heads[0], cosine_table, sine_values).astype(jnp.bfloat16)
    key_per_head = rotate_fwd(split_heads[1], cosine_table, sine_values).astype(jnp.bfloat16)
    value_per_head = split_heads[2].astype(jnp.bfloat16)
    attention_logits = (
        jnp.einsum("sjr,szr->sjz", query_per_head, key_per_head, preferred_element_type=jnp.float32)
        * logit_scale
    )
    attention_logits = jnp.where(allowed, attention_logits, big_negative)
    row_top = jnp.max(attention_logits, axis=-1, keepdims=True)
    expd = jnp.exp(attention_logits - row_top)
    row_total = jnp.sum(expd, axis=-1, keepdims=True)
    log_total = row_top + jnp.log(row_total)
    softmax_probs_narrow = (expd / row_total).astype(jnp.bfloat16)
    attended_values = jnp.einsum(
        "sur,srk->suk", softmax_probs_narrow, value_per_head, preferred_element_type=jnp.float32
    ).astype(jnp.bfloat16)
    merged = attended_values.transpose(1, 0, 2).reshape(length, head_count * HEAD_DIM)
    attn_part = jnp.dot(merged, full_out, preferred_element_type=jnp.float32)
    middle = stream + lax.psum(attn_part, "tensor")
    normed_two, hat_two, inv_two = norm_fwd(middle, gain_two)
    in_two = normed_two.astype(jnp.bfloat16)
    lifted = jnp.einsum("ld,sdf->slf", in_two, full_in, preferred_element_type=jnp.float32)
    gelu_val, gelu_slope = gelu_parts(lifted[0])
    hidden = (gelu_val * lifted[1]).astype(jnp.bfloat16)
    mlp_part = jnp.dot(hidden, full_down, preferred_element_type=jnp.float32)
    output = middle + lax.psum(mlp_part.astype(jnp.bfloat16), "tensor").astype(jnp.float32)
    grad_down = jnp.einsum("lf,ld->fd", hidden, cotangent, preferred_element_type=jnp.float32)
    grad_hidden = jnp.einsum("ld,fd->lf", cotangent, full_down, preferred_element_type=jnp.float32)
    grad_up = jnp.stack([grad_hidden * lifted[1] * gelu_slope, grad_hidden * gelu_val]).astype(
        jnp.bfloat16
    )
    grad_in = jnp.einsum("ld,slf->sdf", in_two, grad_up, preferred_element_type=jnp.float32)
    two_part = jnp.einsum("slf,sdf->ld", grad_up, full_in, preferred_element_type=jnp.float32)
    grad_two = lax.psum(two_part.astype(jnp.bfloat16), "tensor").astype(jnp.float32)
    back_two, gain_two_part = norm_back(grad_two, gain_two, hat_two, inv_two)
    grad_middle = cotangent.astype(jnp.float32) + back_two
    middle_low = grad_middle.astype(jnp.bfloat16)
    grad_out = jnp.einsum("le,ld->ed", merged, middle_low, preferred_element_type=jnp.float32)
    grad_merged = jnp.einsum(
        "ld,ed->le", middle_low, full_out, preferred_element_type=jnp.float32
    ).astype(jnp.bfloat16)
    attended_gradient = grad_merged.reshape(length, head_count, HEAD_DIM).transpose(1, 0, 2)
    again = (
        jnp.einsum("sjr,szr->sjz", query_per_head, key_per_head, preferred_element_type=jnp.float32)
        * logit_scale
    )
    again = jnp.where(allowed, again, big_negative)
    soft_again = jnp.exp(again - log_total)
    value_gradient = jnp.einsum(
        "xuy,xup->xyp", softmax_probs_narrow, attended_gradient, preferred_element_type=jnp.float32
    )
    softmax_gradient = jnp.einsum(
        "sjr,szr->sjz", attended_gradient, value_per_head, preferred_element_type=jnp.float32
    )
    delta_rows = jnp.sum(
        attended_gradient.astype(jnp.float32) * attended_values.astype(jnp.float32),
        axis=-1,
        keepdims=True,
    )
    score_gradient = (soft_again * (softmax_gradient - delta_rows) * logit_scale).astype(
        jnp.bfloat16
    )
    query_gradient = inverse_rotation(
        jnp.einsum(
            "sur,srk->suk", score_gradient, key_per_head, preferred_element_type=jnp.float32
        ),
        cosine_table,
        sine_values,
    )
    key_gradient = inverse_rotation(
        jnp.einsum(
            "xuy,xup->xyp", score_gradient, query_per_head, preferred_element_type=jnp.float32
        ),
        cosine_table,
        sine_values,
    )
    grad_proj = jnp.stack([query_gradient, key_gradient, value_gradient]).astype(jnp.bfloat16)
    grad_proj = grad_proj.transpose(0, 2, 1, 3).reshape(3, length, head_count * HEAD_DIM)
    grad_qkv = jnp.einsum("ld,sle->sde", in_one, grad_proj, preferred_element_type=jnp.float32)
    one_part = jnp.einsum("sle,sde->ld", grad_proj, full_qkv, preferred_element_type=jnp.float32)
    grad_one = lax.psum(one_part.astype(jnp.bfloat16), "tensor").astype(jnp.float32)
    back_one, grad_gain_one = norm_back(grad_one, gain_one, hat_one, inv_one)
    grad_tokens = grad_middle + back_one
    share_qkv, share_out, share_in, share_down, share_one, share_two = (
        lax.psum_scatter(grad_qkv, "dp", scatter_dimension=1, tiled=True),
        lax.psum_scatter(grad_out, "dp", scatter_dimension=1, tiled=True),
        lax.psum_scatter(grad_in, "dp", scatter_dimension=1, tiled=True),
        lax.psum_scatter(grad_down, "dp", scatter_dimension=1, tiled=True),
        lax.psum_scatter(grad_gain_one, "dp", scatter_dimension=0, tiled=True),
        lax.psum_scatter(gain_two_part, "dp", scatter_dimension=0, tiled=True),
    )
    share_gains = jnp.stack([share_one, share_two])
    n_qkv, m_qkv, s_qkv = adamw(w_qkv, share_qkv, first_qkv, second_qkv, decay_rate)
    n_out, m_out, s_out = adamw(w_out, share_out, first_out, second_out, decay_rate)
    n_in, m_in, s_in = adamw(w_in, share_in, first_in, second_in, decay_rate)
    n_down, m_down, s_down = adamw(w_down, share_down, first_down, second_down, decay_rate)
    n_gains, m_gains, s_gains = adamw(gains, share_gains, first_gains, second_gains, 0.0)
    return (
        output,
        grad_tokens,
        share_qkv,
        share_out,
        share_in,
        share_down,
        share_gains,
        n_qkv,
        n_out,
        n_in,
        n_down,
        n_gains,
        m_qkv,
        m_out,
        m_in,
        m_down,
        m_gains,
        s_qkv,
        s_out,
        s_in,
        s_down,
        s_gains,
    )


def solution(mesh):
    placed = (
        P("dp", None),
        P("dp", None),
        P("dp", None),
        P(None, "dp", "tensor"),
        P("tensor", "dp"),
        P(None, "dp", "tensor"),
        P("tensor", "dp"),
        P(None, "dp"),
        P(None, "dp", "tensor"),
        P("tensor", "dp"),
        P(None, "dp", "tensor"),
        P("tensor", "dp"),
        P(None, "dp"),
        P(None, "dp", "tensor"),
        P("tensor", "dp"),
        P(None, "dp", "tensor"),
        P("tensor", "dp"),
        P(None, "dp"),
    )
    return jax.shard_map(
        local,
        mesh=mesh,
        in_specs=placed,
        out_specs=(
            P("dp", None),
            P("dp", None),
            P(None, "dp", "tensor"),
            P("tensor", "dp"),
            P(None, "dp", "tensor"),
            P("tensor", "dp"),
            P(None, "dp"),
            P(None, "dp", "tensor"),
            P("tensor", "dp"),
            P(None, "dp", "tensor"),
            P("tensor", "dp"),
            P(None, "dp"),
            P(None, "dp", "tensor"),
            P("tensor", "dp"),
            P(None, "dp", "tensor"),
            P("tensor", "dp"),
            P(None, "dp"),
            P(None, "dp", "tensor"),
            P("tensor", "dp"),
            P(None, "dp", "tensor"),
            P("tensor", "dp"),
            P(None, "dp"),
        ),
        check_vma=False,
    )
```

profile of v0, /device:TPU:0, one launch (start us, length us, event | category | flops | bytes accessed | tf_op | source)
XLA Modules:
  0.0 554.1 jit_solution(13716953608073374803)
XLA Ops:
  9.5 38.8 %all_gather.16 = bf16[3,768,192]{2,0,1:T(4,128)(2,1)S(1)} all-gather(bf16[3,96,192]{2,0,1:T(4,128)(2,1)S(1)} %copy.116), channel_id=1, replica_groups=mesh['dp'=8,'tensor'=4] {'dp'}, dimensions={1}, use_global_device_ids=true | all-gather | bytes 995328 | tf_op jit(solution)/shard_map/all_gather | solution.py:98
  49.2 18.6 %all-gather = bf16[8,96,2]{1,2,0:T(2,128)(2,1)S(1)} all-gather(bf16[1,96,2]{1,2,0:T(2,128)(2,1)S(1)} %convert_bitcast_fusion), channel_id=1, replica_groups=mesh['dp'=8,'tensor'=4] {'dp'}, dimensions={0}, use_global_device_ids=true | all-gather | bytes 3456 | tf_op jit(solution)/shard_map/all_gather | solution.py:102
  75.1 31.1 %all_gather.17 = bf16[192,768]{0,1:T(8,128)(2,1)S(1)} all-gather(bf16[192,96]{0,1:T(8,128)(2,1)S(1)} %copy.119), channel_id=1, replica_groups=mesh['dp'=8,'tensor'=4] {'dp'}, dimensions={1}, use_global_device_ids=true | all-gather | bytes 331776 | tf_op jit(solution)/shard_map/all_gather | solution.py:99
  108.9 34.3 %all_gather.19 = bf16[288,768]{0,1:T(8,128)(2,1)} all-gather(bf16[288,96]{0,1:T(8,128)(2,1)S(1)} %copy.122), channel_id=1, replica_groups=mesh['dp'=8,'tensor'=4] {'dp'}, dimensions={1}, use_global_device_ids=true | all-gather | bytes 497664 | tf_op jit(solution)/shard_map/all_gather | solution.py:101
  143.2 32.4 %all_gather.18 = bf16[2,768,288]{2,0,1:T(2,128)(2,1)S(1)} all-gather(bf16[2,96,288]{2,0,1:T(2,128)(2,1)S(1)} %copy.163), channel_id=1, replica_groups=mesh['dp'=8,'tensor'=4] {'dp'}, dimensions={1}, use_global_device_ids=true | all-gather | bytes 995328 | tf_op jit(solution)/shard_map/all_gather | solution.py:100
  183.1 2.4 convolution_convert_fusion
  185.5 29.4 %all-reduce.10.cloned.1.call-done = bf16[512,768]{1,0:T(8,128)(2,1)} async-done(((bf16[512,768]{1,0:T(8,128)(2,1)}), bf16[512,768]{1,0:T(8,128)(2,1)}) %all-reduce.10.cloned.1.call-update) | async-done | bytes 786448 | tf_op jit(solution)/shard_map/psum | solution.py:150
  214.9 2.0 fusion.21
  220.5 2.3 multiply_convert_fusion
  229.5 3.0 convolution_bitcast_fusion.3
  232.6 3.0 convolution_bitcast_fusion
  235.7 5.1 copy.152
  240.8 3.9 reshape.164
  245.4 3.4 convolution_bitcast_fusion.1
  248.8 4.2 copy.148
  253.1 4.7 reshape.160
  269.3 2.0 all-reduce.12.cloned.1.call-done
  271.3 2.2 fusion.23
  273.5 21.9 %all-reduce.2 = (f32[768]{0:T(1024)S(1)}, f32[768]{0:T(1024)S(1)}) all-reduce(f32[768]{0:T(1024)S(1)} %get-tuple-element.110, f32[768]{0:T(1024)S(1)} %get-tuple-element.112), channel_id=7, replica_groups=mesh['dp'=8,'tensor'=4] {'dp'}, use_global_device_ids=true, to_apply=%region_22.23.clone | all-reduce | flops 1536 | bytes 12288
  296.2 2.5 convert_add_fusion.1
  300.5 36.5 %reduce-scatter.15.cloned.1.call-done = f32[96,192]{1,0:T(8,128)} async-done(((f32[768,192]{1,0:T(8,128)}), f32[96,192]{1,0:T(8,128)}) %reduce-scatter.15.cloned.1.call-update) | async-done | bytes 73744
  338.8 64.9 %reduce-scatter.19.cloned.1.call-done = f32[96,288]{1,0:T(8,128)} async-done(((f32[768,288]{1,0:T(8,128)}), f32[96,288]{1,0:T(8,128)}) %reduce-scatter.19.cloned.1.call-update) | async-done | bytes 110608
  405.6 67.8 %reduce-scatter.17.cloned.1.call-done = f32[96,576]{1,0:T(8,128)} async-done(((f32[768,576]{1,0:T(8,128)}), f32[96,576]{1,0:T(8,128)}) %reduce-scatter.17.cloned.1.call-update) | async-done | bytes 221200
  478.4 63.9 %reduce-scatter.13.cloned.1.call-done = f32[96,576]{1,0:T(8,128)} async-done(((f32[768,576]{1,0:T(8,128)}), f32[96,576]{1,0:T(8,128)}) %reduce-scatter.13.cloned.1.call-update) | async-done | bytes 221200
  (223 shorter events, 57.9 us)
Async XLA Ops:
  7.2 168.4 %all-reduce.8.cloned.1.call-start = ((), (), s32[]{:S(2)}) async-start(), calls=%async_computation.4 | async-start | bytes 3145728 | tf_op jit(solution)/shard_map/psum | solution.py:135
  8.2 63.5 %copy-start.6 = (pred[512,512]{0,1:T(8,128)(4,1)}, pred[512,512]{0,1:T(8,128)(4,1)S(1)}, u32[]{:S(2)}) copy-start(pred[512,512]{0,1:T(8,128)(4,1)S(1)} %broadcast_compare_fusion) | copy-start | bytes 786436
  74.0 34.5 %copy-start.4 = (bf16[3,512,512]{1,2,0:T(8,128)(2,1)}, bf16[3,512,512]{1,2,0:T(8,128)(2,1)S(1)}, u32[]{:S(2)}) copy-start(bf16[3,512,512]{1,2,0:T(8,128)(2,1)S(1)} %divide_convert_fusion) | copy-start | bytes 4718596
  75.0 33.5 %copy-start.11 = (bf16[3,512,64]{1,2,0:T(8,128)(2,1)}, bf16[3,512,64]{1,2,0:T(8,128)(2,1)S(1)}, u32[]{:S(2)}) copy-start(bf16[3,512,64]{1,2,0:T(8,128)(2,1)S(1)} %convolution_convert_fusion.1) | copy-start | bytes 589828
  108.5 106.4 %all-reduce.10.cloned.1.call-start = ((), (), s32[]{:S(2)}) async-start(), calls=%async_computation.5 | async-start | bytes 1572864 | tf_op jit(solution)/shard_map/psum | solution.py:150
  177.6 37.4 %copy-start.51 = (f32[512]{0:T(512)}, f32[512]{0:T(512)S(1)}, u32[]{:S(2)}) copy-start(f32[512]{0:T(512)S(1)} %add_rsqrt_fusion) | copy-start | bytes 6148
  182.8 88.5 %all-reduce.12.cloned.1.call-start = ((), (), s32[]{:S(2)}) async-start(), calls=%async_computation.10 | async-start | bytes 3145728 | tf_op jit(solution)/shard_map/psum | solution.py:142
  228.0 109.0 %reduce-scatter.15.cloned.1.call-start = ((), (), s32[]{:S(2)}) async-start(), calls=%async_computation.7 | async-start | bytes 884736
  229.5 174.3 %reduce-scatter.19.cloned.1.call-start = ((), (), s32[]{:S(2)}) async-start(), calls=%async_computation.9 | async-start | bytes 1327104
  232.5 240.8 %reduce-scatter.17.cloned.1.call-start = ((), (), s32[]{:S(2)}) async-start(), calls=%async_computation.8 | async-start | bytes 2211840
  244.8 297.5 %reduce-scatter.13.cloned.1.call-start = ((), (), s32[]{:S(2)}) async-start(), calls=%async_computation.6 | async-start | bytes 2211840
  298.7 39.3 %copy-start.40 = (f32[192,96]{1,0:T(8,128)S(1)}, f32[192,96]{1,0:T(8,128)}, u32[]{:S(2)}) copy-start(f32[192,96]{1,0:T(8,128)} %param.22) | copy-start | bytes 221188
  298.7 39.3 %copy-start.47 = (f32[192,96]{1,0:T(8,128)S(1)}, f32[192,96]{1,0:T(8,128)}, u32[]{:S(2)}) copy-start(f32[192,96]{1,0:T(8,128)} %param.27) | copy-start | bytes 221188
  298.7 39.3 %copy-start.48 = (f32[192,96]{1,0:T(8,128)S(1)}, f32[192,96]{1,0:T(8,128)}, u32[]{:S(2)}) copy-start(f32[192,96]{1,0:T(8,128)} %param.32) | copy-start | bytes 221188
  298.7 106.0 %copy-start.37 = (f32[288,96]{1,0:T(8,128)S(1)}, f32[288,96]{1,0:T(8,128)}, u32[]{:S(2)}) copy-start(f32[288,96]{1,0:T(8,128)} %param.24) | copy-start | bytes 331780
  298.8 106.0 %copy-start.45 = (f32[288,96]{1,0:T(8,128)S(1)}, f32[288,96]{1,0:T(8,128)}, u32[]{:S(2)}) copy-start(f32[288,96]{1,0:T(8,128)} %param.29) | copy-start | bytes 331780
  298.8 106.0 %copy-start.46 = (f32[288,96]{1,0:T(8,128)S(1)}, f32[288,96]{1,0:T(8,128)}, u32[]{:S(2)}) copy-start(f32[288,96]{1,0:T(8,128)} %param.34) | copy-start | bytes 331780
  338.0 137.3 %copy-start.41 = (f32[192,96]{1,0:T(8,128)}, f32[192,96]{1,0:T(8,128)S(1)}, u32[]{:S(2)}) copy-start(f32[192,96]{1,0:T(8,128)S(1)} %copy.151) | copy-start | bytes 221188
  338.8 136.7 %copy-start.28 = (f32[2,96,288]{1,2,0:T(8,128)S(1)}, f32[2,96,288]{1,2,0:T(8,128)}, u32[]{:S(2)}) copy-start(f32[2,96,288]{1,2,0:T(8,128)} %copy.134) | copy-start | bytes 663556
  338.8 136.7 %copy-start.29 = (f32[2,96,288]{1,2,0:T(8,128)S(1)}, f32[2,96,288]{1,2,0:T(8,128)}, u32[]{:S(2)}) copy-start(f32[2,96,288]{1,2,0:T(8,128)} %copy.132) | copy-start | bytes 663556
  338.8 136.7 %copy-start.30 = (f32[2,96,288]{1,2,0:T(8,128)S(1)}, f32[2,96,288]{1,2,0:T(8,128)}, u32[]{:S(2)}) copy-start(f32[2,96,288]{1,2,0:T(8,128)} %copy.133) | copy-start | bytes 663556
  404.8 71.0 %copy-start.38 = (f32[288,96]{1,0:T(8,128)}, f32[288,96]{1,0:T(8,128)S(1)}, u32[]{:S(2)}) copy-start(f32[288,96]{1,0:T(8,128)S(1)} %copy.155) | copy-start | bytes 331780
  476.6 67.7 %copy-start.26 = (f32[3,96,192]{1,2,0:T(8,128)S(1)}, f32[3,96,192]{1,2,0:T(8,128)}, u32[]{:S(2)}) copy-start(f32[3,96,192]{1,2,0:T(8,128)} %copy.131) | copy-start | bytes 663556
  476.6 67.7 %copy-start.27 = (f32[3,96,192]{1,2,0:T(8,128)S(1)}, f32[3,96,192]{1,2,0:T(8,128)}, u32[]{:S(2)}) copy-start(f32[3,96,192]{1,2,0:T(8,128)} %copy.130) | copy-start | bytes 663556
  (47 other events, 207.4 us)
Sparse Core Ops, SparseCore 0:
  108.6 40.3 all-reduce.7
  182.9 31.9 all-reduce.9
  228.1 43.1 all-reduce.11
  274.4 62.5 reduce-scatter.14
  340.6 63.0 reduce-scatter.18
  407.5 65.8 reduce-scatter.16
  476.9 65.3 reduce-scatter.12
where the time goes:
time: 555 us; the launch traced here: 554 us
  waiting for transfers between devices  265 us (48%)
  blocking collectives  177 us (32%)
  local copies, waits for them, and re-layouts  49.9 us (9%)
  matrix products  26.7 us (5%)
  other arithmetic  19.7 us (4%)
  between operations  15.7 us (3%)
    unnamed x11, waiting for transfers between devices  233 us
    unnamed x157, local copies, waits for them, and re-layouts  48.6 us
    all_gather x1, blocking collectives, local(): lax.all_gather(w_qkv.astype(jnp.bfloat16), 'dp', axis=1, tiled=True)  38.8 us
    all_gather x1, blocking collectives, local(): lax.all_gather(w_down.astype(jnp.bfloat16), 'dp', axis=1, tiled=True)  34.3 us
    all_gather x1, blocking collectives, local(): lax.all_gather(w_in.astype(jnp.bfloat16), 'dp', axis=1, tiled=True)  32.4 us
    all_gather x1, blocking collectives, local(): lax.all_gather(w_out.astype(jnp.bfloat16), 'dp', axis=1, tiled=True)  31.1 us
    psum x1, waiting for transfers between devices, local(): lax.psum(two_part.astype(jnp.bfloat16), 'tensor').astype(jnp.float32)  29.4 us
    unnamed x1, blocking collectives  21.9 us
  transfers between devices with their start and end apart: 7, of which 6 were waited for; matrix products, arithmetic and copies ran while one was open for 10% of the time, Pallas kernels for 0%

commit v1 on v0

v1 whole, which is shorter than its diff:
```python
import jax
import jax.numpy as jnp
from jax import lax
from jax.sharding import PartitionSpec as P

HEAD_DIM = 64
STEP = 3


norm_eps = 1e-05
rope_base = 160000.0
learn_rate = 0.01
beta_one = 0.9
beta_two = 0.98
adam_eps = 1e-08
decay_rate = 0.01
big_negative = -1e30

BF = jnp.bfloat16
F32 = jnp.float32


def rope_tables(count, head_width):
    half_dim = head_width // 2
    frequency = rope_base ** (-(jnp.arange(half_dim, dtype=jnp.float32) * 2.0 / head_width))
    angles = jnp.arange(count, dtype=jnp.float32)[:, None] * frequency[None, :]
    cosine_table = jnp.concatenate([jnp.cos(angles), jnp.cos(angles)], axis=1)
    sine_values = jnp.concatenate([jnp.sin(angles), jnp.sin(angles)], axis=1)
    return (cosine_table, sine_values)


def rotate_fwd(values, cosine_table, sine_values):
    half_dim = values.shape[-1] // 2
    turned = jnp.concatenate([-values[..., half_dim:], values[..., :half_dim]], axis=-1)
    return values * cosine_table + turned * sine_values


def inverse_rotation(gradient, cosine_table, sine_values):
    half_dim = gradient.shape[-1] // 2
    scaled = gradient * sine_values
    turned = jnp.concatenate([scaled[..., half_dim:], -scaled[..., :half_dim]], axis=-1)
    return gradient * cosine_table + turned


def gelu_parts(inputs):
    normal_cdf = 0.5 * (1.0 + lax.erf(inputs * 0.7071067811865476))
    density = jnp.exp(-0.5 * inputs * inputs) * 0.3989422804014327
    return (inputs * normal_cdf, normal_cdf + inputs * density)


def norm_fwd(values, gain_vec):
    center = values - jnp.mean(values, axis=-1, keepdims=True)
    inverse = lax.rsqrt(jnp.mean(center * center, axis=-1, keepdims=True) + norm_eps)
    normed = center * inverse
    return (normed * gain_vec, normed, inverse)


def norm_back(grad_norm, gain_vec, normed, inverse):
    scaled = grad_norm * gain_vec
    return (
        scaled
        - jnp.mean(scaled, axis=-1, keepdims=True)
        - normed * jnp.mean(scaled * normed, axis=-1, keepdims=True)
    ) * inverse


def adamw(weight, gradient, first_mom, second, decay_now):
    first_new = beta_one * first_mom + (1.0 - beta_one) * gradient
    second_new = beta_two * second + (1.0 - beta_two) * gradient * gradient
    corr_one = 1.0 - beta_one**STEP
    corr_two = 1.0 - beta_two**STEP
    update = (
        first_new / corr_one / (jnp.sqrt(second_new / corr_two) + adam_eps) + decay_now * weight
    )
    return (-learn_rate * update, first_new, second_new)


def swap(values, axis, mask):
    count = lax.axis_size(axis)
    return lax.ppermute(values, axis, [(i, i ^ mask) for i in range(count)])


def place_blocks(pieces, masks, index):
    out = jnp.zeros((len(pieces),) + pieces[0].shape, pieces[0].dtype)
    for piece, mask in zip(pieces, masks):
        out = lax.dynamic_update_slice(out, piece[None], (index ^ mask, 0, 0))
    return out


def gather_direct(shard):
    count = lax.axis_size("dp")
    if count != 8:
        return lax.all_gather(shard, "dp", axis=0, tiled=True)
    index = lax.axis_index("dp")
    order = (1, 2, 4, 3, 6, 5, 7)
    pieces = [shard] + [swap(shard, "dp", m) for m in order]
    out = place_blocks(pieces, (0,) + order, index)
    return out.reshape(count * shard.shape[0], shard.shape[1])


def gather_two_level(shard):
    count = lax.axis_size("dp")
    if count != 8:
        return lax.all_gather(shard, "dp", axis=0, tiled=True)
    index = lax.axis_index("dp")
    order = (2, 4, 6)
    pieces = [shard] + [swap(shard, "dp", m) for m in order]
    column = place_blocks(pieces, (0, 1, 2, 3), index // 2)
    other = swap(column, "dp", 1)
    odd = index % 2
    low = jnp.where(odd == 0, column, other)
    high = jnp.where(odd == 0, other, column)
    return jnp.stack([low, high], axis=1).reshape(count * shard.shape[0], shard.shape[1])


def scatter_two_level(grad):
    count = lax.axis_size("dp")
    if count != 8:
        return lax.psum_scatter(grad.astype(F32), "dp", scatter_dimension=0, tiled=True)
    index = lax.axis_index("dp")
    odd, level = index % 2, index // 2
    rows = grad.shape[0] // count
    blocks = grad.reshape(count // 2, 2, rows, grad.shape[1])
    keep = lax.dynamic_index_in_dim(blocks, odd, 1, keepdims=False)
    send = lax.dynamic_index_in_dim(blocks, 1 - odd, 1, keepdims=False)
    pair = (keep.astype(F32) + swap(send, "dp", 1).astype(F32)).astype(BF)
    total = lax.dynamic_index_in_dim(pair, level, 0, keepdims=False).astype(F32)
    for m in (1, 2, 3):
        part = lax.dynamic_index_in_dim(pair, level ^ m, 0, keepdims=False)
        total = total + swap(part, "dp", 2 * m).astype(F32)
    return total


def reduce_tensor(part):
    count = lax.axis_size("tensor")
    if count != 4:
        return lax.psum(part.astype(F32), "tensor")
    half = part.shape[0] // 2
    core = lax.axis_index("tensor") % 2
    low = part.astype(BF)
    mine = lax.dynamic_slice_in_dim(low, core * half, half, 0)
    theirs = lax.dynamic_slice_in_dim(low, (1 - core) * half, half, 0)
    chip = (mine.astype(F32) + swap(theirs, "tensor", 1).astype(F32)).astype(BF)
    total = chip.astype(F32) + swap(chip, "tensor", 2).astype(F32)
    other = swap(total, "tensor", 1)
    return jnp.where(
        core == 0,
        jnp.concatenate([total, other], axis=0),
        jnp.concatenate([other, total], axis=0),
    )


def local(
    tokens,
    segment_ids,
    cotangent,
    w_qkv,
    w_out,
    w_in,
    w_down,
    gains,
    first_qkv,
    first_out,
    first_in,
    first_down,
    first_gains,
    second_qkv,
    second_out,
    second_in,
    second_down,
    second_gains,
):
    head_total = w_qkv.shape[2]
    hidden_total = w_in.shape[2]
    shard_a = jnp.concatenate(
        [w_qkv[0], w_qkv[1], w_qkv[2], gains[0][:, None]], axis=1
    ).astype(BF)
    shard_b = jnp.concatenate(
        [w_in[0], w_in[1], w_out.T, w_down.T, gains[1][:, None]], axis=1
    ).astype(BF)
    full_a = gather_direct(shard_a)
    full_b = gather_two_level(shard_b)
    wide = 3 * head_total
    full_qkv = full_a[:, :wide]
    gain_one = full_a[:, wide].astype(F32)
    full_in = full_b[:, : 2 * hidden_total]
    at = 2 * hidden_total
    full_out = full_b[:, at : at + head_total]
    at = at + head_total
    full_down = full_b[:, at : at + hidden_total]
    at = at + hidden_total
    gain_two = full_b[:, at].astype(F32)

    segments = segment_ids[0]
    length = tokens.shape[0]
    head_count = head_total // HEAD_DIM
    logit_scale = HEAD_DIM ** (-0.5)
    cosine_table, sine_values = rope_tables(length, HEAD_DIM)
    allowed = (segments[:, None] == segments[None, :])[None]
    stream = tokens.astype(F32)
    normed_one, hat_one, inv_one = norm_fwd(stream, gain_one)
    in_one = normed_one.astype(BF)
    projected = jnp.dot(in_one, full_qkv, preferred_element_type=F32)
    split_heads = projected.reshape(length, 3, head_count, HEAD_DIM).transpose(1, 2, 0, 3)
    query_per_head = rotate_fwd(split_heads[0], cosine_table, sine_values).astype(BF)
    key_per_head = rotate_fwd(split_heads[1], cosine_table, sine_values).astype(BF)
    value_per_head = split_heads[2].astype(BF)
    attention_logits = (
        jnp.einsum("sjr,szr->sjz", query_per_head, key_per_head, preferred_element_type=F32)
        * logit_scale
    )
    attention_logits = jnp.where(allowed, attention_logits, big_negative)
    row_top = jnp.max(attention_logits, axis=-1, keepdims=True)
    expd = jnp.exp(attention_logits - row_top)
    row_total = jnp.sum(expd, axis=-1, keepdims=True)
    log_total = row_top + jnp.log(row_total)
    softmax_probs_narrow = (expd / row_total).astype(BF)
    attended_values = jnp.einsum(
        "sur,srk->suk", softmax_probs_narrow, value_per_head, preferred_element_type=F32
    ).astype(BF)
    merged = attended_values.transpose(1, 0, 2).reshape(length, head_total)
    attn_part = jnp.einsum("le,de->ld", merged, full_out, preferred_element_type=F32)
    middle = stream + reduce_tensor(attn_part)
    normed_two, hat_two, inv_two = norm_fwd(middle, gain_two)
    in_two = normed_two.astype(BF)
    lifted = jnp.dot(in_two, full_in, preferred_element_type=F32)
    lift_up, lift_gate = lifted[:, :hidden_total], lifted[:, hidden_total:]
    gelu_val, gelu_slope = gelu_parts(lift_up)
    hidden = (gelu_val * lift_gate).astype(BF)
    grad_hidden = jnp.dot(cotangent, full_down, preferred_element_type=F32)
    grad_up = jnp.concatenate(
        [grad_hidden * lift_gate * gelu_slope, grad_hidden * gelu_val], axis=1
    ).astype(BF)
    two_part = jnp.einsum("lf,df->ld", grad_up, full_in, preferred_element_type=F32)
    grad_two = reduce_tensor(two_part)
    mlp_part = jnp.einsum("lf,df->ld", hidden, full_down, preferred_element_type=F32)
    output = middle + reduce_tensor(mlp_part)
    grad_ffn = jnp.concatenate(
        [
            jnp.einsum("ld,lf->df", in_two, grad_up, preferred_element_type=F32),
            jnp.einsum("ld,lf->df", cotangent, hidden, preferred_element_type=F32),
            jnp.sum(two_part * hat_two, axis=0)[:, None],
        ],
        axis=1,
    ).astype(BF)
    share_ffn = scatter_two_level(grad_ffn)

    grad_middle = cotangent.astype(F32) + norm_back(grad_two, gain_two, hat_two, inv_two)
    middle_low = grad_middle.astype(BF)
    grad_out = jnp.einsum("ld,le->de", middle_low, merged, preferred_element_type=F32)
    grad_merged = jnp.dot(middle_low, full_out, preferred_element_type=F32).astype(BF)
    attended_gradient = grad_merged.reshape(length, head_count, HEAD_DIM).transpose(1, 0, 2)
    again = (
        jnp.einsum("sjr,szr->sjz", query_per_head, key_per_head, preferred_element_type=F32)
        * logit_scale
    )
    again = jnp.where(allowed, again, big_negative)
    soft_again = jnp.exp(again - log_total)
    value_gradient = jnp.einsum(
        "xuy,xup->xyp", softmax_probs_narrow, attended_gradient, preferred_element_type=F32
    )
    softmax_gradient = jnp.einsum(
        "sjr,szr->sjz", attended_gradient, value_per_head, preferred_element_type=F32
    )
    delta_rows = jnp.sum(
        attended_gradient.astype(F32) * attended_values.astype(F32),
        axis=-1,
        keepdims=True,
    )
    score_gradient = (soft_again * (softmax_gradient - delta_rows) * logit_scale).astype(BF)
    query_gradient = inverse_rotation(
        jnp.einsum("sur,srk->suk", score_gradient, key_per_head, preferred_element_type=F32),
        cosine_table,
        sine_values,
    )
    key_gradient = inverse_rotation(
        jnp.einsum("xuy,xup->xyp", score_gradient, query_per_head, preferred_element_type=F32),
        cosine_table,
        sine_values,
    )
    grad_proj = jnp.stack([query_gradient, key_gradient, value_gradient]).astype(BF)
    grad_proj = grad_proj.transpose(2, 0, 1, 3).reshape(length, wide)
    one_part = jnp.einsum("le,de->ld", grad_proj, full_qkv, preferred_element_type=F32)
    grad_attn = jnp.concatenate(
        [
            jnp.einsum("ld,le->de", in_one, grad_proj, preferred_element_type=F32),
            grad_out,
            jnp.sum(one_part * hat_one, axis=0)[:, None],
        ],
        axis=1,
    ).astype(BF)
    share_attn = scatter_two_level(grad_attn)
    grad_one = reduce_tensor(one_part)
    grad_tokens = grad_middle + norm_back(grad_one, gain_one, hat_one, inv_one)

    share_qkv = jnp.stack([share_attn[:, i * head_total : (i + 1) * head_total] for i in range(3)])
    share_out = share_attn[:, wide : wide + head_total].T
    share_in = jnp.stack([share_ffn[:, i * hidden_total : (i + 1) * hidden_total] for i in range(2)])
    share_down = share_ffn[:, 2 * hidden_total : 3 * hidden_total].T
    share_gains = jnp.stack([share_attn[:, wide + head_total], share_ffn[:, 3 * hidden_total]])
    if lax.axis_size("tensor") == 4:
        share_gains = share_gains + swap(share_gains, "tensor", 1)
        share_gains = share_gains + swap(share_gains, "tensor", 2)
    else:
        share_gains = lax.psum(share_gains, "tensor")
    n_qkv, m_qkv, s_qkv = adamw(w_qkv, share_qkv, first_qkv, second_qkv, decay_rate)
    n_out, m_out, s_out = adamw(w_out, share_out, first_out, second_out, decay_rate)
    n_in, m_in, s_in = adamw(w_in, share_in, first_in, second_in, decay_rate)
    n_down, m_down, s_down = adamw(w_down, share_down, first_down, second_down, decay_rate)
    n_gains, m_gains, s_gains = adamw(gains, share_gains, first_gains, second_gains, 0.0)
    return (
        output,
        grad_tokens,
        share_qkv,
        share_out,
        share_in,
        share_down,
        share_gains,
        n_qkv,
        n_out,
        n_in,
        n_down,
        n_gains,
        m_qkv,
        m_out,
        m_in,
        m_down,
        m_gains,
        s_qkv,
        s_out,
        s_in,
        s_down,
        s_gains,
    )


def solution(mesh):
    placed = (
        P("dp", None),
        P("dp", None),
        P("dp", None),
        P(None, "dp", "tensor"),
        P("tensor", "dp"),
        P(None, "dp", "tensor"),
        P("tensor", "dp"),
        P(None, "dp"),
        P(None, "dp", "tensor"),
        P("tensor", "dp"),
        P(None, "dp", "tensor"),
        P("tensor", "dp"),
        P(None, "dp"),
        P(None, "dp", "tensor"),
        P("tensor", "dp"),
        P(None, "dp", "tensor"),
        P("tensor", "dp"),
        P(None, "dp"),
    )
    return jax.shard_map(
        local,
        mesh=mesh,
        in_specs=placed,
        out_specs=(
            P("dp", None),
            P("dp", None),
            P(None, "dp", "tensor"),
            P("tensor", "dp"),
            P(None, "dp", "tensor"),
            P("tensor", "dp"),
            P(None, "dp"),
            P(None, "dp", "tensor"),
            P("tensor", "dp"),
            P(None, "dp", "tensor"),
            P("tensor", "dp"),
            P(None, "dp"),
            P(None, "dp", "tensor"),
            P("tensor", "dp"),
            P(None, "dp", "tensor"),
            P("tensor", "dp"),
            P(None, "dp"),
            P(None, "dp", "tensor"),
            P("tensor", "dp"),
            P(None, "dp", "tensor"),
            P("tensor", "dp"),
            P(None, "dp"),
        ),
        check_vma=False,
    )
```

time: 555 us -> 234 us (0.42)
  blocking collectives: 177 us -> 0 us
  waiting for transfers between devices: 265 us -> 95.8 us
  starting transfers between devices: 0.47 us -> 39.9 us
  between operations: 15.7 us -> 2.04 us
  other arithmetic: 19.7 us -> 29.5 us
  matrix products: 26.7 us -> 19.1 us
    unnamed x11 -> x0, waiting for transfers between devices: 233 us -> none
    all_gather x5 -> x0, blocking collectives: 155 us -> none  [the longest x1 38.8 us: local(): lax.all_gather(w_qkv.astype(jnp.bfloat16), 'dp', axis=1, tiled=True)]
    ppermute x0 -> x33, waiting for transfers between devices: none -> 95.8 us  [swap(): return lax.ppermute(values, axis, [(i, i ^ mask) for i in range(count)])]
    ppermute x0 -> x33, starting transfers between devices: none -> 39.9 us  [swap(): return lax.ppermute(values, axis, [(i, i ^ mask) for i in range(count)])]
    psum x3 -> x0, waiting for transfers between devices: 31.3 us -> none  [the longest x1 29.4 us: local(): lax.psum(two_part.astype(jnp.bfloat16), 'tensor').astype(jnp.float32)]
    unnamed x157 -> x154, local copies, waits for them, and re-layouts: 48.6 us -> 23.9 us
    unnamed x1 -> x0, blocking collectives: 21.9 us -> none
    dot_general x0 -> x2, other arithmetic: none -> 5.82 us  [the longest x1 3.19 us: local(): jnp.einsum('ld,le->de', in_one, grad_proj, preferred_element_type=F32)]
  transfers between devices with their start and end apart: 7 -> 33, of which waited for: 6 -> 16; matrix products, arithmetic and copies ran while one was open for 10% -> 26% of each run, Pallas kernels for 0% -> 0%
where the time goes in v1:
time: 234 us; the launch traced here: 233 us
  waiting for transfers between devices  95.8 us (41%)
  local copies, waits for them, and re-layouts  46.8 us (20%)
  starting transfers between devices  39.9 us (17%)
  other arithmetic  29.5 us (13%)
  matrix products  19.1 us (8%)
    ppermute x33, waiting for transfers between devices, swap(): return lax.ppermute(values, axis, [(i, i ^ mask) for i in range(count)])  95.8 us
    ppermute x33, starting transfers between devices, swap(): return lax.ppermute(values, axis, [(i, i ^ mask) for i in range(count)])  39.9 us
    unnamed x154, local copies, waits for them, and re-layouts  23.9 us
    broadcast_in_dim x3, local copies, waits for them, and re-layouts, place_blocks(): out = lax.dynamic_update_slice(out, piece[None], (index ^ mask, 0, 0))  5.4 us
    dynamic_update_slice x11, local copies, waits for them, and re-layouts, place_blocks(): out = lax.dynamic_update_slice(out, piece[None], (index ^ mask, 0, 0))  5.08 us
  transfers between devices with their start and end apart: 33, of which 16 were waited for; matrix products, arithmetic and copies ran while one was open for 26% of the time, Pallas kernels for 0%

profile of v1, /device:TPU:0, one launch (start us, length us, event | category | flops | bytes accessed | tf_op | source)
XLA Modules:
  0.0 233.1 jit_solution(15480174479798753142)
XLA Ops:
  2.7 3.0 %collective-permute-start = (bf16[96,577]{1,0:T(8,128)(2,1)S(1)}, bf16[96,577]{1,0:T(8,128)(2,1)S(1)}, u32[]{:S(2)}, u32[]{:S(2)}) collective-permute-start(bf16[96,577]{1,0:T(8,128)(2,1)S(1)} %pad_maximum_fusion.11), channel_id=1, source_target_pairs={{0,4},{4,0},{8,12},{12,8},{16,20},{20,16},{24,28},{28,24},{1,5},{5... | collective-permute-start | bytes 332360 | tf_op jit(solution)/shard_map/ppermute | solution.py:80
  7.3 2.6 %collective-permute-start.2 = (bf16[96,577]{1,0:T(8,128)(2,1)S(1)}, bf16[96,577]{1,0:T(8,128)(2,1)S(1)}, u32[]{:S(2)}, u32[]{:S(2)}) collective-permute-start(bf16[96,577]{1,0:T(8,128)(2,1)S(1)} %pad_maximum_fusion.11), channel_id=1, source_target_pairs={{0,16},{4,20},{8,24},{12,28},{16,0},{20,4},{24,8},{28,12},{1,17},{... | collective-permute-start | bytes 332360 | tf_op jit(solution)/shard_map/ppermute | solution.py:80
  18.0 2.7 %collective-permute-start.5 = (bf16[96,577]{1,0:T(8,128)(2,1)S(1)}, bf16[96,577]{1,0:T(8,128)(2,1)S(1)}, u32[]{:S(2)}, u32[]{:S(2)}) collective-permute-start(bf16[96,577]{1,0:T(8,128)(2,1)S(1)} %pad_maximum_fusion.11), channel_id=1, source_target_pairs={{0,20},{4,16},{8,28},{12,24},{16,4},{20,0},{24,12},{28,8},{1,21},{... | collective-permute-start | bytes 332360 | tf_op jit(solution)/shard_map/ppermute | solution.py:80
  22.7 2.7 %collective-permute-start.8 = (bf16[96,1057]{0,1:T(8,128)(2,1)}, bf16[96,1057]{0,1:T(8,128)(2,1)}, u32[]{:S(2)}, u32[]{:S(2)}) collective-permute-start(bf16[96,1057]{0,1:T(8,128)(2,1)} %constant_dynamic-update-slice_fusion.1), channel_id=1, source_target_pairs={{0,16},{4,20},{8,24},{12,28},{16,0},{20,4},{24,8},{28,12},{1,17},{... | collective-permute-start | bytes 608840 | tf_op jit(solution)/shard_map/ppermute | solution.py:80
  26.3 3.5 %collective-permute-done.5 = bf16[96,577]{1,0:T(8,128)(2,1)S(1)} collective-permute-done((bf16[96,577]{1,0:T(8,128)(2,1)S(1)}, bf16[96,577]{1,0:T(8,128)(2,1)S(1)}, u32[]{:S(2)}, u32[]{:S(2)}) %collective-permute-start.5) | collective-permute-done | bytes 110816 | tf_op jit(solution)/shard_map/ppermute | solution.py:80
  36.8 13.3 %collective-permute-done.8 = bf16[96,1057]{0,1:T(8,128)(2,1)} collective-permute-done((bf16[96,1057]{0,1:T(8,128)(2,1)}, bf16[96,1057]{0,1:T(8,128)(2,1)}, u32[]{:S(2)}, u32[]{:S(2)}) %collective-permute-start.8) | collective-permute-done | bytes 202976 | tf_op jit(solution)/shard_map/ppermute | solution.py:80
  61.8 16.5 %collective-permute-done.10 = bf16[4,96,1057]{2,1,0:T(8,128)(2,1)S(1)} collective-permute-done((bf16[4,96,1057]{2,1,0:T(8,128)(2,1)}, bf16[4,96,1057]{2,1,0:T(8,128)(2,1)S(1)}, u32[]{:S(2)}, u32[]{:S(2)}) %collective-permute-start.10) | collective-permute-done | bytes 811808 | tf_op jit(solution)/shard_map/ppermute | solution.py:80
  84.9 9.6 %collective-permute-done.12 = bf16[256,768]{1,0:T(8,128)(2,1)S(1)} collective-permute-done((bf16[256,768]{1,0:T(8,128)(2,1)S(1)}, bf16[256,768]{1,0:T(8,128)(2,1)S(1)}, u32[]{:S(2)}, u32[]{:S(2)}) %collective-permute-start.12) | collective-permute-done | bytes 393248 | tf_op jit(solution)/shard_map/ppermute | solution.py:80
  95.8 2.4 %collective-permute-done.13 = f32[256,768]{1,0:T(8,128)} collective-permute-done((f32[256,768]{1,0:T(8,128)}, f32[256,768]{1,0:T(8,128)}, u32[]{:S(2)}, u32[]{:S(2)}) %collective-permute-start.13) | collective-permute-done | bytes 786464 | tf_op jit(solution)/shard_map/ppermute | solution.py:80
  98.1 2.3 fusion.75
  108.0 8.7 %collective-permute-done.18 = bf16[256,768]{1,0:T(8,128)(2,1)S(1)} collective-permute-done((bf16[256,768]{1,0:T(8,128)(2,1)S(1)}, bf16[256,768]{1,0:T(8,128)(2,1)S(1)}, u32[]{:S(2)}, u32[]{:S(2)}) %collective-permute-start.18) | collective-permute-done | bytes 393248 | tf_op jit(solution)/shard_map/ppermute | solution.py:80
  118.6 10.0 %collective-permute-done.15 = bf16[256,768]{1,0:T(8,128)(2,1)S(1)} collective-permute-done((bf16[256,768]{1,0:T(8,128)(2,1)S(1)}, bf16[256,768]{1,0:T(8,128)(2,1)S(1)}, u32[]{:S(2)}, u32[]{:S(2)}) %collective-permute-start.15) | collective-permute-done | bytes 393248 | tf_op jit(solution)/shard_map/ppermute | solution.py:80
  131.0 2.6 %convert_bitcast_fusion = (bf16[768,512]{0,1:T(8,128)(2,1)}, f32[512,768]{1,0:T(8,128)S(1)}, f32[512,768]{1,0:T(8,128)}) fusion(f32[512]{0:T(512)S(1)} %broadcast_multiply_fusion.4, f32[512]{0:T(512)S(1)} %add_rsqrt_fusion, f32[512,768]{1,0:T(8,128)S(1)} %get-tuple-element.115, f32[512]{0:T(512)S(1)} %broadcast_multiply_fusion.6, ...), kind=kLoop, calls=%fused_computation.108 | loop fusion | flops 6684672 | bytes 9448449 | tf_op jit(solution)/shard_map/ld,le->de/dot_general | solution.py:250
  136.2 2.3 multiply_convert_fusion
  144.3 2.9 %convolution_convert_fusion.1 = bf16[768,576]{0,1:T(8,128)(2,1)} fusion(bf16[512,288]{0,1:T(8,128)(2,1)} %copy-done.49, bf16[512,288]{0,1:T(8,128)(2,1)} %copy-done.48, f32[512,768]{1,0:T(8,128)S(1)} %get-tuple-element.115, f32[768]{0:T(1024)S(1)} %copy-done.51, f32[512]{0:T(512)S(1)} %copy-done.57, f32[512]{0:T(512)S(1)} %copy-done.53), kind=kOutput, calls=%fused_computation.37 | convolution fusion | flops 456179712 | bytes 3054592 | tf_op jit(solution)/shard_map/ld,lf->df/dot_general | solution.py:240
  150.3 2.3 copy.117
  156.4 3.5 %collective-permute-done.21 = bf16[256,768]{1,0:T(8,128)(2,1)} collective-permute-done((bf16[256,768]{1,0:T(8,128)(2,1)S(1)}, bf16[256,768]{1,0:T(8,128)(2,1)}, u32[]{:S(2)}, u32[]{:S(2)}) %collective-permute-start.21) | collective-permute-done | bytes 393248 | tf_op jit(solution)/shard_map/ppermute | solution.py:80
  171.0 2.3 copy.115
  177.1 4.6 %collective-permute-start.28 = (bf16[96,865]{1,0:T(8,128)(2,1)}, bf16[96,865]{1,0:T(8,128)(2,1)}, u32[]{:S(2)}, u32[]{:S(2)}) collective-permute-start(bf16[96,865]{1,0:T(8,128)(2,1)} %get-tuple-element.128), channel_id=1, source_target_pairs={{0,8},{4,12},{8,0},{12,4},{16,24},{20,28},{24,16},{28,20},{1,9},{5... | collective-permute-start | bytes 498248 | tf_op jit(solution)/shard_map/ppermute | solution.py:80
  187.4 3.2 %fusion.68 = (bf16[768,512]{0,1:T(8,128)(2,1)S(1)}, f32[512,768]{1,0:T(8,128)}) fusion(f32[768]{0:T(1024)S(1)} %copy-done.55, f32[512]{0:T(512)S(1)} %copy-done.61, f32[512]{0:T(512)S(1)} %copy-done.59, bf16[512,768]{1,0:T(8,128)(2,1)S(1)} %copy-done.3, f32[512,768]{1,0:T(8,128)S(1)} %copy-done.5, f32[512]{0:T(512)S(1)} %broadcast_multiply_fusion.2, ...), kind=kLoop, calls=%fused_computation.215 | loop fusion | flops 5505024 | bytes 6302721 | tf_op jit(solution)/shard_map/ld,le->de/dot_general | solution.py:286
  193.3 4.4 %collective-permute-done.30 = bf16[96,865]{1,0:T(8,128)(2,1)} collective-permute-done((bf16[96,865]{1,0:T(8,128)(2,1)}, bf16[96,865]{1,0:T(8,128)(2,1)}, u32[]{:S(2)}, u32[]{:S(2)}) %collective-permute-start.30) | collective-permute-done | bytes 166112 | tf_op jit(solution)/shard_map/ppermute | solution.py:80
  200.2 10.1 %collective-permute-done.23 = bf16[4,96,769]{2,1,0:T(8,128)(2,1)S(1)} collective-permute-done((bf16[4,96,769]{2,1,0:T(8,128)(2,1)S(1)}, bf16[4,96,769]{2,1,0:T(8,128)(2,1)S(1)}, u32[]{:S(2)}, u32[]{:S(2)}) %collective-permute-start.23) | collective-permute-done | bytes 590624 | tf_op jit(solution)/shard_map/ppermute | solution.py:80
  211.1 2.3 %collective-permute-start.25 = (bf16[96,769]{1,0:T(8,128)(2,1)S(1)}, bf16[96,769]{1,0:T(8,128)(2,1)S(1)}, u32[]{:S(2)}, u32[]{:S(2)}) collective-permute-start(bf16[96,769]{1,0:T(8,128)(2,1)S(1)} %get-tuple-element.133), channel_id=1, source_target_pairs={{0,16},{4,20},{8,24},{12,28},{16,0},{20,4},{24,8},{28,12},{1,17},{... | collective-permute-start | bytes 442952 | tf_op jit(solution)/shard_map/ppermute | solution.py:80
  219.0 7.1 %collective-permute-done.25 = bf16[96,769]{1,0:T(8,128)(2,1)S(1)} collective-permute-done((bf16[96,769]{1,0:T(8,128)(2,1)S(1)}, bf16[96,769]{1,0:T(8,128)(2,1)S(1)}, u32[]{:S(2)}, u32[]{:S(2)}) %collective-permute-start.25) | collective-permute-done | bytes 147680 | tf_op jit(solution)/shard_map/ppermute | solution.py:80
  (318 shorter events, 106.2 us)
Async XLA Ops:
  2.7 15.3 %collective-permute-start = (bf16[96,577]{1,0:T(8,128)(2,1)S(1)}, bf16[96,577]{1,0:T(8,128)(2,1)S(1)}, u32[]{:S(2)}, u32[]{:S(2)}) collective-permute-start(bf16[96,577]{1,0:T(8,128)(2,1)S(1)} %pad_maximum_fusion.11), channel_id=1, source_target_pairs={{0,4},{4,0},{8,12},{12,8},{16,20},{20,16},{24,28},{28,24},{1,5},{5... | collective-permute-start | bytes 332360 | tf_op jit(solution)/shard_map/ppermute | solution.py:80
  5.7 15.0 %collective-permute-start.1 = (bf16[96,577]{1,0:T(8,128)(2,1)S(1)}, bf16[96,577]{1,0:T(8,128)(2,1)S(1)}, u32[]{:S(2)}, u32[]{:S(2)}) collective-permute-start(bf16[96,577]{1,0:T(8,128)(2,1)S(1)} %pad_maximum_fusion.11), channel_id=1, source_target_pairs={{0,8},{4,12},{8,0},{12,4},{16,24},{20,28},{24,16},{28,20},{1,9},{5... | collective-permute-start | bytes 332360 | tf_op jit(solution)/shard_map/ppermute | solution.py:80
  7.3 14.4 %collective-permute-start.2 = (bf16[96,577]{1,0:T(8,128)(2,1)S(1)}, bf16[96,577]{1,0:T(8,128)(2,1)S(1)}, u32[]{:S(2)}, u32[]{:S(2)}) collective-permute-start(bf16[96,577]{1,0:T(8,128)(2,1)S(1)} %pad_maximum_fusion.11), channel_id=1, source_target_pairs={{0,16},{4,20},{8,24},{12,28},{16,0},{20,4},{24,8},{28,12},{1,17},{... | collective-permute-start | bytes 332360 | tf_op jit(solution)/shard_map/ppermute | solution.py:80
  9.8 12.8 %collective-permute-start.3 = (bf16[96,577]{1,0:T(8,128)(2,1)S(1)}, bf16[96,577]{1,0:T(8,128)(2,1)S(1)}, u32[]{:S(2)}, u32[]{:S(2)}) collective-permute-start(bf16[96,577]{1,0:T(8,128)(2,1)S(1)} %pad_maximum_fusion.11), channel_id=1, source_target_pairs={{0,12},{4,8},{8,4},{12,0},{16,28},{20,24},{24,20},{28,16},{1,13},{... | collective-permute-start | bytes 332360 | tf_op jit(solution)/shard_map/ppermute | solution.py:80
  10.3 15.1 %collective-permute-start.4 = (bf16[96,577]{1,0:T(8,128)(2,1)S(1)}, bf16[96,577]{1,0:T(8,128)(2,1)S(1)}, u32[]{:S(2)}, u32[]{:S(2)}) collective-permute-start(bf16[96,577]{1,0:T(8,128)(2,1)S(1)} %pad_maximum_fusion.11), channel_id=1, source_target_pairs={{0,24},{4,28},{8,16},{12,20},{16,8},{20,12},{24,0},{28,4},{1,25},{... | collective-permute-start | bytes 332360 | tf_op jit(solution)/shard_map/ppermute | solution.py:80
  18.0 11.9 %collective-permute-start.5 = (bf16[96,577]{1,0:T(8,128)(2,1)S(1)}, bf16[96,577]{1,0:T(8,128)(2,1)S(1)}, u32[]{:S(2)}, u32[]{:S(2)}) collective-permute-start(bf16[96,577]{1,0:T(8,128)(2,1)S(1)} %pad_maximum_fusion.11), channel_id=1, source_target_pairs={{0,20},{4,16},{8,28},{12,24},{16,4},{20,0},{24,12},{28,8},{1,21},{... | collective-permute-start | bytes 332360 | tf_op jit(solution)/shard_map/ppermute | solution.py:80
  20.7 9.2 %collective-permute-start.6 = (bf16[96,577]{1,0:T(8,128)(2,1)S(1)}, bf16[96,577]{1,0:T(8,128)(2,1)S(1)}, u32[]{:S(2)}, u32[]{:S(2)}) collective-permute-start(bf16[96,577]{1,0:T(8,128)(2,1)S(1)} %pad_maximum_fusion.11), channel_id=1, source_target_pairs={{0,28},{4,24},{8,20},{12,16},{16,12},{20,8},{24,4},{28,0},{1,29},{... | collective-permute-start | bytes 332360 | tf_op jit(solution)/shard_map/ppermute | solution.py:80
  21.7 13.4 %collective-permute-start.7 = (bf16[96,1057]{0,1:T(8,128)(2,1)}, bf16[96,1057]{0,1:T(8,128)(2,1)}, u32[]{:S(2)}, u32[]{:S(2)}) collective-permute-start(bf16[96,1057]{0,1:T(8,128)(2,1)} %constant_dynamic-update-slice_fusion.1), channel_id=1, source_target_pairs={{0,8},{4,12},{8,0},{12,4},{16,24},{20,28},{24,16},{28,20},{1,9},{5... | collective-permute-start | bytes 608840 | tf_op jit(solution)/shard_map/ppermute | solution.py:80
  22.7 27.4 %collective-permute-start.8 = (bf16[96,1057]{0,1:T(8,128)(2,1)}, bf16[96,1057]{0,1:T(8,128)(2,1)}, u32[]{:S(2)}, u32[]{:S(2)}) collective-permute-start(bf16[96,1057]{0,1:T(8,128)(2,1)} %constant_dynamic-update-slice_fusion.1), channel_id=1, source_target_pairs={{0,16},{4,20},{8,24},{12,28},{16,0},{20,4},{24,8},{28,12},{1,17},{... | collective-permute-start | bytes 608840 | tf_op jit(solution)/shard_map/ppermute | solution.py:80
  25.4 26.6 %collective-permute-start.9 = (bf16[96,1057]{0,1:T(8,128)(2,1)}, bf16[96,1057]{0,1:T(8,128)(2,1)}, u32[]{:S(2)}, u32[]{:S(2)}) collective-permute-start(bf16[96,1057]{0,1:T(8,128)(2,1)} %constant_dynamic-update-slice_fusion.1), channel_id=1, source_target_pairs={{0,24},{4,28},{8,16},{12,20},{16,8},{20,12},{24,0},{28,4},{1,25},{... | collective-permute-start | bytes 608840 | tf_op jit(solution)/shard_map/ppermute | solution.py:80
  58.6 19.7 %collective-permute-start.10 = (bf16[4,96,1057]{2,1,0:T(8,128)(2,1)}, bf16[4,96,1057]{2,1,0:T(8,128)(2,1)S(1)}, u32[]{:S(2)}, u32[]{:S(2)}) collective-permute-start(bf16[4,96,1057]{2,1,0:T(8,128)(2,1)} %constant_dynamic-update-slice_fusion.2), channel_id=1, source_target_pairs={{0,4},{4,0},{8,12},{12,8},{16,20},{20,16},{24,28},{28,24},{1,5},{5... | collective-permute-start | bytes 2435336 | tf_op jit(solution)/shard_map/ppermute | solution.py:80
  83.3 11.2 %collective-permute-start.12 = (bf16[256,768]{1,0:T(8,128)(2,1)S(1)}, bf16[256,768]{1,0:T(8,128)(2,1)S(1)}, u32[]{:S(2)}, u32[]{:S(2)}) collective-permute-start(bf16[256,768]{1,0:T(8,128)(2,1)S(1)} %add_convert_fusion.3), channel_id=1, source_target_pairs={{0,2},{1,3},{2,0},{3,1},{4,6},{5,7},{6,4},{7,5},{8,10},{9,11},{10,... | collective-permute-start | bytes 1179656 | tf_op jit(solution)/shard_map/ppermute | solution.py:80
  105.5 11.2 %collective-permute-start.18 = (bf16[256,768]{1,0:T(8,128)(2,1)S(1)}, bf16[256,768]{1,0:T(8,128)(2,1)S(1)}, u32[]{:S(2)}, u32[]{:S(2)}) collective-permute-start(bf16[256,768]{1,0:T(8,128)(2,1)S(1)} %add_convert_fusion.1), channel_id=1, source_target_pairs={{0,2},{1,3},{2,0},{3,1},{4,6},{5,7},{6,4},{7,5},{8,10},{9,11},{10,... | collective-permute-start | bytes 1179656 | tf_op jit(solution)/shard_map/ppermute | solution.py:80
  116.8 11.9 %collective-permute-start.19 = (f32[256,768]{1,0:T(8,128)S(1)}, f32[256,768]{1,0:T(8,128)S(1)}, u32[]{:S(2)}, u32[]{:S(2)}) collective-permute-start(f32[256,768]{1,0:T(8,128)S(1)} %convert_add_fusion.4), channel_id=1, source_target_pairs={{0,1},{1,0},{2,3},{3,2},{4,5},{5,4},{6,7},{7,6},{8,9},{9,8},{10,11... | collective-permute-start | bytes 2359304 | tf_op jit(solution)/shard_map/ppermute | solution.py:80
  117.0 11.6 %collective-permute-start.15 = (bf16[256,768]{1,0:T(8,128)(2,1)S(1)}, bf16[256,768]{1,0:T(8,128)(2,1)S(1)}, u32[]{:S(2)}, u32[]{:S(2)}) collective-permute-start(bf16[256,768]{1,0:T(8,128)(2,1)S(1)} %add_convert_fusion.2), channel_id=1, source_target_pairs={{0,2},{1,3},{2,0},{3,1},{4,6},{5,7},{6,4},{7,5},{8,10},{9,11},{10,... | collective-permute-start | bytes 1179656 | tf_op jit(solution)/shard_map/ppermute | solution.py:80
  148.3 11.6 %collective-permute-start.21 = (bf16[256,768]{1,0:T(8,128)(2,1)S(1)}, bf16[256,768]{1,0:T(8,128)(2,1)}, u32[]{:S(2)}, u32[]{:S(2)}) collective-permute-start(bf16[256,768]{1,0:T(8,128)(2,1)S(1)} %add_convert_fusion), channel_id=1, source_target_pairs={{0,2},{1,3},{2,0},{3,1},{4,6},{5,7},{6,4},{7,5},{8,10},{9,11},{10,... | collective-permute-start | bytes 1179656 | tf_op jit(solution)/shard_map/ppermute | solution.py:80
  155.8 19.1 %collective-permute-start.27 = (bf16[4,96,865]{2,1,0:T(8,128)(2,1)}, bf16[4,96,865]{2,1,0:T(8,128)(2,1)}, u32[]{:S(2)}, u32[]{:S(2)}) collective-permute-start(bf16[4,96,865]{2,1,0:T(8,128)(2,1)} %dynamic-slice_bitcast_fusion), channel_id=1, source_target_pairs={{0,4},{4,0},{8,12},{12,8},{16,20},{20,16},{24,28},{28,24},{1,5},{5... | collective-permute-start | bytes 1992968 | tf_op jit(solution)/shard_map/ppermute | solution.py:80
  161.0 24.2 %collective-permute-start.22 = (f32[256,768]{1,0:T(8,128)S(1)}, f32[256,768]{1,0:T(8,128)}, u32[]{:S(2)}, u32[]{:S(2)}) collective-permute-start(f32[256,768]{1,0:T(8,128)S(1)} %convert_add_fusion.3), channel_id=1, source_target_pairs={{0,1},{1,0},{2,3},{3,2},{4,5},{5,4},{6,7},{7,6},{8,9},{9,8},{10,11... | collective-permute-start | bytes 2359304 | tf_op jit(solution)/shard_map/ppermute | solution.py:80
  177.1 16.1 %collective-permute-start.28 = (bf16[96,865]{1,0:T(8,128)(2,1)}, bf16[96,865]{1,0:T(8,128)(2,1)}, u32[]{:S(2)}, u32[]{:S(2)}) collective-permute-start(bf16[96,865]{1,0:T(8,128)(2,1)} %get-tuple-element.128), channel_id=1, source_target_pairs={{0,8},{4,12},{8,0},{12,4},{16,24},{20,28},{24,16},{28,20},{1,9},{5... | collective-permute-start | bytes 498248 | tf_op jit(solution)/shard_map/ppermute | solution.py:80
  181.8 11.5 %collective-permute-start.29 = (bf16[96,865]{1,0:T(8,128)(2,1)}, bf16[96,865]{1,0:T(8,128)(2,1)}, u32[]{:S(2)}, u32[]{:S(2)}) collective-permute-start(bf16[96,865]{1,0:T(8,128)(2,1)} %get-tuple-element.130), channel_id=1, source_target_pairs={{0,16},{4,20},{8,24},{12,28},{16,0},{20,4},{24,8},{28,12},{1,17},{... | collective-permute-start | bytes 498248 | tf_op jit(solution)/shard_map/ppermute | solution.py:80
  183.7 14.0 %collective-permute-start.30 = (bf16[96,865]{1,0:T(8,128)(2,1)}, bf16[96,865]{1,0:T(8,128)(2,1)}, u32[]{:S(2)}, u32[]{:S(2)}) collective-permute-start(bf16[96,865]{1,0:T(8,128)(2,1)} %get-tuple-element.129), channel_id=1, source_target_pairs={{0,24},{4,28},{8,16},{12,20},{16,8},{20,12},{24,0},{28,4},{1,25},{... | collective-permute-start | bytes 498248 | tf_op jit(solution)/shard_map/ppermute | solution.py:80
  192.9 17.3 %collective-permute-start.23 = (bf16[4,96,769]{2,1,0:T(8,128)(2,1)S(1)}, bf16[4,96,769]{2,1,0:T(8,128)(2,1)S(1)}, u32[]{:S(2)}, u32[]{:S(2)}) collective-permute-start(bf16[4,96,769]{2,1,0:T(8,128)(2,1)S(1)} %dynamic-slice_bitcast_fusion.1), channel_id=1, source_target_pairs={{0,4},{4,0},{8,12},{12,8},{16,20},{20,16},{24,28},{28,24},{1,5},{5... | collective-permute-start | bytes 1771784 | tf_op jit(solution)/shard_map/ppermute | solution.py:80
  211.1 15.0 %collective-permute-start.25 = (bf16[96,769]{1,0:T(8,128)(2,1)S(1)}, bf16[96,769]{1,0:T(8,128)(2,1)S(1)}, u32[]{:S(2)}, u32[]{:S(2)}) collective-permute-start(bf16[96,769]{1,0:T(8,128)(2,1)S(1)} %get-tuple-element.133), channel_id=1, source_target_pairs={{0,16},{4,20},{8,24},{12,28},{16,0},{20,4},{24,8},{28,12},{1,17},{... | collective-permute-start | bytes 442952 | tf_op jit(solution)/shard_map/ppermute | solution.py:80
  213.5 12.7 %collective-permute-start.26 = (bf16[96,769]{1,0:T(8,128)(2,1)S(1)}, bf16[96,769]{1,0:T(8,128)(2,1)S(1)}, u32[]{:S(2)}, u32[]{:S(2)}) collective-permute-start(bf16[96,769]{1,0:T(8,128)(2,1)S(1)} %get-tuple-element.132), channel_id=1, source_target_pairs={{0,24},{4,28},{8,16},{12,20},{16,8},{20,12},{24,0},{28,4},{1,25},{... | collective-permute-start | bytes 442952 | tf_op jit(solution)/shard_map/ppermute | solution.py:80
  (76 other events, 582.8 us)

commit v2 on v0

v2 whole, which is shorter than its diff:
```python
import jax
import jax.numpy as jnp
from jax import lax
from jax.experimental import pallas as pl
from jax.experimental.pallas import tpu as pltpu
from jax.sharding import PartitionSpec as P

HEAD_DIM = 64
STEP = 3


norm_eps = 1e-05
rope_base = 160000.0
learn_rate = 0.01
beta_one = 0.9
beta_two = 0.98
adam_eps = 1e-08
decay_rate = 0.01
big_negative = -1e30

BF = jnp.bfloat16
F32 = jnp.float32


def rope_tables(count, width, deps):
    half_dim = HEAD_DIM // 2
    spot = (jnp.arange(width) % half_dim).astype(jnp.float32)
    frequency = rope_base ** (-(spot * 2.0 / HEAD_DIM))
    place = gate(jnp.arange(count, dtype=jnp.float32)[:, None], deps)
    angles = place * frequency[None, :]
    return (jnp.cos(angles), jnp.sin(angles))


def gelu_parts(inputs):
    normal_cdf = 0.5 * (1.0 + lax.erf(inputs * 0.7071067811865476))
    density = jnp.exp(-0.5 * inputs * inputs) * 0.3989422804014327
    return (inputs * normal_cdf, normal_cdf + inputs * density)


def adamw(weight, gradient, first_mom, second, decay_now):
    first_new = beta_one * first_mom + (1.0 - beta_one) * gradient
    second_new = beta_two * second + (1.0 - beta_two) * gradient * gradient
    corr_one = 1.0 - beta_one**STEP
    corr_two = 1.0 - beta_two**STEP
    update = (
        first_new / corr_one / (jnp.sqrt(second_new / corr_two) + adam_eps) + decay_now * weight
    )
    return (-learn_rate * update, first_new, second_new)


def swap(values, axis, mask):
    count = lax.axis_size(axis)
    return lax.ppermute(values, axis, [(i, i ^ mask) for i in range(count)])


def pack(first, second, gains, row, deps=()):
    rows = first.shape[1]
    used = first.shape[0] * first.shape[2] + second.shape[0] + 1
    width = -(-used // 128) * 128
    return stream(
        lambda *refs: pack_kernel(row, *refs), [((rows, width), BF)], [first, second, gains], smem=0, deps=deps, vmem=16
    )[0]


def gather_pieces(pack_a, pack_b):
    if lax.axis_size("dp") != 8:
        full_a = lax.all_gather(pack_a(()), "dp", axis=0, tiled=True)
        full_b = lax.all_gather(pack_b(()), "dp", axis=0, tiled=True)
        return [full_a], None, [full_b], None, []
    order = (4, 6, 2)
    shard_a, shard_b = pack_a(()), pack_b(())
    far_one, far_two, near = [swap(shard_a, "dp", m) for m in order]
    sides = [swap(piece, "dp", 1) for piece in (shard_a, near, far_one)]
    sides.append(swap(gate(far_two, sides[1:]), "dp", 1))
    pieces_a = [shard_a, near, far_one, far_two] + sides
    masks_a = [[m] for m in (0, 2, 4, 6, 1, 3, 5, 7)]
    shard_b = gate(shard_b, [far_one, far_two])
    column = [swap(shard_b, "dp", m) for m in order]
    side = swap(shard_b, "dp", 1)
    stacked = stack(column)
    pieces_b = [shard_b, stacked, side, swap(stacked, "dp", 1)]
    return pieces_a, masks_a, pieces_b, [[0], [4, 6, 2], [1], [5, 7, 3]], column + [side]


def pair_kernel(where_ref, keep_ref, got_ref, own_ref, *far_refs):
    level = where_ref[0] >> 1
    for m, ref in enumerate((own_ref,) + far_refs):
        at = level ^ m
        ref[...] = (keep_ref[at].astype(F32) + got_ref[at].astype(F32)).astype(BF)


def scatter_start(where, grads, deps=()):
    if len(grads) == 1:
        return [lax.psum_scatter(grads[0].astype(F32), "dp", scatter_dimension=0, tiled=True)], []
    keep, send = grads
    got = swap(gate(send, deps) if deps else send, "dp", 1)
    parts = call(pair_kernel, [(keep.shape[1:], BF)] * keep.shape[0], [where, keep, got])
    return [parts[0]] + [swap(parts[m], "dp", 2 * m) for m in range(1, len(parts))], [got]


def grad_outs(depth, width):
    count = lax.axis_size("dp")
    if count != 8:
        return [((depth, width), BF)]
    return [((count // 2, depth // count, width), BF)] * 2


def emit_grad(where_ref, grad_scr, refs):
    if len(refs) == 1:
        refs[0][...] = grad_scr[...]
        return
    keep_ref, send_ref = refs
    levels, rows, _width = keep_ref.shape
    odd = where_ref[0] & 1
    for level in range(levels):
        at = pl.multiple_of((2 * level + odd) * rows, rows)
        keep_ref[level] = grad_scr[pl.ds(at, rows), :]
        at = pl.multiple_of((2 * level + 1 - odd) * rows, rows)
        send_ref[level] = grad_scr[pl.ds(at, rows), :]


def add_kernel(a_ref, b_ref, out_ref):
    out_ref[...] = (a_ref[...].astype(F32) + b_ref[...].astype(F32)).astype(BF)


def reduce_start(mine, theirs, deps=()):
    got = swap(theirs, "tensor", 1)
    return call(add_kernel, [(mine.shape, BF)], [mine, got], smem=0, deps=deps)[0]


def reduce_finish(chip, deps=()):
    got = swap(chip, "tensor", 2)
    if deps:
        got = gate(got, deps)
    return chip, got, swap(chip, "tensor", 1), swap(got, "tensor", 1)


def dot(a, b):
    return jnp.dot(a, b, preferred_element_type=F32)


def dot_nt(a, b):
    return lax.dot_general(a, b, (((1,), (1,)), ((), ())), preferred_element_type=F32)


def dot_tn(a, b):
    return lax.dot_general(a, b, (((0,), (0,)), ((), ())), preferred_element_type=F32)


def head_mask(rows, width, head):
    lane = lax.broadcasted_iota(jnp.int32, (rows, width), 1)
    return (lane >= head * HEAD_DIM) & (lane < (head + 1) * HEAD_DIM)


def only_head(values, head):
    return jnp.where(head_mask(values.shape[0], values.shape[1], head), values, jnp.zeros_like(values))


def turn_matrix(width):
    half = HEAD_DIM // 2
    source = lax.broadcasted_iota(jnp.int32, (width, width), 0)
    target = lax.broadcasted_iota(jnp.int32, (width, width), 1)
    low = (target & (HEAD_DIM - 1)) < half
    value = jnp.where(low & (source == target + half), -1.0, 0.0)
    return (value + jnp.where((~low) & (source == target - half), 1.0, 0.0)).astype(BF)


def column_as_row(block, lane):
    pick = (lax.broadcasted_iota(jnp.int32, (16, block.shape[1]), 1) == lane).astype(F32).astype(BF)
    return dot_nt(pick, block)[0:1]


def normalize(values):
    center = values - jnp.mean(values, axis=-1, keepdims=True)
    inverse = lax.rsqrt(jnp.mean(center * center, axis=-1, keepdims=True) + norm_eps)
    return center * inverse, inverse


def norm_back(grad_norm, gain_row, normed, inverse):
    scaled = grad_norm * gain_row
    return (
        scaled
        - jnp.mean(scaled, axis=-1, keepdims=True)
        - normed * jnp.mean(scaled * normed, axis=-1, keepdims=True)
    ) * inverse


def place_pieces(where_ref, pieces, masks, out_ref):
    if masks is None:
        out_ref[...] = pieces[0][...]
        return
    for piece, own in zip(pieces, masks):
        rows = piece.shape[-2]
        for i, mask in enumerate(own):
            at = pl.multiple_of((where_ref[0] ^ mask) * rows, rows)
            out_ref[pl.ds(at, rows), :] = piece[i] if len(piece.shape) == 3 else piece[...]


def call(kernel, outs, operands, scratch=(), smem=1, deps=(), vmem=8):
    count = len(operands)

    def body(*refs):
        kernel(*refs[:count], *refs[count + len(deps) :])

    return pl.pallas_call(
        body,
        out_shape=[jax.ShapeDtypeStruct(s, d) for s, d in outs],
        in_specs=[pl.BlockSpec(memory_space=pltpu.SMEM)] * smem
        + [pl.BlockSpec()] * (count - smem)
        + [pl.BlockSpec(memory_space=pl.ANY)] * len(deps),
        out_specs=[pl.BlockSpec()] * len(outs),
        scratch_shapes=list(scratch),
        compiler_params=pltpu.CompilerParams(vmem_limit_bytes=vmem * 1024 * 1024),
    )(*operands, *deps)


def stream(kernel, outs, operands, scratch=(), smem=1, deps=(), vmem=58):
    count, total = len(operands), len(outs)
    late = count - smem
    room = [pltpu.VMEM(x.shape, x.dtype) for x in operands[smem:]] + [pltpu.VMEM(x, d) for x, d in outs]

    def body(*refs):
        given, results = refs[smem:count], refs[count + len(deps) : count + len(deps) + total]
        own = refs[count + len(deps) + total :]
        flags, own = own[-1], own[:-1]
        own, held, made = own[: -late - total], own[-late - total : -total], own[-total:]
        copies = [pltpu.make_async_copy(given[i], held[i], flags.at[i]) for i in range(late)]
        for copy in copies:
            copy.start()
        waiting = {id(ref): copy for ref, copy in zip(held, copies)}
        place = {id(ref): i for i, ref in enumerate(made)}
        sent = []
        shipped = {}

        def ready(*wanted):
            for ref in wanted:
                copy = waiting.pop(id(ref), None)
                if copy is not None:
                    copy.wait()

        def ship(ref, rows=None):
            i = place[id(ref)]
            part = shipped.get(i, 0)
            shipped[i] = part + 1
            source, target = (ref, results[i]) if rows is None else (ref.at[rows], results[i].at[rows])
            copy = pltpu.make_async_copy(source, target, flags.at[late + 2 * i + part])
            copy.start()
            sent.append(copy)

        kernel(ready, ship, *refs[:smem], *held, *made, *own)
        ready(*held)
        for i, ref in enumerate(made):
            if i not in shipped:
                ship(ref)
        for copy in sent:
            copy.wait()

    anywhere = pl.BlockSpec(memory_space=pl.ANY)
    return pl.pallas_call(
        body,
        out_shape=[jax.ShapeDtypeStruct(s, d) for s, d in outs],
        in_specs=[pl.BlockSpec(memory_space=pltpu.SMEM)] * smem + [anywhere] * (late + len(deps)),
        out_specs=[anywhere] * total,
        scratch_shapes=list(scratch) + room + [pltpu.SemaphoreType.DMA((late + 2 * total,))],
        compiler_params=pltpu.CompilerParams(vmem_limit_bytes=vmem * 1024 * 1024),
    )(*operands, *deps)


def gate(value, deps):
    return pl.pallas_call(
        lambda *refs: None,
        out_shape=jax.ShapeDtypeStruct(value.shape, value.dtype),
        in_specs=[pl.BlockSpec(memory_space=pl.ANY)] * (1 + len(deps)),
        out_specs=pl.BlockSpec(memory_space=pl.ANY),
        input_output_aliases={0: 0},
        compiler_params=pltpu.CompilerParams(vmem_limit_bytes=1024 * 1024),
    )(value, *deps)


def pack_kernel(row, ready, ship, first_ref, second_ref, gain_ref, out_ref):
    width = out_ref.shape[1]
    ready(first_ref, second_ref, gain_ref)
    gain = jnp.broadcast_to(gain_ref[row : row + 1, :], (8, gain_ref.shape[1])).T
    parts = [first_ref[i] for i in range(first_ref.shape[0])] + [second_ref[...].T, gain[:, 0:1]]
    used = sum(part.shape[1] for part in parts)
    parts.append(jnp.zeros((out_ref.shape[0], width - used), F32))
    out_ref[...] = jnp.concatenate(parts, axis=1).astype(BF)


def stack(pieces):
    def body(*refs):
        flags = refs[-1]
        copies = [pltpu.make_async_copy(ref, refs[-2].at[i], flags.at[i]) for i, ref in enumerate(refs[:-2])]
        for copy in copies:
            copy.start()
        for copy in copies:
            copy.wait()

    anywhere = pl.BlockSpec(memory_space=pl.ANY)
    return pl.pallas_call(
        body,
        out_shape=jax.ShapeDtypeStruct((len(pieces),) + pieces[0].shape, pieces[0].dtype),
        in_specs=[anywhere] * len(pieces),
        out_specs=anywhere,
        scratch_shapes=[pltpu.SemaphoreType.DMA((len(pieces),))],
        compiler_params=pltpu.CompilerParams(vmem_limit_bytes=1024 * 1024),
    )(*pieces)


CHUNK = 128


def halves(core, length):
    half = length // 2
    return ((False, (1 - core) * half), (True, core * half))


def attention_kernel(masks, count, width, ready, ship, where_ref, tok_ref, segc_ref, segr_ref, cos_ref, sin_ref, *rest):
    pieces = rest[:count]
    n1_ref, q_ref, k_ref, v_ref, o_ref, ab_ref, gain_ref, mine_ref, theirs_ref, full_ref, w_scr, vm_scr = rest[count:]
    length = tok_ref.shape[0]
    heads = width // HEAD_DIM
    ready(*pieces)
    place_pieces(where_ref, pieces, masks, full_ref)
    ship(full_ref)
    gain = column_as_row(full_ref[:, 4 * width :], 0)
    gain_ref[...] = jnp.broadcast_to(gain, gain_ref.shape)
    turn = turn_matrix(width)
    for s in range(3):
        w_scr[s] = full_ref[:, s * width : (s + 1) * width]
    for s in range(2):
        w_scr[3 + s] = dot(w_scr[s], turn).astype(BF)
    w_scr[5] = full_ref[:, 3 * width : 4 * width]
    ready(tok_ref, cos_ref, sin_ref, segc_ref, segr_ref)

    def project(i, _):
        rows = pl.ds(pl.multiple_of(i * CHUNK, CHUNK), CHUNK)
        hat, _unused = normalize(tok_ref[rows, :].astype(F32))
        normed = (hat * gain).astype(BF)
        n1_ref[rows, :] = normed
        cosine, sine = cos_ref[rows, :], sin_ref[rows, :]
        q_ref[rows, :] = (dot(normed, w_scr[0]) * cosine + dot(normed, w_scr[3]) * sine).astype(BF)
        k_ref[rows, :] = (dot(normed, w_scr[1]) * cosine + dot(normed, w_scr[4]) * sine).astype(BF)
        v_ref[rows, :] = dot(normed, w_scr[2]).astype(BF)
        return 0

    lax.fori_loop(0, length // CHUNK, project, 0)
    for ref in (n1_ref, q_ref, k_ref, v_ref):
        ship(ref)
    for h in range(heads):
        vm_scr[h] = only_head(v_ref[...], h)
    core = where_ref[1] & 1
    for is_mine, first in halves(core, length):
        def attend(i, _):
            at = pl.multiple_of(i * CHUNK, CHUNK)
            rows = pl.ds(pl.multiple_of(first + at, CHUNK), CHUNK)
            allowed = segc_ref[rows, :] == segr_ref[...]
            query, keys = q_ref[rows, :], k_ref[...]
            total = jnp.zeros((CHUNK, width), F32)
            for h in range(heads):
                logits = dot_nt(only_head(query, h), keys) * HEAD_DIM ** (-0.5)
                logits = jnp.where(allowed, logits, big_negative)
                expd = jnp.exp(logits - jnp.max(logits, axis=-1, keepdims=True))
                probs = (expd / jnp.sum(expd, axis=-1, keepdims=True)).astype(BF)
                ab_ref[h, rows, :] = probs
                total = total + dot(probs, vm_scr[h])
            attended = total.astype(BF)
            o_ref[rows, :] = attended
            part = dot_nt(attended, w_scr[5]).astype(BF)
            if is_mine:
                mine_ref[pl.ds(at, CHUNK), :] = part
            else:
                theirs_ref[pl.ds(at, CHUNK), :] = part
            return 0

        lax.fori_loop(0, length // 2 // CHUNK, attend, 0)
        ship(mine_ref if is_mine else theirs_ref)


def feed_kernel(masks, count, width, ready, ship, where_ref, tok_ref, cot_ref, a_ref, b_ref, c_ref, d_ref, *rest):
    pieces = rest[:count]
    (h_ref, n2_ref, z_ref, du_ref, dv_ref, gain_ref, mine_ref, theirs_ref, full_ref, w_scr) = rest[count:]
    length = tok_ref.shape[0]
    core = where_ref[1] & 1
    ready(*pieces)
    place_pieces(where_ref, pieces, masks, full_ref)
    ship(full_ref)
    last = 3 * width // 128 * 128
    gain = column_as_row(full_ref[:, last:], 3 * width - last)
    gain_ref[...] = jnp.broadcast_to(gain, gain_ref.shape)
    for s in range(3):
        w_scr[s] = full_ref[:, s * width : (s + 1) * width]
    ready(tok_ref, cot_ref, a_ref, b_ref, c_ref, d_ref)
    for is_mine, first in halves(core, length):
        low, high = (a_ref, b_ref) if is_mine else (c_ref, d_ref)

        def step(i, _):
            at = pl.multiple_of(i * CHUNK, CHUNK)
            rows = pl.ds(pl.multiple_of(first + at, CHUNK), CHUNK)
            here = pl.ds(at, CHUNK)
            middle = tok_ref[rows, :].astype(F32) + (low[here, :].astype(F32) + high[here, :].astype(F32))
            h_ref[rows, :] = middle
            hat, _unused = normalize(middle)
            normed = (hat * gain).astype(BF)
            n2_ref[rows, :] = normed
            up, gate = dot(normed, w_scr[0]), dot(normed, w_scr[1])
            value, slope = gelu_parts(up)
            z_ref[rows, :] = (value * gate).astype(BF)
            back = dot(cot_ref[rows, :], w_scr[2])
            du, dv = (back * gate * slope).astype(BF), (back * value).astype(BF)
            du_ref[rows, :] = du
            dv_ref[rows, :] = dv
            part = dot_nt(du, w_scr[0]) + dot_nt(dv, w_scr[1])
            part = part.astype(BF)
            if is_mine:
                mine_ref[here, :] = part
            else:
                theirs_ref[here, :] = part
            return 0

        lax.fori_loop(0, length // 2 // CHUNK, step, 0)
        rows = pl.ds(pl.multiple_of(first, length // 2), length // 2)
        for ref in (h_ref, n2_ref, z_ref, du_ref, dv_ref):
            ship(ref, rows)
        ship(mine_ref if is_mine else theirs_ref)


def feed_grad_kernel(width, ready, ship, where_ref, n2_ref, cot_ref, z_ref, du_ref, dv_ref, full_ref, mine_ref, theirs_ref, *rest):
    grad_ref, w_scr = rest[-2:]
    ready(n2_ref, du_ref)
    grad_ref[:, 0:width] = dot_tn(n2_ref[...], du_ref[...]).astype(BF)
    ready(dv_ref)
    grad_ref[:, width : 2 * width] = dot_tn(n2_ref[...], dv_ref[...]).astype(BF)
    ready(cot_ref, z_ref)
    grad_ref[:, 2 * width : 3 * width] = dot_tn(cot_ref[...], z_ref[...]).astype(BF)
    emit_grad(where_ref, grad_ref, rest[:-2])
    for ref in rest[:-2]:
        ship(ref)
    ready(full_ref)
    w_scr[...] = full_ref[:, 2 * width : 3 * width]
    length = z_ref.shape[0]
    core = where_ref[1] & 1
    for is_mine, first in halves(core, length):
        rows = pl.ds(pl.multiple_of(first, length // 2), length // 2)
        part = dot_nt(z_ref[rows, :], w_scr[...]).astype(BF)
        if is_mine:
            mine_ref[...] = part
        else:
            theirs_ref[...] = part


SPAN = 256


def back_kernel(width, ready, ship, where_ref, a_ref, b_ref, c_ref, d_ref, h_ref, cot_ref, gain_ref, full_ref, q_ref, k_ref, v_ref, o_ref, ab_ref,
                n1_ref, cos_ref, sin_ref, om_ref, ot_ref, dh_ref, mine_ref, theirs_ref, *rest):
    grad_ref, low_scr, do_scr, w_scr, km_scr, qm_scr, dk_scr, dv_scr, dp_scr = rest[-9:]
    length = h_ref.shape[0]
    half = length // 2
    heads = width // HEAD_DIM
    core = where_ref[1] & 1
    ready(gain_ref, full_ref, a_ref, b_ref, c_ref, d_ref, h_ref, cot_ref)
    gain = gain_ref[0:1, :]
    for s in range(4):
        w_scr[s] = full_ref[:, s * width : (s + 1) * width]
    for is_mine, first in halves(core, length):
        low, high = (a_ref, b_ref) if is_mine else (c_ref, d_ref)

        def step(i, _):
            at = pl.multiple_of(i * CHUNK, CHUNK)
            rows = pl.ds(pl.multiple_of(first + at, CHUNK), CHUNK)
            here = pl.ds(at, CHUNK)
            grad = low[here, :].astype(F32) + high[here, :].astype(F32)
            hat, inverse = normalize(h_ref[rows, :])
            total = cot_ref[rows, :].astype(F32) + norm_back(grad, gain, hat, inverse)
            dh_ref[rows, :] = total
            narrow = total.astype(BF)
            low_scr[rows, :] = narrow
            do_scr[rows, :] = dot(narrow, w_scr[3]).astype(BF)
            return 0

        lax.fori_loop(0, half // CHUNK, step, 0)
    ship(dh_ref)
    turn = turn_matrix(width)
    ready(q_ref, k_ref, v_ref, o_ref, ab_ref)
    kt = (-dot(k_ref[...], turn)).astype(BF)
    qt = (-dot(q_ref[...], turn)).astype(BF)
    for h in range(heads):
        km_scr[h, :, 0:width] = only_head(k_ref[...], h)
        km_scr[h, :, 256 : 256 + width] = only_head(kt, h)
        qm_scr[h, :, 0:width] = only_head(q_ref[...], h)
        qm_scr[h, :, 256 : 256 + width] = only_head(qt, h)

    ready(cos_ref, sin_ref)
    for i in range(length // SPAN):
        rows = pl.ds(i * SPAN, SPAN)
        grad_o = do_scr[rows, :]
        product = grad_o.astype(F32) * o_ref[rows, :].astype(F32)
        dq = None
        dk = None
        dv = None
        for h in range(heads):
            own = only_head(grad_o, h)
            delta = jnp.sum(only_head(product, h), axis=-1, keepdims=True)
            da = dot_nt(own, v_ref[...])
            probs = ab_ref[h, rows, :]
            term = dot_tn(probs, own)
            dv = term if dv is None else dv + term
            ds = (probs.astype(F32) * (da - delta) * HEAD_DIM ** (-0.5)).astype(BF)
            term = dot(ds, km_scr[h])
            dq = term if dq is None else dq + term
            term = dot_tn(ds, qm_scr[h, rows, :])
            dk = term if dk is None else dk + term
        dp_scr[0, rows, :] = (dq[:, :width] * cos_ref[rows, :] + dq[:, 256 : 256 + width] * sin_ref[rows, :]).astype(BF)
        if i == 0:
            dk_scr[...] = dk
            dv_scr[...] = dv
        else:
            dk_scr[...] += dk
            dv_scr[...] += dv
    dp_scr[1] = (dk_scr[:, :width] * cos_ref[...] + dk_scr[:, 256 : 256 + width] * sin_ref[...]).astype(BF)
    dp_scr[2] = dv_scr[...].astype(BF)
    ready(n1_ref)
    for s in range(3):
        grad_ref[:, s * width : (s + 1) * width] = dot_tn(n1_ref[...], dp_scr[s]).astype(BF)
    grad_ref[:, 3 * width :] = dot_tn(low_scr[...], o_ref[...]).astype(BF)
    emit_grad(where_ref, grad_ref, rest[:-9])
    for ref in rest[:-9]:
        ship(ref)
    ready(om_ref, ot_ref)
    for is_mine, first in halves(core, length):
        out, other = (mine_ref, om_ref) if is_mine else (theirs_ref, ot_ref)
        rows = pl.ds(pl.multiple_of(first, half), half)
        part = dot_nt(dp_scr[0, rows, :], w_scr[0]) + dot_nt(dp_scr[1, rows, :], w_scr[1]) + dot_nt(dp_scr[2, rows, :], w_scr[2])
        out[0] = part.astype(BF)
        out[1] = other[...]
        ship(out)


def output_kernel(ready, ship, where_ref, h_ref, tok_ref, dh_ref, gain_ref, a_ref, b_ref, c_ref, d_ref, out_ref, grad_ref):
    length = h_ref.shape[0]
    core = where_ref[1] & 1
    ready(h_ref, tok_ref, dh_ref, gain_ref, a_ref, b_ref, c_ref, d_ref)
    gain = gain_ref[0:1, :]
    for is_mine, first in halves(core, length):
        low, high = (a_ref, b_ref) if is_mine else (c_ref, d_ref)

        def step(i, _):
            at = pl.multiple_of(i * CHUNK, CHUNK)
            rows = pl.ds(pl.multiple_of(first + at, CHUNK), CHUNK)
            here = pl.ds(at, CHUNK)
            out_ref[rows, :] = h_ref[rows, :] + (low[1, here, :].astype(F32) + high[1, here, :].astype(F32))
            grad = low[0, here, :].astype(F32) + high[0, here, :].astype(F32)
            hat, inverse = normalize(tok_ref[rows, :].astype(F32))
            grad_ref[rows, :] = dh_ref[rows, :] + norm_back(grad, gain, hat, inverse)
            return 0

        lax.fori_loop(0, length // 2 // CHUNK, step, 0)
        rows = pl.ds(pl.multiple_of(first, length // 2), length // 2)
        ship(out_ref, rows)
        ship(grad_ref, rows)


def total_of(refs):
    total = refs[0][...].astype(F32)
    for ref in refs[1:]:
        total = total + ref[...].astype(F32)
    return total


def step_kernel(groups, plan, *refs):
    at = 0
    shards = []
    for count in groups:
        shards.append(total_of(refs[at : at + count]))
        at += count
    outs = refs[at + 3 * len(plan) :]
    for leaf, (transposed, slices) in enumerate(plan):
        w_ref, f_ref, s_ref = refs[at : at + 3]
        at += 3
        g_out, d_out, f_out, s_out = outs[4 * leaf : 4 * leaf + 4]
        for i, (group, first, columns) in enumerate(slices):
            grad = shards[group][:, first : first + columns]
            if transposed:
                grad = grad.T
            where = (i,) if len(w_ref.shape) == 3 else Ellipsis
            delta, first_new, second_new = adamw(w_ref[where], grad, f_ref[where], s_ref[where], decay_rate)
            g_out[where] = grad
            d_out[where] = delta
            f_out[where] = first_new
            s_out[where] = second_new


def gain_kernel(columns, gain_row, w_ref, gains_ref, *refs):
    shard = total_of(refs[:-1])
    total = jnp.zeros((shard.shape[0], 1), F32)
    for i, first in enumerate(columns):
        width = w_ref.shape[2]
        narrow = w_ref[i].astype(BF).astype(F32)
        total = total + jnp.sum(narrow * shard[:, first : first + width], axis=-1, keepdims=True)
    wide = jnp.broadcast_to(total, (shard.shape[0], 128)).T
    gain = gains_ref[gain_row : gain_row + 1, :].astype(BF).astype(F32)
    refs[-1][...] = wide[0:8, :] / gain


def gain_call(columns, gain_row, weight, gains, pieces, deps=()):
    return call(
        lambda *refs: gain_kernel(columns, gain_row, *refs),
        [((8, gains.shape[1]), F32)],
        [weight, gains, *pieces],
        smem=0,
        deps=deps,
    )[0]


def sum_small(values):
    if lax.axis_size("tensor") != 4:
        return lax.psum(values, "tensor")
    return (values + swap(values, "tensor", 1)) + (swap(values, "tensor", 2) + swap(values, "tensor", 3))


def step_call(groups, plan, leaves):
    operands = [piece for group in groups for piece in group]
    for leaf in leaves:
        operands += list(leaf)
    outs = [(leaf[0].shape, F32) for leaf in leaves for _ in range(4)]

    def kernel(*refs):
        step_kernel([len(g) for g in groups], plan, *refs)

    flat = call(kernel, outs, operands, smem=0)
    return [flat[4 * i : 4 * i + 4] for i in range(len(leaves))]


def local(
    tokens,
    segment_ids,
    cotangent,
    w_qkv,
    w_out,
    w_in,
    w_down,
    gains,
    first_qkv,
    first_out,
    first_in,
    first_down,
    first_gains,
    second_qkv,
    second_out,
    second_in,
    second_down,
    second_gains,
):
    heads = w_qkv.shape[2]
    hidden = w_in.shape[2]
    length, depth = tokens.shape
    half = length // 2
    where = jnp.stack([lax.axis_index("dp"), lax.axis_index("tensor")]).astype(jnp.int32)
    pieces_a, masks_a, pieces_b, masks_b, early = gather_pieces(
        lambda deps: pack(w_qkv, w_out, gains, 0, deps), lambda deps: pack(w_in, w_down, gains, 1, deps)
    )
    wide_a, wide_b = pieces_a[0].shape[-1], pieces_b[0].shape[-1]
    repeat = heads // HEAD_DIM
    cosine_table, sine_values = rope_tables(length, heads, pieces_a[1:2])
    segments = segment_ids.astype(jnp.int32)

    n1, q, k, v, o, ab, gain_one, mine, theirs, full_a = stream(
        lambda *refs: attention_kernel(masks_a, len(pieces_a), heads, *refs),
        [
            ((length, depth), BF),
            ((length, heads), BF),
            ((length, heads), BF),
            ((length, heads), BF),
            ((length, heads), BF),
            ((repeat, length, length), BF),
            ((8, depth), F32),
            ((half, depth), BF),
            ((half, depth), BF),
            ((depth, wide_a), BF),
        ],
        [where, tokens, segments.reshape(length, 1), segments, cosine_table, sine_values, *pieces_a],
        [pltpu.VMEM((6, depth, heads), BF), pltpu.VMEM((repeat, length, heads), BF)],
    )
    terms = reduce_finish(reduce_start(mine, gate(theirs, early) if early else theirs))
    middle, n2, z, du, dv2, gain_two, mine, theirs, full_b = stream(
        lambda *refs: feed_kernel(masks_b, len(pieces_b), hidden, *refs),
        [
            ((length, depth), F32),
            ((length, depth), BF),
            ((length, hidden), BF),
            ((length, hidden), BF),
            ((length, hidden), BF),
            ((8, depth), F32),
            ((half, depth), BF),
            ((half, depth), BF),
            ((depth, wide_b), BF),
        ],
        [where, tokens, cotangent, *terms, *pieces_b],
        [pltpu.VMEM((3, depth, hidden), BF)],
    )
    chip = reduce_start(mine, theirs)
    width = 3 * hidden
    out_mine, out_theirs, *grad_feed = stream(
        lambda *refs: feed_grad_kernel(hidden, *refs),
        [((half, depth), BF), ((half, depth), BF)] + grad_outs(depth, width),
        [where, n2, cotangent, z, du, dv2, full_b],
        [pltpu.VMEM((depth, width), BF), pltpu.VMEM((depth, hidden), BF)],
        deps=[chip],
    )
    terms = reduce_finish(chip, [out_mine])
    feed_pieces, feed_got = scatter_start(where, grad_feed)
    width = 4 * heads
    dh, mine, theirs, *grad_attn = stream(
        lambda *refs: back_kernel(heads, *refs),
        [((length, depth), F32), ((2, half, depth), BF), ((2, half, depth), BF)] + grad_outs(depth, width),
        [where, *terms, middle, cotangent, gain_two, full_a, q, k, v, o, ab, n1, cosine_table, sine_values, out_mine, out_theirs],
        [
            pltpu.VMEM((depth, width), BF),
            pltpu.VMEM((length, depth), BF),
            pltpu.VMEM((length, heads), BF),
            pltpu.VMEM((4, depth, heads), BF),
            pltpu.VMEM((repeat, length, 512), BF),
            pltpu.VMEM((repeat, length, 512), BF),
            pltpu.VMEM((length, 512), F32),
            pltpu.VMEM((length, heads), F32),
            pltpu.VMEM((3, length, heads), BF),
        ],
    )
    attn_pieces, attn_got = scatter_start(where, grad_attn)
    terms = reduce_finish(reduce_start(mine, gate(theirs, feed_got) if feed_got else theirs), feed_pieces[1:] + attn_got)
    output, grad_tokens = stream(
        output_kernel,
        [((length, depth), F32), ((length, depth), F32)],
        [where, middle, tokens, dh, gain_one, *terms],
    )

    gain_sum_two = gain_call([0, hidden], 1, w_in, gains, feed_pieces)
    leaf_in, leaf_down = step_call(
        [feed_pieces],
        [(False, [(0, 0, hidden), (0, hidden, hidden)]), (True, [(0, 2 * hidden, hidden)])],
        [(w_in, first_in, second_in), (w_down, first_down, second_down)],
    )
    gain_sum_one = gain_call([0, heads, 2 * heads], 0, w_qkv, gains, attn_pieces, [grad_tokens, leaf_in[0]])
    share_gains = sum_small(jnp.concatenate([gain_sum_one[0:1], gain_sum_two[0:1]], axis=0))
    leaf_qkv, leaf_out = step_call(
        [attn_pieces],
        [(False, [(0, 0, heads), (0, heads, heads), (0, 2 * heads, heads)]), (True, [(0, 3 * heads, heads)])],
        [(w_qkv, first_qkv, second_qkv), (w_out, first_out, second_out)],
    )
    n_gains, m_gains, s_gains = adamw(gains, share_gains, first_gains, second_gains, 0.0)
    by_kind = list(zip(leaf_qkv, leaf_out, leaf_in, leaf_down, (share_gains, n_gains, m_gains, s_gains)))
    return (output, grad_tokens, *by_kind[0], *by_kind[1], *by_kind[2], *by_kind[3])


def solution(mesh):
    placed = (
        P("dp", None),
        P("dp", None),
        P("dp", None),
        P(None, "dp", "tensor"),
        P("tensor", "dp"),
        P(None, "dp", "tensor"),
        P("tensor", "dp"),
        P(None, "dp"),
        P(None, "dp", "tensor"),
        P("tensor", "dp"),
        P(None, "dp", "tensor"),
        P("tensor", "dp"),
        P(None, "dp"),
        P(None, "dp", "tensor"),
        P("tensor", "dp"),
        P(None, "dp", "tensor"),
        P("tensor", "dp"),
        P(None, "dp"),
    )
    return jax.shard_map(
        local,
        mesh=mesh,
        in_specs=placed,
        out_specs=(
            P("dp", None),
            P("dp", None),
            P(None, "dp", "tensor"),
            P("tensor", "dp"),
            P(None, "dp", "tensor"),
            P("tensor", "dp"),
            P(None, "dp"),
            P(None, "dp", "tensor"),
            P("tensor", "dp"),
            P(None, "dp", "tensor"),
            P("tensor", "dp"),
            P(None, "dp"),
            P(None, "dp", "tensor"),
            P("tensor", "dp"),
            P(None, "dp", "tensor"),
            P("tensor", "dp"),
            P(None, "dp"),
            P(None, "dp", "tensor"),
            P("tensor", "dp"),
            P(None, "dp", "tensor"),
            P("tensor", "dp"),
            P(None, "dp"),
        ),
        check_vma=False,
    )
```

time: 555 us -> 158 us (0.28)
  waiting for transfers between devices: 265 us -> 43.2 us
  blocking collectives: 177 us -> 0 us
  Pallas kernels: 0 us -> 53.6 us
  starting transfers between devices: 0.47 us -> 37.4 us
  local copies, waits for them, and re-layouts: 49.9 us -> 17.7 us
  matrix products: 26.7 us -> 0 us
  other arithmetic: 19.7 us -> 4.4 us
  between operations: 15.7 us -> 1.28 us
    unnamed x11 -> x0, waiting for transfers between devices: 233 us -> none
    all_gather x5 -> x0, blocking collectives: 155 us -> none  [the longest x1 38.8 us: local(): lax.all_gather(w_qkv.astype(jnp.bfloat16), 'dp', axis=1, tiled=True)]
    pallas_call x0 -> x24, Pallas kernels: none -> 53.6 us  [the longest x7 47.5 us: stream(): pl.pallas_call(body, out_shape=[jax.ShapeDtypeStruct(s, d) for s, d in ou...]
    ppermute x0 -> x35, waiting for transfers between devices: none -> 43.2 us  [swap(): return lax.ppermute(values, axis, [(i, i ^ mask) for i in range(count)])]
    ppermute x0 -> x35, starting transfers between devices: none -> 37.4 us  [swap(): return lax.ppermute(values, axis, [(i, i ^ mask) for i in range(count)])]
    unnamed x157 -> x117, local copies, waits for them, and re-layouts: 48.6 us -> 16.1 us
    psum x3 -> x0, waiting for transfers between devices: 31.3 us -> none  [the longest x1 29.4 us: local(): lax.psum(two_part.astype(jnp.bfloat16), 'tensor').astype(jnp.float32)]
    unnamed x1 -> x0, blocking collectives: 21.9 us -> none
  transfers between devices with their start and end apart: 7 -> 35, of which waited for: 6 -> 14; matrix products, arithmetic and copies ran while one was open for 10% -> 3% of each run, Pallas kernels for 0% -> 27%
where the time goes in v2:
time: 158 us
  Pallas kernels  53.6 us (34%)
  waiting for transfers between devices  43.2 us (27%)
  starting transfers between devices  37.4 us (24%)
  local copies, waits for them, and re-layouts  17.7 us (11%)
  other arithmetic  4.4 us (3%)
    pallas_call x7, Pallas kernels, stream(): pl.pallas_call(body, out_shape=[jax.ShapeDtypeStruct(s, d) for s, d in ou...  47.5 us
    ppermute x35, waiting for transfers between devices, swap(): return lax.ppermute(values, axis, [(i, i ^ mask) for i in range(count)])  43.2 us
    ppermute x35, starting transfers between devices, swap(): return lax.ppermute(values, axis, [(i, i ^ mask) for i in range(count)])  37.4 us
    unnamed x117, local copies, waits for them, and re-layouts  16.1 us
    pallas_call x9, Pallas kernels, call(): pl.pallas_call(body, out_shape=[jax.ShapeDtypeStruct(s, d) for s, d in ou...  5.4 us
  transfers between devices with their start and end apart: 35, of which 14 were waited for; matrix products, arithmetic and copies ran while one was open for 3% of the time, Pallas kernels for 27%

profile of v2, /device:TPU:0, one launch (start us, length us, event | category | flops | bytes accessed | tf_op | source)
XLA Modules:
  0.0 157.6 jit_solution(14422712453735782967)
XLA Ops:
  3.9 4.1 %collective-permute-start.1 = (bf16[96,896]{1,0:T(8,128)(2,1)S(1)}, bf16[96,896]{1,0:T(8,128)(2,1)S(1)}, u32[]{:S(2)}, u32[]{:S(2)}) collective-permute-start(bf16[96,896]{1,0:T(8,128)(2,1)S(1)} %shard_map.345.refs_6_), channel_id=1, source_target_pairs={{0,16},{4,20},{8,24},{12,28},{16,0},{20,4},{24,8},{28,12},{1,17},{... | collective-permute-start | bytes 516104 | tf_op jit(solution)/shard_map/ppermute | solution.py:53
  17.7 2.1 %collective-permute-start.5 = (bf16[96,896]{1,0:T(8,128)(2,1)S(1)}, bf16[96,896]{1,0:T(8,128)(2,1)S(1)}, u32[]{:S(2)}, u32[]{:S(2)}) collective-permute-start(bf16[96,896]{1,0:T(8,128)(2,1)S(1)} %collective-permute-done.1.refs_8_.refs_1_), channel_id=1, source_target_pairs={{0,4},{4,0},{8,12},{12,8},{16,20},{20,16},{24,28},{28,24},{1,5},{5... | collective-permute-start | bytes 516104 | tf_op jit(solution)/shard_map/ppermute | solution.py:53
  22.5 3.1 %collective-permute-start.9 = (bf16[96,896]{1,0:T(8,128)(2,1)S(1)}, bf16[96,896]{1,0:T(8,128)(2,1)S(1)}, u32[]{:S(2)}, u32[]{:S(2)}) collective-permute-start(bf16[96,896]{1,0:T(8,128)(2,1)S(1)} %shard_map.350.refs_7_), channel_id=1, source_target_pairs={{0,8},{4,12},{8,0},{12,4},{16,24},{20,28},{24,16},{28,20},{1,9},{5... | collective-permute-start | bytes 516104 | tf_op jit(solution)/shard_map/ppermute | solution.py:53
  25.9 3.4 %collective-permute-start.8 = (bf16[96,896]{1,0:T(8,128)(2,1)S(1)}, bf16[96,896]{1,0:T(8,128)(2,1)S(1)}, u32[]{:S(2)}, u32[]{:S(2)}) collective-permute-start(bf16[96,896]{1,0:T(8,128)(2,1)S(1)} %shard_map.350.refs_7_), channel_id=1, source_target_pairs={{0,24},{4,28},{8,16},{12,20},{16,8},{20,12},{24,0},{28,4},{1,25},{... | collective-permute-start | bytes 516104 | tf_op jit(solution)/shard_map/ppermute | solution.py:53
  30.0 3.1 %multiply_sine_fusion = (f32[512,192]{1,0:T(8,128)}, f32[512,192]{1,0:T(8,128)}) fusion(f32[192]{0:T(256)S(1)} %fusion.4, f32[512]{0:T(512)S(1)} %reduce), kind=kLoop, calls=%fused_computation | loop fusion | flops 98304 | bytes 789248 | tf_op jit(solution)/shard_map/sin | solution.py:31
  33.0 1.8 %collective-permute-done.6.refs_13_ = bf16[96,896]{1,0:T(8,128)(2,1)S(1)} collective-permute-done((bf16[96,896]{1,0:T(8,128)(2,1)S(1)}, bf16[96,896]{1,0:T(8,128)(2,1)S(1)}, u32[]{:S(2)}, u32[]{:S(2)}) %collective-permute-start.6) | collective-permute-done | bytes 172064 | tf_op jit(solution)/shard_map/ppermute | solution.py:53
  35.6 11.7 %shard_map.348 = (bf16[512,768]{1,0:T(8,128)(2,1)}, bf16[512,192]{1,0:T(8,128)(2,1)}, bf16[512,192]{1,0:T(8,128)(2,1)}, bf16[512,192]{1,0:T(8,128)(2,1)}, bf16[5...) custom-call(s32[2]{0:T(128)} %pad_add_fusion.refs_0_, ...), custom_call_target="tpu_custom_call" | custom-call | tf_op jit(solution)/shard_map/pallas_call | solution.py:259
  48.4 1.7 %collective-permute-done.11.refs_1_ = bf16[256,768]{1,0:T(8,128)(2,1)S(1)} collective-permute-done((bf16[256,768]{1,0:T(8,128)(2,1)S(1)}, bf16[256,768]{1,0:T(8,128)(2,1)S(1)}, u32[]{:S(2)}, u32[]{:S(2)}) %collective-permute-start.11) | collective-permute-done | bytes 393248 | tf_op jit(solution)/shard_map/ppermute | solution.py:53
  53.1 8.3 %collective-permute-done.12.refs_4_ = bf16[256,768]{1,0:T(8,128)(2,1)S(1)} collective-permute-done((bf16[256,768]{1,0:T(8,128)(2,1)S(1)}, bf16[256,768]{1,0:T(8,128)(2,1)S(1)}, u32[]{:S(2)}, u32[]{:S(2)}) %collective-permute-start.12) | collective-permute-done | bytes 393248 | tf_op jit(solution)/shard_map/ppermute | solution.py:53
  61.4 4.6 %collective-permute-done.15.refs_10_ = bf16[3,96,896]{2,1,0:T(8,128)(2,1)S(1)} collective-permute-done((bf16[3,96,896]{2,1,0:T(8,128)(2,1)S(1)}, bf16[3,96,896]{2,1,0:T(8,128)(2,1)S(1)}, u32[]{:S(2)}, u32[]{:S(2)}) %collective-permute-start.15) | collective-permute-done | bytes 516128 | tf_op jit(solution)/shard_map/ppermute | solution.py:53
  67.8 9.2 %shard_map.354 = (f32[512,768]{1,0:T(8,128)}, bf16[512,768]{1,0:T(8,128)(2,1)}, bf16[512,288]{1,0:T(8,128)(2,1)}, bf16[512,288]{1,0:T(8,128)(2,1)}, bf16[512,288...) custom-call(s32[2]{0:T(128)} %pad_add_fusion.refs_0_, ...), custom_call_target="tpu_custom_call" | custom-call | tf_op jit(solution)/shard_map/pallas_call | solution.py:259
  77.0 1.9 %collective-permute-done.16.refs_1_ = bf16[256,768]{1,0:T(8,128)(2,1)S(1)} collective-permute-done((bf16[256,768]{1,0:T(8,128)(2,1)}, bf16[256,768]{1,0:T(8,128)(2,1)S(1)}, u32[]{:S(2)}, u32[]{:S(2)}) %collective-permute-start.16) | collective-permute-done | bytes 393248 | tf_op jit(solution)/shard_map/ppermute | solution.py:53
  80.8 6.2 %shard_map.356 = (bf16[256,768]{1,0:T(8,128)(2,1)}, bf16[256,768]{1,0:T(8,128)(2,1)}, bf16[4,96,864]{2,1,0:T(8,128)(2,1)}, bf16[4,96,864]{2,1,0:T(8,128)(2,1)}) custom-call(s32[2]{0:T(128)} %pad_add_fusion.refs_0_, bf16[512,768]{1,0:T(8,128)(2,1)} %get-tuple-element.81.refs_1_, bf16[512,768]{1,0:T(8,128)(2,1)} %refs_6_.3, ...), custom_call_target="tpu_custom_call" | custom-call | tf_op jit(solution)/shard_map/pallas_call | solution.py:259
  87.6 3.7 %collective-permute-done.17.refs_0_ = bf16[256,768]{1,0:T(8,128)(2,1)S(1)} collective-permute-done((bf16[256,768]{1,0:T(8,128)(2,1)S(1)}, bf16[256,768]{1,0:T(8,128)(2,1)S(1)}, u32[]{:S(2)}, u32[]{:S(2)}) %collective-permute-start.17) | collective-permute-done | bytes 393248 | tf_op jit(solution)/shard_map/ppermute | solution.py:53
  94.8 12.6 %shard_map.358 = (f32[512,768]{1,0:T(8,128)}, bf16[2,256,768]{2,1,0:T(8,128)(2,1)}, bf16[2,256,768]{2,1,0:T(8,128)(2,1)}, bf16[4,96,768]{2,1,0:T(8,128)(2,1)}, bf16[4,96,768]{2,1,0:T(8,128)(2,1)}) custom-call(s32[2]{0:T(128)} %pad_add_fusion.refs_0_, bf16[256,768]{1,0:T(8,128)(2,1)} %copy-done, bf16[256,768]{1,0:T(8,128)(2,1)} %copy-done.9, ...), custom_call_target="tpu_custom_call" | custom-call | tf_op jit(solution)/shard_map/pallas_call | solution.py:259
  109.5 2.4 %collective-permute-done.21.refs_1_ = bf16[2,256,768]{2,1,0:T(8,128)(2,1)S(1)} collective-permute-done((bf16[2,256,768]{2,1,0:T(8,128)(2,1)}, bf16[2,256,768]{2,1,0:T(8,128)(2,1)S(1)}, u32[]{:S(2)}, u32[]{:S(2)}) %collective-permute-start.21) | collective-permute-done | bytes 786464 | tf_op jit(solution)/shard_map/ppermute | solution.py:53
  114.0 3.9 %collective-permute-start.23 = (bf16[96,864]{1,0:T(8,128)(2,1)S(1)}, bf16[96,864]{1,0:T(8,128)(2,1)S(1)}, u32[]{:S(2)}, u32[]{:S(2)}) collective-permute-start(bf16[96,864]{1,0:T(8,128)(2,1)S(1)} %get-tuple-element.102), channel_id=1, source_target_pairs={{0,8},{4,12},{8,0},{12,4},{16,24},{20,28},{24,16},{28,20},{1,9},{5... | collective-permute-start | bytes 497672 | tf_op jit(solution)/shard_map/ppermute | solution.py:53
  118.6 1.7 %collective-permute-start.25 = (bf16[96,864]{1,0:T(8,128)(2,1)S(1)}, bf16[96,864]{1,0:T(8,128)(2,1)S(1)}, u32[]{:S(2)}, u32[]{:S(2)}) collective-permute-start(bf16[96,864]{1,0:T(8,128)(2,1)S(1)} %get-tuple-element.104), channel_id=1, source_target_pairs={{0,24},{4,28},{8,16},{12,20},{16,8},{20,12},{24,0},{28,4},{1,25},{... | collective-permute-start | bytes 497672 | tf_op jit(solution)/shard_map/ppermute | solution.py:53
  120.3 3.1 %collective-permute-done.23.refs_1_.refs_3_ = bf16[96,864]{1,0:T(8,128)(2,1)S(1)} collective-permute-done((bf16[96,864]{1,0:T(8,128)(2,1)S(1)}, bf16[96,864]{1,0:T(8,128)(2,1)S(1)}, u32[]{:S(2)}, u32[]{:S(2)}) %collective-permute-start.23) | collective-permute-done | bytes 165920 | tf_op jit(solution)/shard_map/ppermute | solution.py:53
  123.3 9.3 %collective-permute-done.24.refs_2_.refs_4_ = bf16[96,864]{1,0:T(8,128)(2,1)S(1)} collective-permute-done((bf16[96,864]{1,0:T(8,128)(2,1)S(1)}, bf16[96,864]{1,0:T(8,128)(2,1)S(1)}, u32[]{:S(2)}, u32[]{:S(2)}) %collective-permute-start.24) | collective-permute-done | bytes 165920 | tf_op jit(solution)/shard_map/ppermute | solution.py:53
  133.5 3.4 %collective-permute-start.29 = (bf16[96,768]{1,0:T(8,128)(2,1)S(1)}, bf16[96,768]{1,0:T(8,128)(2,1)S(1)}, u32[]{:S(2)}, u32[]{:S(2)}) collective-permute-start(bf16[96,768]{1,0:T(8,128)(2,1)S(1)} %get-tuple-element.110), channel_id=1, source_target_pairs={{0,8},{4,12},{8,0},{12,4},{16,24},{20,28},{24,16},{28,20},{1,9},{5... | collective-permute-start | bytes 442376 | tf_op jit(solution)/shard_map/ppermute | solution.py:53
  136.9 2.4 %collective-permute-start.31 = (bf16[96,768]{1,0:T(8,128)(2,1)S(1)}, bf16[96,768]{1,0:T(8,128)(2,1)S(1)}, u32[]{:S(2)}, u32[]{:S(2)}) collective-permute-start(bf16[96,768]{1,0:T(8,128)(2,1)S(1)} %get-tuple-element.112), channel_id=1, source_target_pairs={{0,24},{4,28},{8,16},{12,20},{16,8},{20,12},{24,0},{28,4},{1,25},{... | collective-permute-start | bytes 442376 | tf_op jit(solution)/shard_map/ppermute | solution.py:53
  142.5 6.5 %shard_map.363 = (f32[512,768]{1,0:T(8,128)}, f32[512,768]{1,0:T(8,128)}) custom-call(s32[2]{0:T(128)} %pad_add_fusion.refs_0_, f32[512,768]{1,0:T(8,128)} %get-tuple-element.78.refs_5_.refs_1_, bf16[512,768]{1,0:T(8,128)(2,1)} %refs_2_.9, f32[512,768]{1,0:T(8,128)} %get-tuple-element.96.refs_3_, f32[8,768]{1,0:T(8,128)} %get-tuple-element.97.refs_4_, ...), custom_call_target="tpu_custom_call" | custom-call | tf_op jit(solution)/shard_map/pallas_call | solution.py:259
  149.0 1.7 %collective-permute-done.30.refs_2_.refs_4_ = bf16[96,768]{1,0:T(8,128)(2,1)S(1)} collective-permute-done((bf16[96,768]{1,0:T(8,128)(2,1)S(1)}, bf16[96,768]{1,0:T(8,128)(2,1)S(1)}, u32[]{:S(2)}, u32[]{:S(2)}) %collective-permute-start.30) | collective-permute-done | bytes 147488 | tf_op jit(solution)/shard_map/ppermute | solution.py:53
  (197 shorter events, 44.4 us)
Async XLA Ops:
  3.9 13.8 %collective-permute-start.1 = (bf16[96,896]{1,0:T(8,128)(2,1)S(1)}, bf16[96,896]{1,0:T(8,128)(2,1)S(1)}, u32[]{:S(2)}, u32[]{:S(2)}) collective-permute-start(bf16[96,896]{1,0:T(8,128)(2,1)S(1)} %shard_map.345.refs_6_), channel_id=1, source_target_pairs={{0,16},{4,20},{8,24},{12,28},{16,0},{20,4},{24,8},{28,12},{1,17},{... | collective-permute-start | bytes 516104 | tf_op jit(solution)/shard_map/ppermute | solution.py:53
  8.0 11.8 %collective-permute-start = (bf16[96,896]{1,0:T(8,128)(2,1)S(1)}, bf16[96,896]{1,0:T(8,128)(2,1)S(1)}, u32[]{:S(2)}, u32[]{:S(2)}) collective-permute-start(bf16[96,896]{1,0:T(8,128)(2,1)S(1)} %shard_map.345.refs_6_), channel_id=1, source_target_pairs={{0,8},{4,12},{8,0},{12,4},{16,24},{20,28},{24,16},{28,20},{1,9},{5... | collective-permute-start | bytes 516104 | tf_op jit(solution)/shard_map/ppermute | solution.py:53
  9.5 19.8 %collective-permute-start.3 = (bf16[96,896]{1,0:T(8,128)(2,1)S(1)}, bf16[96,896]{1,0:T(8,128)(2,1)S(1)}, u32[]{:S(2)}, u32[]{:S(2)}) collective-permute-start(bf16[96,896]{1,0:T(8,128)(2,1)S(1)} %shard_map.345.refs_6_), channel_id=1, source_target_pairs={{0,4},{4,0},{8,12},{12,8},{16,20},{20,16},{24,28},{28,24},{1,5},{5... | collective-permute-start | bytes 516104 | tf_op jit(solution)/shard_map/ppermute | solution.py:53
  11.0 9.9 %collective-permute-start.2 = (bf16[96,896]{1,0:T(8,128)(2,1)S(1)}, bf16[96,896]{1,0:T(8,128)(2,1)S(1)}, u32[]{:S(2)}, u32[]{:S(2)}) collective-permute-start(bf16[96,896]{1,0:T(8,128)(2,1)S(1)} %shard_map.345.refs_6_), channel_id=1, source_target_pairs={{0,24},{4,28},{8,16},{12,20},{16,8},{20,12},{24,0},{28,4},{1,25},{... | collective-permute-start | bytes 516104 | tf_op jit(solution)/shard_map/ppermute | solution.py:53
  19.8 9.5 %collective-permute-start.4 = (bf16[96,896]{1,0:T(8,128)(2,1)S(1)}, bf16[96,896]{1,0:T(8,128)(2,1)S(1)}, u32[]{:S(2)}, u32[]{:S(2)}) collective-permute-start(bf16[96,896]{1,0:T(8,128)(2,1)S(1)} %collective-permute-done.refs_1_.refs_7_), channel_id=1, source_target_pairs={{0,4},{4,0},{8,12},{12,8},{16,20},{20,16},{24,28},{28,24},{1,5},{5... | collective-permute-start | bytes 516104 | tf_op jit(solution)/shard_map/ppermute | solution.py:53
  20.9 26.3 %collective-permute-start.10 = (bf16[96,896]{1,0:T(8,128)(2,1)S(1)}, bf16[96,896]{1,0:T(8,128)(2,1)S(1)}, u32[]{:S(2)}, u32[]{:S(2)}) collective-permute-start(bf16[96,896]{1,0:T(8,128)(2,1)S(1)} %shard_map.350.refs_7_), channel_id=1, source_target_pairs={{0,4},{4,0},{8,12},{12,8},{16,20},{20,16},{24,28},{28,24},{1,5},{5... | collective-permute-start | bytes 516104 | tf_op jit(solution)/shard_map/ppermute | solution.py:53
  22.5 24.7 %collective-permute-start.9 = (bf16[96,896]{1,0:T(8,128)(2,1)S(1)}, bf16[96,896]{1,0:T(8,128)(2,1)S(1)}, u32[]{:S(2)}, u32[]{:S(2)}) collective-permute-start(bf16[96,896]{1,0:T(8,128)(2,1)S(1)} %shard_map.350.refs_7_), channel_id=1, source_target_pairs={{0,8},{4,12},{8,0},{12,4},{16,24},{20,28},{24,16},{28,20},{1,9},{5... | collective-permute-start | bytes 516104 | tf_op jit(solution)/shard_map/ppermute | solution.py:53
  25.9 21.4 %collective-permute-start.8 = (bf16[96,896]{1,0:T(8,128)(2,1)S(1)}, bf16[96,896]{1,0:T(8,128)(2,1)S(1)}, u32[]{:S(2)}, u32[]{:S(2)}) collective-permute-start(bf16[96,896]{1,0:T(8,128)(2,1)S(1)} %shard_map.350.refs_7_), channel_id=1, source_target_pairs={{0,24},{4,28},{8,16},{12,20},{16,8},{20,12},{24,0},{28,4},{1,25},{... | collective-permute-start | bytes 516104 | tf_op jit(solution)/shard_map/ppermute | solution.py:53
  29.3 17.9 %collective-permute-start.7 = (bf16[96,896]{1,0:T(8,128)(2,1)S(1)}, bf16[96,896]{1,0:T(8,128)(2,1)S(1)}, u32[]{:S(2)}, u32[]{:S(2)}) collective-permute-start(bf16[96,896]{1,0:T(8,128)(2,1)S(1)} %shard_map.350.refs_7_), channel_id=1, source_target_pairs={{0,16},{4,20},{8,24},{12,28},{16,0},{20,4},{24,8},{28,12},{1,17},{... | collective-permute-start | bytes 516104 | tf_op jit(solution)/shard_map/ppermute | solution.py:53
  50.2 11.2 %collective-permute-start.12 = (bf16[256,768]{1,0:T(8,128)(2,1)S(1)}, bf16[256,768]{1,0:T(8,128)(2,1)S(1)}, u32[]{:S(2)}, u32[]{:S(2)}) collective-permute-start(bf16[256,768]{1,0:T(8,128)(2,1)S(1)} %shard_map.352.refs_3_), channel_id=1, source_target_pairs={{0,2},{1,3},{2,0},{3,1},{4,6},{5,7},{6,4},{7,5},{8,10},{9,11},{10,... | collective-permute-start | bytes 1179656 | tf_op jit(solution)/shard_map/ppermute | solution.py:53
  52.5 13.6 %collective-permute-start.15 = (bf16[3,96,896]{2,1,0:T(8,128)(2,1)S(1)}, bf16[3,96,896]{2,1,0:T(8,128)(2,1)S(1)}, u32[]{:S(2)}, u32[]{:S(2)}) collective-permute-start(bf16[3,96,896]{2,1,0:T(8,128)(2,1)S(1)} %shard_map.353.refs_8_), channel_id=1, source_target_pairs={{0,4},{4,0},{8,12},{12,8},{16,20},{20,16},{24,28},{28,24},{1,5},{5... | collective-permute-start | bytes 1548296 | tf_op jit(solution)/shard_map/ppermute | solution.py:53
  53.1 13.0 %collective-permute-start.13 = (bf16[256,768]{1,0:T(8,128)(2,1)S(1)}, bf16[256,768]{1,0:T(8,128)(2,1)S(1)}, u32[]{:S(2)}, u32[]{:S(2)}) collective-permute-start(bf16[256,768]{1,0:T(8,128)(2,1)S(1)} %shard_map.352.refs_3_), channel_id=1, source_target_pairs={{0,1},{1,0},{2,3},{3,2},{4,5},{5,4},{6,7},{7,6},{8,9},{9,8},{10,11... | collective-permute-start | bytes 1179656 | tf_op jit(solution)/shard_map/ppermute | solution.py:53
  80.1 11.2 %collective-permute-start.17 = (bf16[256,768]{1,0:T(8,128)(2,1)S(1)}, bf16[256,768]{1,0:T(8,128)(2,1)S(1)}, u32[]{:S(2)}, u32[]{:S(2)}) collective-permute-start(bf16[256,768]{1,0:T(8,128)(2,1)S(1)} %shard_map.355.refs_7_.refs_1_), channel_id=1, source_target_pairs={{0,2},{1,3},{2,0},{3,1},{4,6},{5,7},{6,4},{7,5},{8,10},{9,11},{10,... | collective-permute-start | bytes 1179656 | tf_op jit(solution)/shard_map/ppermute | solution.py:53
  87.0 20.4 %collective-permute-start.20 = (bf16[4,96,864]{2,1,0:T(8,128)(2,1)}, bf16[4,96,864]{2,1,0:T(8,128)(2,1)S(1)}, u32[]{:S(2)}, u32[]{:S(2)}) collective-permute-start(bf16[4,96,864]{2,1,0:T(8,128)(2,1)} %get-tuple-element.100), channel_id=1, source_target_pairs={{0,4},{4,0},{8,12},{12,8},{16,20},{20,16},{24,28},{28,24},{1,5},{5... | collective-permute-start | bytes 1990664 | tf_op jit(solution)/shard_map/ppermute | solution.py:53
  112.1 20.5 %collective-permute-start.22 = (bf16[2,256,768]{2,1,0:T(8,128)(2,1)S(1)}, bf16[2,256,768]{2,1,0:T(8,128)(2,1)S(1)}, u32[]{:S(2)}, u32[]{:S(2)}) collective-permute-start(bf16[2,256,768]{2,1,0:T(8,128)(2,1)S(1)} %shard_map.360.refs_5_), channel_id=1, source_target_pairs={{0,2},{1,3},{2,0},{3,1},{4,6},{5,7},{6,4},{7,5},{8,10},{9,11},{10,... | collective-permute-start | bytes 2359304 | tf_op jit(solution)/shard_map/ppermute | solution.py:53
  112.7 19.9 %collective-permute-start.26 = (bf16[4,96,768]{2,1,0:T(8,128)(2,1)S(1)}, bf16[4,96,768]{2,1,0:T(8,128)(2,1)S(1)}, u32[]{:S(2)}, u32[]{:S(2)}) collective-permute-start(bf16[4,96,768]{2,1,0:T(8,128)(2,1)S(1)} %copy-done.57), channel_id=1, source_target_pairs={{0,4},{4,0},{8,12},{12,8},{16,20},{20,16},{24,28},{28,24},{1,5},{5... | collective-permute-start | bytes 1769480 | tf_op jit(solution)/shard_map/ppermute | solution.py:53
  114.0 9.4 %collective-permute-start.23 = (bf16[96,864]{1,0:T(8,128)(2,1)S(1)}, bf16[96,864]{1,0:T(8,128)(2,1)S(1)}, u32[]{:S(2)}, u32[]{:S(2)}) collective-permute-start(bf16[96,864]{1,0:T(8,128)(2,1)S(1)} %get-tuple-element.102), channel_id=1, source_target_pairs={{0,8},{4,12},{8,0},{12,4},{16,24},{20,28},{24,16},{28,20},{1,9},{5... | collective-permute-start | bytes 497672 | tf_op jit(solution)/shard_map/ppermute | solution.py:53
  117.8 14.8 %collective-permute-start.24 = (bf16[96,864]{1,0:T(8,128)(2,1)S(1)}, bf16[96,864]{1,0:T(8,128)(2,1)S(1)}, u32[]{:S(2)}, u32[]{:S(2)}) collective-permute-start(bf16[96,864]{1,0:T(8,128)(2,1)S(1)} %get-tuple-element.103), channel_id=1, source_target_pairs={{0,16},{4,20},{8,24},{12,28},{16,0},{20,4},{24,8},{28,12},{1,17},{... | collective-permute-start | bytes 497672 | tf_op jit(solution)/shard_map/ppermute | solution.py:53
  118.6 14.0 %collective-permute-start.25 = (bf16[96,864]{1,0:T(8,128)(2,1)S(1)}, bf16[96,864]{1,0:T(8,128)(2,1)S(1)}, u32[]{:S(2)}, u32[]{:S(2)}) collective-permute-start(bf16[96,864]{1,0:T(8,128)(2,1)S(1)} %get-tuple-element.104), channel_id=1, source_target_pairs={{0,24},{4,28},{8,16},{12,20},{16,8},{20,12},{24,0},{28,4},{1,25},{... | collective-permute-start | bytes 497672 | tf_op jit(solution)/shard_map/ppermute | solution.py:53
  123.3 17.9 %collective-permute-start.27 = (bf16[2,256,768]{2,1,0:T(8,128)(2,1)S(1)}, bf16[2,256,768]{2,1,0:T(8,128)(2,1)S(1)}, u32[]{:S(2)}, u32[]{:S(2)}) collective-permute-start(bf16[2,256,768]{2,1,0:T(8,128)(2,1)S(1)} %shard_map.360.refs_5_), channel_id=1, source_target_pairs={{0,1},{1,0},{2,3},{3,2},{4,5},{5,4},{6,7},{7,6},{8,9},{9,8},{10,11... | collective-permute-start | bytes 2359304 | tf_op jit(solution)/shard_map/ppermute | solution.py:53
  132.7 8.6 %collective-permute-start.28 = (bf16[2,256,768]{2,1,0:T(8,128)(2,1)S(1)}, bf16[2,256,768]{2,1,0:T(8,128)(2,1)S(1)}, u32[]{:S(2)}, u32[]{:S(2)}) collective-permute-start(bf16[2,256,768]{2,1,0:T(8,128)(2,1)S(1)} %shard_map.362.refs_6_), channel_id=1, source_target_pairs={{0,1},{1,0},{2,3},{3,2},{4,5},{5,4},{6,7},{7,6},{8,9},{9,8},{10,11... | collective-permute-start | bytes 2359304 | tf_op jit(solution)/shard_map/ppermute | solution.py:53
  133.5 15.5 %collective-permute-start.29 = (bf16[96,768]{1,0:T(8,128)(2,1)S(1)}, bf16[96,768]{1,0:T(8,128)(2,1)S(1)}, u32[]{:S(2)}, u32[]{:S(2)}) collective-permute-start(bf16[96,768]{1,0:T(8,128)(2,1)S(1)} %get-tuple-element.110), channel_id=1, source_target_pairs={{0,8},{4,12},{8,0},{12,4},{16,24},{20,28},{24,16},{28,20},{1,9},{5... | collective-permute-start | bytes 442376 | tf_op jit(solution)/shard_map/ppermute | solution.py:53
  136.9 13.9 %collective-permute-start.30 = (bf16[96,768]{1,0:T(8,128)(2,1)S(1)}, bf16[96,768]{1,0:T(8,128)(2,1)S(1)}, u32[]{:S(2)}, u32[]{:S(2)}) collective-permute-start(bf16[96,768]{1,0:T(8,128)(2,1)S(1)} %get-tuple-element.111), channel_id=1, source_target_pairs={{0,16},{4,20},{8,24},{12,28},{16,0},{20,4},{24,8},{28,12},{1,17},{... | collective-permute-start | bytes 442376 | tf_op jit(solution)/shard_map/ppermute | solution.py:53
  136.9 13.9 %collective-permute-start.31 = (bf16[96,768]{1,0:T(8,128)(2,1)S(1)}, bf16[96,768]{1,0:T(8,128)(2,1)S(1)}, u32[]{:S(2)}, u32[]{:S(2)}) collective-permute-start(bf16[96,768]{1,0:T(8,128)(2,1)S(1)} %get-tuple-element.112), channel_id=1, source_target_pairs={{0,24},{4,28},{8,16},{12,20},{16,8},{20,12},{24,0},{28,4},{1,25},{... | collective-permute-start | bytes 442376 | tf_op jit(solution)/shard_map/ppermute | solution.py:53
  (69 other events, 424.5 us)

commit v3 on v2

--- a/solution.py
+++ b/solution.py
@@ -22,12 +22,11 @@
 F32 = jnp.float32
 
 
-def rope_tables(count, width, deps):
+def rope_tables(count, width):
     half_dim = HEAD_DIM // 2
     spot = (jnp.arange(width) % half_dim).astype(jnp.float32)
     frequency = rope_base ** (-(spot * 2.0 / HEAD_DIM))
-    place = gate(jnp.arange(count, dtype=jnp.float32)[:, None], deps)
-    angles = place * frequency[None, :]
+    angles = jnp.arange(count, dtype=jnp.float32)[:, None] * frequency[None, :]
     return (jnp.cos(angles), jnp.sin(angles))
 
 
@@ -58,28 +57,28 @@
     used = first.shape[0] * first.shape[2] + second.shape[0] + 1
     width = -(-used // 128) * 128
     return stream(
-        lambda *refs: pack_kernel(row, *refs), [((rows, width), BF)], [first, second, gains], smem=0, deps=deps, vmem=16
+        lambda *refs: pack_kernel(row, *refs), [((rows, width), BF)], [first, second, gains], smem=0, deps=deps, vmem=16, near=(0,), far=(0, 1, 2)
     )[0]
 
 
-def gather_pieces(pack_a, pack_b):
+def gather_pieces(beside, pack_a, pack_b):
     if lax.axis_size("dp") != 8:
         full_a = lax.all_gather(pack_a(()), "dp", axis=0, tiled=True)
         full_b = lax.all_gather(pack_b(()), "dp", axis=0, tiled=True)
-        return [full_a], None, [full_b], None, []
+        return [full_a], None, [full_b], None, [], []
     order = (4, 6, 2)
     shard_a, shard_b = pack_a(()), pack_b(())
     far_one, far_two, near = [swap(shard_a, "dp", m) for m in order]
-    sides = [swap(piece, "dp", 1) for piece in (shard_a, near, far_one)]
-    sides.append(swap(gate(far_two, sides[1:]), "dp", 1))
+    side = swap(shard_a, "dp", 1)
+    sides = [side, swap(gate(side, beside), "dp", 2), swap(far_one, "dp", 1), swap(far_two, "dp", 1)]
     pieces_a = [shard_a, near, far_one, far_two] + sides
     masks_a = [[m] for m in (0, 2, 4, 6, 1, 3, 5, 7)]
-    shard_b = gate(shard_b, [far_one, far_two])
+    shard_b = gate(shard_b, [far_one, far_two, sides[1]])
     column = [swap(shard_b, "dp", m) for m in order]
     side = swap(shard_b, "dp", 1)
     stacked = stack(column)
     pieces_b = [shard_b, stacked, side, swap(stacked, "dp", 1)]
-    return pieces_a, masks_a, pieces_b, [[0], [4, 6, 2], [1], [5, 7, 3]], column + [side]
+    return pieces_a, masks_a, pieces_b, [[0], [4, 6, 2], [1], [5, 7, 3]], column + [side], [stacked]
 
 
 def pair_kernel(where_ref, keep_ref, got_ref, own_ref, *far_refs):
@@ -91,11 +90,54 @@
 
 def scatter_start(where, grads, deps=()):
     if len(grads) == 1:
-        return [lax.psum_scatter(grads[0].astype(F32), "dp", scatter_dimension=0, tiled=True)], []
+        return [lax.psum_scatter(grads[0].astype(F32), "dp", scatter_dimension=0, tiled=True)], [], []
     keep, send = grads
-    got = swap(gate(send, deps) if deps else send, "dp", 1)
-    parts = call(pair_kernel, [(keep.shape[1:], BF)] * keep.shape[0], [where, keep, got])
-    return [parts[0]] + [swap(parts[m], "dp", 2 * m) for m in range(1, len(parts))], [got]
+    got = swap(send, "dp", 1)
+    parts = call(pair_kernel, [(keep.shape[1:], BF)] * keep.shape[0], [where, keep, got], deps=deps)
+    return [parts[0]] + [swap(parts[m], "dp", 2 * m) for m in range(1, len(parts))], [got], [parts[0]]
+
+
+def far_kernel(where_ref, *refs):
+    terms, (own_ref, send_ref) = refs[:-2], refs[-2:]
+    rows = own_ref.shape[0]
+    odd = where_ref[0] & 1
+    for ref, at in ((own_ref, odd), (send_ref, 1 - odd)):
+        span = pl.ds(pl.multiple_of(at * rows, rows), rows)
+        total = terms[0][span, :].astype(F32)
+        for term in terms[1:]:
+            total = total + term[span, :].astype(F32)
+        ref[...] = total.astype(BF)
+
+
+def scatter_far_first(where, grads):
+    if len(grads) == 1:
+        pieces, got, _unused = scatter_start(where, grads)
+        return lambda deps: pieces, got
+    got = [swap(grads[m], "dp", 2 * m) for m in range(1, len(grads))]
+    rows, width = grads[0].shape
+
+    def finish(deps):
+        own, send = call(far_kernel, [((rows // 2, width), BF)] * 2, [where, grads[0], *got], deps=deps)
+        return [own, swap(send, "dp", 1)]
+
+    return finish, got
+
+
+def far_outs(depth, width):
+    count = lax.axis_size("dp")
+    if count != 8:
+        return [((depth, width), BF)]
+    return [((2 * depth // count, width), BF)] * (count // 2)
+
+
+def emit_far(where_ref, grad_scr, refs):
+    level = where_ref[0] >> 1
+    for m, ref in enumerate(refs):
+        if len(refs) == 1:
+            ref[...] = grad_scr[...]
+        else:
+            at = pl.multiple_of((level ^ m) * ref.shape[0], ref.shape[0])
+            ref[...] = grad_scr[pl.ds(at, ref.shape[0]), :]
 
 
 def grad_outs(depth, width):
@@ -132,7 +174,7 @@
     got = swap(chip, "tensor", 2)
     if deps:
         got = gate(got, deps)
-    return chip, got, swap(chip, "tensor", 1), swap(got, "tensor", 1)
+    return [chip, got, swap(chip, "tensor", 1), swap(got, "tensor", 1)]
 
 
 def dot(a, b):
@@ -214,21 +256,25 @@
     )(*operands, *deps)
 
 
-def stream(kernel, outs, operands, scratch=(), smem=1, deps=(), vmem=58):
+def stream(kernel, outs, operands, scratch=(), smem=1, deps=(), vmem=40, near=(), far=()):
     count, total = len(operands), len(outs)
     late = count - smem
-    room = [pltpu.VMEM(x.shape, x.dtype) for x in operands[smem:]] + [pltpu.VMEM(x, d) for x, d in outs]
+    room = [pltpu.VMEM(x.shape, x.dtype) for x in operands[smem:]]
+    room += [pltpu.VMEM(*out) for i, out in enumerate(outs) if i not in near]
+    gone = total - len(near)
 
     def body(*refs):
         given, results = refs[smem:count], refs[count + len(deps) : count + len(deps) + total]
         own = refs[count + len(deps) + total :]
         flags, own = own[-1], own[:-1]
-        own, held, made = own[: -late - total], own[-late - total : -total], own[-total:]
+        own, held, made = own[: -late - gone], own[-late - gone : -gone or None], list(own[len(own) - gone :])
+        for i in sorted(near):
+            made.insert(i, results[i])
         copies = [pltpu.make_async_copy(given[i], held[i], flags.at[i]) for i in range(late)]
         for copy in copies:
             copy.start()
         waiting = {id(ref): copy for ref, copy in zip(held, copies)}
-        place = {id(ref): i for i, ref in enumerate(made)}
+        place = {id(ref): i for i, ref in enumerate(made) if i not in near}
         sent = []
         shipped = {}
 
@@ -239,7 +285,9 @@
                     copy.wait()
 
         def ship(ref, rows=None):
-            i = place[id(ref)]
+            i = place.get(id(ref))
+            if i is None:
+                return
             part = shipped.get(i, 0)
             shipped[i] = part + 1
             source, target = (ref, results[i]) if rows is None else (ref.at[rows], results[i].at[rows])
@@ -256,17 +304,20 @@
             copy.wait()
 
     anywhere = pl.BlockSpec(memory_space=pl.ANY)
+    pinned = [pltpu.with_memory_space_constraint(x, pltpu.HBM) if i in far else x for i, x in enumerate(operands)]
     return pl.pallas_call(
         body,
-        out_shape=[jax.ShapeDtypeStruct(s, d) for s, d in outs],
+        out_shape=[jax.ShapeDtypeStruct(*out) if i in near else pltpu.HBM(*out) for i, out in enumerate(outs)],
         in_specs=[pl.BlockSpec(memory_space=pltpu.SMEM)] * smem + [anywhere] * (late + len(deps)),
-        out_specs=[anywhere] * total,
+        out_specs=[pl.BlockSpec() if i in near else anywhere for i in range(total)],
         scratch_shapes=list(scratch) + room + [pltpu.SemaphoreType.DMA((late + 2 * total,))],
         compiler_params=pltpu.CompilerParams(vmem_limit_bytes=vmem * 1024 * 1024),
-    )(*operands, *deps)
+    )(*pinned, *deps)
 
 
 def gate(value, deps):
+    if not deps:
+        return value
     return pl.pallas_call(
         lambda *refs: None,
         out_shape=jax.ShapeDtypeStruct(value.shape, value.dtype),
@@ -375,6 +426,7 @@
 
         lax.fori_loop(0, length // 2 // CHUNK, attend, 0)
         ship(mine_ref if is_mine else theirs_ref)
+        ship(ab_ref, (slice(None), pl.ds(pl.multiple_of(first, length // 2), length // 2)))
 
 
 def feed_kernel(masks, count, width, ready, ship, where_ref, tok_ref, cot_ref, a_ref, b_ref, c_ref, d_ref, *rest):
@@ -425,16 +477,19 @@
         ship(mine_ref if is_mine else theirs_ref)
 
 
-def feed_grad_kernel(width, ready, ship, where_ref, n2_ref, cot_ref, z_ref, du_ref, dv_ref, full_ref, mine_ref, theirs_ref, *rest):
-    grad_ref, w_scr = rest[-2:]
+def feed_grad_kernel(width, split, ready, ship, where_ref, n2_ref, du_ref, dv_ref, cot_ref, z_ref, full_ref, mine_ref, theirs_ref, *rest):
+    grad_ref, down_ref, w_scr = rest[-3:]
     ready(n2_ref, du_ref)
     grad_ref[:, 0:width] = dot_tn(n2_ref[...], du_ref[...]).astype(BF)
     ready(dv_ref)
     grad_ref[:, width : 2 * width] = dot_tn(n2_ref[...], dv_ref[...]).astype(BF)
+    emit_grad(where_ref, grad_ref, rest[:split])
+    for ref in rest[:split]:
+        ship(ref)
     ready(cot_ref, z_ref)
-    grad_ref[:, 2 * width : 3 * width] = dot_tn(cot_ref[...], z_ref[...]).astype(BF)
-    emit_grad(where_ref, grad_ref, rest[:-2])
-    for ref in rest[:-2]:
+    down_ref[...] = dot_tn(cot_ref[...], z_ref[...]).astype(BF)
+    emit_far(where_ref, down_ref, rest[split:-3])
+    for ref in rest[split:-3]:
         ship(ref)
     ready(full_ref)
     w_scr[...] = full_ref[:, 2 * width : 3 * width]
@@ -453,7 +508,7 @@
 
 
 def back_kernel(width, ready, ship, where_ref, a_ref, b_ref, c_ref, d_ref, h_ref, cot_ref, gain_ref, full_ref, q_ref, k_ref, v_ref, o_ref, ab_ref,
-                n1_ref, cos_ref, sin_ref, om_ref, ot_ref, dh_ref, mine_ref, theirs_ref, *rest):
+                n1_ref, cos_ref, sin_ref, dh_ref, mine_ref, theirs_ref, *rest):
     grad_ref, low_scr, do_scr, w_scr, km_scr, qm_scr, dk_scr, dv_scr, dp_scr = rest[-9:]
     length = h_ref.shape[0]
     half = length // 2
@@ -527,38 +582,46 @@
     emit_grad(where_ref, grad_ref, rest[:-9])
     for ref in rest[:-9]:
         ship(ref)
-    ready(om_ref, ot_ref)
     for is_mine, first in halves(core, length):
-        out, other = (mine_ref, om_ref) if is_mine else (theirs_ref, ot_ref)
+        out = mine_ref if is_mine else theirs_ref
         rows = pl.ds(pl.multiple_of(first, half), half)
         part = dot_nt(dp_scr[0, rows, :], w_scr[0]) + dot_nt(dp_scr[1, rows, :], w_scr[1]) + dot_nt(dp_scr[2, rows, :], w_scr[2])
-        out[0] = part.astype(BF)
-        out[1] = other[...]
+        out[...] = part.astype(BF)
         ship(out)
 
 
-def output_kernel(ready, ship, where_ref, h_ref, tok_ref, dh_ref, gain_ref, a_ref, b_ref, c_ref, d_ref, out_ref, grad_ref):
-    length = h_ref.shape[0]
+def output_kernel(ready, ship, where_ref, h_ref, a_ref, b_ref, c_ref, d_ref, out_ref, sign_ref):
+    sign_ref[...] = jnp.zeros_like(sign_ref)
+    half = h_ref.shape[0] // 2
     core = where_ref[1] & 1
-    ready(h_ref, tok_ref, dh_ref, gain_ref, a_ref, b_ref, c_ref, d_ref)
+    ready(h_ref, a_ref, b_ref, c_ref, d_ref)
+    for is_mine, first in halves(core, 2 * half):
+        low, high = (a_ref, b_ref) if is_mine else (c_ref, d_ref)
+        rows = pl.ds(pl.multiple_of(first, half), half)
+        out_ref[rows, :] = h_ref[rows, :] + (low[...].astype(F32) + high[...].astype(F32))
+        ship(out_ref, rows)
+
+
+def input_grad_kernel(ready, ship, where_ref, tok_ref, dh_ref, gain_ref, a_ref, b_ref, c_ref, d_ref, grad_ref, sign_ref):
+    sign_ref[...] = jnp.zeros_like(sign_ref)
+    half = dh_ref.shape[0] // 2
+    core = where_ref[1] & 1
+    ready(dh_ref, tok_ref, gain_ref, a_ref, b_ref, c_ref, d_ref)
     gain = gain_ref[0:1, :]
-    for is_mine, first in halves(core, length):
+    for is_mine, first in halves(core, 2 * half):
         low, high = (a_ref, b_ref) if is_mine else (c_ref, d_ref)
 
         def step(i, _):
             at = pl.multiple_of(i * CHUNK, CHUNK)
             rows = pl.ds(pl.multiple_of(first + at, CHUNK), CHUNK)
             here = pl.ds(at, CHUNK)
-            out_ref[rows, :] = h_ref[rows, :] + (low[1, here, :].astype(F32) + high[1, here, :].astype(F32))
-            grad = low[0, here, :].astype(F32) + high[0, here, :].astype(F32)
+            grad = low[here, :].astype(F32) + high[here, :].astype(F32)
             hat, inverse = normalize(tok_ref[rows, :].astype(F32))
             grad_ref[rows, :] = dh_ref[rows, :] + norm_back(grad, gain, hat, inverse)
             return 0
 
-        lax.fori_loop(0, length // 2 // CHUNK, step, 0)
-        rows = pl.ds(pl.multiple_of(first, length // 2), length // 2)
-        ship(out_ref, rows)
-        ship(grad_ref, rows)
+        lax.fori_loop(0, half // CHUNK, step, 0)
+        ship(grad_ref, pl.ds(pl.multiple_of(first, half), half))
 
 
 def total_of(refs):
@@ -623,13 +686,14 @@
     operands = [piece for group in groups for piece in group]
     for leaf in leaves:
         operands += list(leaf)
-    outs = [(leaf[0].shape, F32) for leaf in leaves for _ in range(4)]
+    outs = [(leaf[0].shape, F32) for leaf in leaves for _ in range(4)] + [((8, 128), F32)]
 
     def kernel(*refs):
-        step_kernel([len(g) for g in groups], plan, *refs)
+        step_kernel([len(g) for g in groups], plan, *refs[:-1])
+        refs[-1][...] = jnp.zeros_like(refs[-1])
 
     flat = call(kernel, outs, operands, smem=0)
-    return [flat[4 * i : 4 * i + 4] for i in range(len(leaves))]
+    return [flat[4 * i : 4 * i + 4] for i in range(len(leaves))], flat[-1]
 
 
 def local(
@@ -657,12 +721,13 @@
     length, depth = tokens.shape
     half = length // 2
     where = jnp.stack([lax.axis_index("dp"), lax.axis_index("tensor")]).astype(jnp.int32)
-    pieces_a, masks_a, pieces_b, masks_b, early = gather_pieces(
+    cosine_table, sine_values = rope_tables(length, heads)
+    pieces_a, masks_a, pieces_b, masks_b, early, later = gather_pieces(
+        [cosine_table, sine_values],
         lambda deps: pack(w_qkv, w_out, gains, 0, deps), lambda deps: pack(w_in, w_down, gains, 1, deps)
     )
     wide_a, wide_b = pieces_a[0].shape[-1], pieces_b[0].shape[-1]
     repeat = heads // HEAD_DIM
-    cosine_table, sine_values = rope_tables(length, heads, pieces_a[1:2])
     segments = segment_ids.astype(jnp.int32)
 
     n1, q, k, v, o, ab, gain_one, mine, theirs, full_a = stream(
@@ -681,8 +746,10 @@
         ],
         [where, tokens, segments.reshape(length, 1), segments, cosine_table, sine_values, *pieces_a],
         [pltpu.VMEM((6, depth, heads), BF), pltpu.VMEM((repeat, length, heads), BF)],
-    )
-    terms = reduce_finish(reduce_start(mine, gate(theirs, early) if early else theirs))
+        near=(7, 8),
+        far=(1,),
+    )
+    terms = reduce_finish(reduce_start(mine, gate(theirs, early) if early else theirs, later))
     middle, n2, z, du, dv2, gain_two, mine, theirs, full_b = stream(
         lambda *refs: feed_kernel(masks_b, len(pieces_b), hidden, *refs),
         [
@@ -698,23 +765,35 @@
         ],
         [where, tokens, cotangent, *terms, *pieces_b],
         [pltpu.VMEM((3, depth, hidden), BF)],
+        near=(6, 7),
+        far=(1, 2),
     )
     chip = reduce_start(mine, theirs)
-    width = 3 * hidden
-    out_mine, out_theirs, *grad_feed = stream(
-        lambda *refs: feed_grad_kernel(hidden, *refs),
-        [((half, depth), BF), ((half, depth), BF)] + grad_outs(depth, width),
-        [where, n2, cotangent, z, du, dv2, full_b],
-        [pltpu.VMEM((depth, width), BF), pltpu.VMEM((depth, hidden), BF)],
+    in_outs, down_outs = grad_outs(depth, 2 * hidden), far_outs(depth, hidden)
+    split = len(in_outs)
+    out_mine, out_theirs, *grads = stream(
+        lambda *refs: feed_grad_kernel(hidden, split, *refs),
+        [((half, depth), BF), ((half, depth), BF)] + in_outs + down_outs,
+        [where, n2, du, dv2, cotangent, z, full_b],
+        [pltpu.VMEM((depth, 2 * hidden), BF), pltpu.VMEM((depth, hidden), BF), pltpu.VMEM((depth, hidden), BF)],
         deps=[chip],
-    )
+        near=range(2 + split + len(down_outs)),
+        far=range(1, 7),
+    )
+    out_chip = reduce_start(out_mine, out_theirs)
     terms = reduce_finish(chip, [out_mine])
-    feed_pieces, feed_got = scatter_start(where, grad_feed)
+    in_pieces, in_got, _unused = scatter_start(where, grads[:split])
+    down_finish, down_got = scatter_far_first(where, grads[split:])
+    out_chip = gate(out_chip, terms[1:2])
+    out_got = swap(out_chip, "tensor", 2)
+    small = ((8, 128), F32)
+    whole = ((length, depth), F32)
     width = 4 * heads
+    attn_outs = grad_outs(depth, width)
     dh, mine, theirs, *grad_attn = stream(
         lambda *refs: back_kernel(heads, *refs),
-        [((length, depth), F32), ((2, half, depth), BF), ((2, half, depth), BF)] + grad_outs(depth, width),
-        [where, *terms, middle, cotangent, gain_two, full_a, q, k, v, o, ab, n1, cosine_table, sine_values, out_mine, out_theirs],
+        [((length, depth), F32), ((half, depth), BF), ((half, depth), BF)] + attn_outs,
+        [where, *terms, middle, cotangent, gain_two, full_a, q, k, v, o, ab, n1, cosine_table, sine_values],
         [
             pltpu.VMEM((depth, width), BF),
             pltpu.VMEM((length, depth), BF),
@@ -726,24 +805,33 @@
             pltpu.VMEM((length, heads), F32),
             pltpu.VMEM((3, length, heads), BF),
         ],
-    )
-    attn_pieces, attn_got = scatter_start(where, grad_attn)
-    terms = reduce_finish(reduce_start(mine, gate(theirs, feed_got) if feed_got else theirs), feed_pieces[1:] + attn_got)
-    output, grad_tokens = stream(
-        output_kernel,
-        [((length, depth), F32), ((length, depth), F32)],
-        [where, middle, tokens, dh, gain_one, *terms],
-    )
-
-    gain_sum_two = gain_call([0, hidden], 1, w_in, gains, feed_pieces)
-    leaf_in, leaf_down = step_call(
-        [feed_pieces],
-        [(False, [(0, 0, hidden), (0, hidden, hidden)]), (True, [(0, 2 * hidden, hidden)])],
+        near=range(1, 3 + len(attn_outs)),
+        far=range(5, 17),
+        vmem=44,
+    )
+    theirs = gate(theirs, [out_got] + in_got + down_got)
+    out_terms = [out_chip, out_got, swap(out_chip, "tensor", 1), swap(out_got, "tensor", 1)]
+    attn_pieces, _unused, attn_pair = scatter_start(where, grad_attn, in_pieces[1:])
+    down_pieces = down_finish(attn_pair)
+    output, sign = stream(
+        output_kernel, [whole, small], [where, middle, *out_terms], near=(1,), far=(1,), vmem=10, deps=attn_pair
+    )
+    signs = [sign]
+    terms = reduce_finish(reduce_start(mine, theirs, out_terms[2:]), in_pieces[1:])
+    grad_tokens, sign = stream(
+        input_grad_kernel, [whole, small], [where, tokens, dh, gain_one, *terms], near=(1,), far=(1, 2), vmem=10
+    )
+    signs.append(sign)
+
+    gain_sum_two = gain_call([0, hidden], 1, w_in, gains, in_pieces)
+    (leaf_in, leaf_down), sign = step_call(
+        [in_pieces, down_pieces],
+        [(False, [(0, 0, hidden), (0, hidden, hidden)]), (True, [(1, 0, hidden)])],
         [(w_in, first_in, second_in), (w_down, first_down, second_down)],
     )
-    gain_sum_one = gain_call([0, heads, 2 * heads], 0, w_qkv, gains, attn_pieces, [grad_tokens, leaf_in[0]])
+    gain_sum_one = gain_call([0, heads, 2 * heads], 0, w_qkv, gains, attn_pieces, signs + [sign])
     share_gains = sum_small(jnp.concatenate([gain_sum_one[0:1], gain_sum_two[0:1]], axis=0))
-    leaf_qkv, leaf_out = step_call(
+    (leaf_qkv, leaf_out), _unused = step_call(
         [attn_pieces],
         [(False, [(0, 0, heads), (0, heads, heads), (0, 2 * heads, heads)]), (True, [(0, 3 * heads, heads)])],
         [(w_qkv, first_qkv, second_qkv), (w_out, first_out, second_out)],

time: 158 us -> 140 us (0.89)
  local copies, waits for them, and re-layouts: 17.7 us -> 0.28 us
  starting transfers between devices: 37.4 us -> 42.6 us
  waiting for transfers between devices: 43.2 us -> 40.2 us
  other arithmetic: 4.4 us -> 2.59 us
    unnamed x117 -> x39, local copies, waits for them, and re-layouts: 16.1 us -> 0.12 us
    ppermute x35 -> x43, starting transfers between devices: 37.4 us -> 42.6 us  [swap(): return lax.ppermute(values, axis, [(i, i ^ mask) for i in range(count)])]
    ppermute x35 -> x43, waiting for transfers between devices: 43.2 us -> 40.2 us  [swap(): return lax.ppermute(values, axis, [(i, i ^ mask) for i in range(count)])]
    pallas_call x7 -> x8, Pallas kernels: 47.5 us -> 45.9 us  [stream(): pl.pallas_call(body, out_shape=[jax.ShapeDtypeStruct(*out) if i in near e...]
    pallas_call x9 -> x11, Pallas kernels: 5.4 us -> 5.95 us  [call(): pl.pallas_call(body, out_shape=[jax.ShapeDtypeStruct(s, d) for s, d in ou...]
  transfers between devices with their start and end apart: 35 -> 43, of which waited for: 14 -> 16; matrix products, arithmetic and copies ran while one was open for 3% -> 2% of each run, Pallas kernels for 27% -> 31%
where the time goes in v3:
time: 140 us; the launch traced here: 139 us
  Pallas kernels  52.5 us (38%)
  starting transfers between devices  42.6 us (30%)
  waiting for transfers between devices  40.2 us (29%)
  other arithmetic  2.59 us (2%)
    pallas_call x8, Pallas kernels, stream(): pl.pallas_call(body, out_shape=[jax.ShapeDtypeStruct(*out) if i in near e...  45.9 us
    ppermute x43, starting transfers between devices, swap(): return lax.ppermute(values, axis, [(i, i ^ mask) for i in range(count)])  42.6 us
    ppermute x43, waiting for transfers between devices, swap(): return lax.ppermute(values, axis, [(i, i ^ mask) for i in range(count)])  40.2 us
    pallas_call x11, Pallas kernels, call(): pl.pallas_call(body, out_shape=[jax.ShapeDtypeStruct(s, d) for s, d in ou...  5.95 us
  transfers between devices with their start and end apart: 43, of which 16 were waited for; matrix products, arithmetic and copies ran while one was open for 2% of the time, Pallas kernels for 31%

profile of v3, /device:TPU:0, one launch (start us, length us, event | category | flops | bytes accessed | tf_op | source)
XLA Modules:
  0.0 139.4 jit_solution(11777630203254218829)
XLA Ops:
  1.9 3.0 %collective-permute-start.3 = (bf16[96,896]{1,0:T(8,128)(2,1)S(1)}, bf16[96,896]{1,0:T(8,128)(2,1)S(1)}, u32[]{:S(2)}, u32[]{:S(2)}) collective-permute-start(bf16[96,896]{1,0:T(8,128)(2,1)S(1)} %shard_map.345.refs_6_), channel_id=1, source_target_pairs={{0,4},{4,0},{8,12},{12,8},{16,20},{20,16},{24,28},{28,24},{1,5},{5... | collective-permute-start | bytes 516104 | tf_op jit(solution)/shard_map/ppermute | solution.py:52
  4.9 2.6 %collective-permute-start.1 = (bf16[96,896]{1,0:T(8,128)(2,1)S(1)}, bf16[96,896]{1,0:T(8,128)(2,1)S(1)}, u32[]{:S(2)}, u32[]{:S(2)}) collective-permute-start(bf16[96,896]{1,0:T(8,128)(2,1)S(1)} %shard_map.345.refs_6_), channel_id=1, source_target_pairs={{0,16},{4,20},{8,24},{12,28},{16,0},{20,4},{24,8},{28,12},{1,17},{... | collective-permute-start | bytes 516104 | tf_op jit(solution)/shard_map/ppermute | solution.py:52
  8.8 1.9 %fusion = (f32[512,192]{1,0:T(8,128)S(1)}, f32[512,192]{1,0:T(8,128)S(1)}) fusion(f32[192]{0:T(256)S(1)} %fusion.6), kind=kLoop, calls=%fused_computation.1 | loop fusion | flops 98304 | bytes 787200 | tf_op jit(solution)/shard_map/sin | solution.py:30
  11.2 1.7 %collective-permute-start = (bf16[96,896]{1,0:T(8,128)(2,1)S(1)}, bf16[96,896]{1,0:T(8,128)(2,1)S(1)}, u32[]{:S(2)}, u32[]{:S(2)}) collective-permute-start(bf16[96,896]{1,0:T(8,128)(2,1)S(1)} %shard_map.345.refs_6_), channel_id=1, source_target_pairs={{0,8},{4,12},{8,0},{12,4},{16,24},{20,28},{24,16},{28,20},{1,9},{5... | collective-permute-start | bytes 516104 | tf_op jit(solution)/shard_map/ppermute | solution.py:52
  12.9 7.3 %collective-permute-done.1.refs_8_.refs_1_ = bf16[96,896]{1,0:T(8,128)(2,1)S(1)} collective-permute-done((bf16[96,896]{1,0:T(8,128)(2,1)S(1)}, bf16[96,896]{1,0:T(8,128)(2,1)S(1)}, u32[]{:S(2)}, u32[]{:S(2)}) %collective-permute-start.1) | collective-permute-done | bytes 172064 | tf_op jit(solution)/shard_map/ppermute | solution.py:52
  21.9 1.6 %collective-permute-start.6 = (bf16[96,896]{1,0:T(8,128)(2,1)S(1)}, bf16[96,896]{1,0:T(8,128)(2,1)S(1)}, u32[]{:S(2)}, u32[]{:S(2)}) collective-permute-start(bf16[96,896]{1,0:T(8,128)(2,1)S(1)} %collective-permute-done.2.refs_9_.refs_2_), channel_id=1, source_target_pairs={{0,4},{4,0},{8,12},{12,8},{16,20},{20,16},{24,28},{28,24},{1,5},{5... | collective-permute-start | bytes 516104 | tf_op jit(solution)/shard_map/ppermute | solution.py:52
  24.0 3.3 %collective-permute-start.7 = (bf16[96,896]{1,0:T(8,128)(2,1)S(1)}, bf16[96,896]{1,0:T(8,128)(2,1)S(1)}, u32[]{:S(2)}, u32[]{:S(2)}) collective-permute-start(bf16[96,896]{1,0:T(8,128)(2,1)S(1)} %shard_map.349.refs_7_), channel_id=1, source_target_pairs={{0,16},{4,20},{8,24},{12,28},{16,0},{20,4},{24,8},{28,12},{1,17},{... | collective-permute-start | bytes 516104 | tf_op jit(solution)/shard_map/ppermute | solution.py:52
  27.4 1.6 %collective-permute-start.8 = (bf16[96,896]{1,0:T(8,128)(2,1)S(1)}, bf16[96,896]{1,0:T(8,128)(2,1)S(1)}, u32[]{:S(2)}, u32[]{:S(2)}) collective-permute-start(bf16[96,896]{1,0:T(8,128)(2,1)S(1)} %shard_map.349.refs_7_), channel_id=1, source_target_pairs={{0,24},{4,28},{8,16},{12,20},{16,8},{20,12},{24,0},{28,4},{1,25},{... | collective-permute-start | bytes 516104 | tf_op jit(solution)/shard_map/ppermute | solution.py:52
  29.8 11.0 %shard_map.347 = (bf16[512,768]{1,0:T(8,128)(2,1)}, bf16[512,192]{1,0:T(8,128)(2,1)}, bf16[512,192]{1,0:T(8,128)(2,1)}, bf16[512,192]{1,0:T(8,128)(2,1)}, bf16[5...) custom-call(s32[2]{0:T(128)S(1)} %pad_add_fusion.refs_0_, ...), custom_call_target="tpu_custom_call" | custom-call | tf_op jit(solution)/shard_map/pallas_call | solution.py:308
  45.8 8.4 %collective-permute-done.12.refs_4_ = bf16[256,768]{1,0:T(8,128)(2,1)S(1)} collective-permute-done((bf16[256,768]{1,0:T(8,128)(2,1)S(1)}, bf16[256,768]{1,0:T(8,128)(2,1)S(1)}, u32[]{:S(2)}, u32[]{:S(2)}) %collective-permute-start.12) | collective-permute-done | bytes 393248 | tf_op jit(solution)/shard_map/ppermute | solution.py:52
  54.2 3.9 %collective-permute-done.15.refs_10_ = bf16[3,96,896]{2,1,0:T(8,128)(2,1)S(1)} collective-permute-done((bf16[3,96,896]{2,1,0:T(8,128)(2,1)S(1)}, bf16[3,96,896]{2,1,0:T(8,128)(2,1)S(1)}, u32[]{:S(2)}, u32[]{:S(2)}) %collective-permute-start.15) | collective-permute-done | bytes 516128 | tf_op jit(solution)/shard_map/ppermute | solution.py:52
  58.1 8.3 %shard_map.353 = (f32[512,768]{1,0:T(8,128)}, bf16[512,768]{1,0:T(8,128)(2,1)}, bf16[512,288]{1,0:T(8,128)(2,1)}, bf16[512,288]{1,0:T(8,128)(2,1)}, bf16[512,288...) custom-call(s32[2]{0:T(128)S(1)} %pad_add_fusion.refs_0_, ...), custom_call_target="tpu_custom_call" | custom-call | tf_op jit(solution)/shard_map/pallas_call | solution.py:308
  66.5 1.7 %collective-permute-done.16.refs_1_ = bf16[256,768]{1,0:T(8,128)(2,1)S(1)} collective-permute-done((bf16[256,768]{1,0:T(8,128)(2,1)S(1)}, bf16[256,768]{1,0:T(8,128)(2,1)S(1)}, u32[]{:S(2)}, u32[]{:S(2)}) %collective-permute-start.16) | collective-permute-done | bytes 393248 | tf_op jit(solution)/shard_map/ppermute | solution.py:52
  68.8 4.9 %shard_map.355 = (bf16[256,768]{1,0:T(8,128)(2,1)S(1)}, bf16[256,768]{1,0:T(8,128)(2,1)S(1)}, bf16[4,96,576]{2,1,0:T(8,128)(2,1)S(1)}, bf16[4,96,576]{2,1,0:T(8,...) custom-call(s32[2]{0:T(128)S(1)} %pad_add_fusion.refs_0_, ...), custom_call_target="tpu_custom_call" | custom-call | tf_op jit(solution)/shard_map/pallas_call | solution.py:308
  74.3 5.2 %collective-permute-done.18.refs_0_ = bf16[256,768]{1,0:T(8,128)(2,1)S(1)} collective-permute-done((bf16[256,768]{1,0:T(8,128)(2,1)S(1)}, bf16[256,768]{1,0:T(8,128)(2,1)S(1)}, u32[]{:S(2)}, u32[]{:S(2)}) %collective-permute-start.18) | collective-permute-done | bytes 393248 | tf_op jit(solution)/shard_map/ppermute | solution.py:52
  82.6 2.2 %collective-permute-start.30 = (bf16[192,288]{1,0:T(8,128)(2,1)S(1)}, bf16[192,288]{1,0:T(8,128)(2,1)S(1)}, u32[]{:S(2)}, u32[]{:S(2)}) collective-permute-start(bf16[192,288]{1,0:T(8,128)(2,1)S(1)} %get-tuple-element.119), channel_id=1, source_target_pairs={{0,16},{4,20},{8,24},{12,28},{16,0},{20,4},{24,8},{28,12},{1,17},{... | collective-permute-start | bytes 331784 | tf_op jit(solution)/shard_map/ppermute | solution.py:52
  85.8 11.5 %shard_map.359 = (f32[512,768]{1,0:T(8,128)}, bf16[256,768]{1,0:T(8,128)(2,1)S(1)}, bf16[256,768]{1,0:T(8,128)(2,1)S(1)}, bf16[4,96,768]{2,1,0:T(8,128)(2,1)S(1)}, bf16[4,96,768]{2,1,0:T(8,128)(2,1)S(1)}) custom-call(s32[2]{0:T(128)S(1)} %pad_add_fusion.refs_0_, bf16[256,768]{1,0:T(8,128)(2,1)S(1)} %shard_map.354.refs_7_.refs_1_, ...), custom_call_target="tpu_custom_call" | custom-call | tf_op jit(solution)/shard_map/pallas_call | solution.py:308
  103.7 2.3 %collective-permute-start.27 = (bf16[96,576]{1,0:T(8,128)(2,1)S(1)}, bf16[96,576]{1,0:T(8,128)(2,1)S(1)}, u32[]{:S(2)}, u32[]{:S(2)}) collective-permute-start(bf16[96,576]{1,0:T(8,128)(2,1)S(1)} %get-tuple-element.110), channel_id=1, source_target_pairs={{0,16},{4,20},{8,24},{12,28},{16,0},{20,4},{24,8},{28,12},{1,17},{... | collective-permute-start | bytes 331784 | tf_op jit(solution)/shard_map/ppermute | solution.py:52
  107.1 2.3 %collective-permute-done.26.refs_3_.refs_1_ = bf16[96,576]{1,0:T(8,128)(2,1)S(1)} collective-permute-done((bf16[96,576]{1,0:T(8,128)(2,1)S(1)}, bf16[96,576]{1,0:T(8,128)(2,1)S(1)}, u32[]{:S(2)}, u32[]{:S(2)}) %collective-permute-start.26) | collective-permute-done | bytes 110624 | tf_op jit(solution)/shard_map/ppermute | solution.py:52
  109.3 6.7 %collective-permute-done.27.refs_4_.refs_2_ = bf16[96,576]{1,0:T(8,128)(2,1)S(1)} collective-permute-done((bf16[96,576]{1,0:T(8,128)(2,1)S(1)}, bf16[96,576]{1,0:T(8,128)(2,1)S(1)}, u32[]{:S(2)}, u32[]{:S(2)}) %collective-permute-start.27) | collective-permute-done | bytes 110624 | tf_op jit(solution)/shard_map/ppermute | solution.py:52
  118.9 1.9 %collective-permute-start.36 = (bf16[96,768]{1,0:T(8,128)(2,1)S(1)}, bf16[96,768]{1,0:T(8,128)(2,1)S(1)}, u32[]{:S(2)}, u32[]{:S(2)}) collective-permute-start(bf16[96,768]{1,0:T(8,128)(2,1)S(1)} %get-tuple-element.122), channel_id=1, source_target_pairs={{0,8},{4,12},{8,0},{12,4},{16,24},{20,28},{24,16},{28,20},{1,9},{5... | collective-permute-start | bytes 442376 | tf_op jit(solution)/shard_map/ppermute | solution.py:52
  122.2 2.2 %collective-permute-start.38 = (bf16[96,768]{1,0:T(8,128)(2,1)S(1)}, bf16[96,768]{1,0:T(8,128)(2,1)S(1)}, u32[]{:S(2)}, u32[]{:S(2)}) collective-permute-start(bf16[96,768]{1,0:T(8,128)(2,1)S(1)} %get-tuple-element.124), channel_id=1, source_target_pairs={{0,24},{4,28},{8,16},{12,20},{16,8},{20,12},{24,0},{28,4},{1,25},{... | collective-permute-start | bytes 442376 | tf_op jit(solution)/shard_map/ppermute | solution.py:52
  124.6 3.3 %shard_map.362 = (f32[512,768]{1,0:T(8,128)}, f32[8,128]{1,0:T(8,128)S(1)}) custom-call(s32[2]{0:T(128)S(1)} %pad_add_fusion.refs_0_, f32[512,768]{1,0:T(8,128)} %get-tuple-element.87.refs_5_.refs_1_, bf16[256,768]{1,0:T(8,128)(2,1)S(1)} %shard_map.358.refs_2_, bf16[256,768]{1,0:T(8,128)(2,1)S(1)} %collective-permute-done.19.refs_3_.refs_1_, ...), custom_call_target="tpu_custom_call" | custom-call | tf_op jit(solution)/shard_map/pallas_call | solution.py:308
  129.7 4.5 %shard_map.366 = (f32[512,768]{1,0:T(8,128)}, f32[8,128]{1,0:T(8,128)S(1)}) custom-call(s32[2]{0:T(128)S(1)} %pad_add_fusion.refs_0_, bf16[512,768]{1,0:T(8,128)(2,1)} %refs_1_.11, f32[512,768]{1,0:T(8,128)} %get-tuple-element.114.refs_2_, f32[8,768]{1,0:T(8,128)S(1)} %copy-done.15, bf16[256,768]{1,0:T(8,128)(2,1)S(1)} %shard_map.364.refs_4_, ...), custom_call_target="tpu_custom_call" | custom-call | tf_op jit(solution)/shard_map/pallas_call | solution.py:308
  (136 shorter events, 34.9 us)
Async XLA Ops:
  4.9 15.3 %collective-permute-start.1 = (bf16[96,896]{1,0:T(8,128)(2,1)S(1)}, bf16[96,896]{1,0:T(8,128)(2,1)S(1)}, u32[]{:S(2)}, u32[]{:S(2)}) collective-permute-start(bf16[96,896]{1,0:T(8,128)(2,1)S(1)} %shard_map.345.refs_6_), channel_id=1, source_target_pairs={{0,16},{4,20},{8,24},{12,28},{16,0},{20,4},{24,8},{28,12},{1,17},{... | collective-permute-start | bytes 516104 | tf_op jit(solution)/shard_map/ppermute | solution.py:52
  7.5 14.4 %collective-permute-start.2 = (bf16[96,896]{1,0:T(8,128)(2,1)S(1)}, bf16[96,896]{1,0:T(8,128)(2,1)S(1)}, u32[]{:S(2)}, u32[]{:S(2)}) collective-permute-start(bf16[96,896]{1,0:T(8,128)(2,1)S(1)} %shard_map.345.refs_6_), channel_id=1, source_target_pairs={{0,24},{4,28},{8,16},{12,20},{16,8},{20,12},{24,0},{28,4},{1,25},{... | collective-permute-start | bytes 516104 | tf_op jit(solution)/shard_map/ppermute | solution.py:52
  10.8 12.8 %collective-permute-start.4 = (bf16[96,896]{1,0:T(8,128)(2,1)S(1)}, bf16[96,896]{1,0:T(8,128)(2,1)S(1)}, u32[]{:S(2)}, u32[]{:S(2)}) collective-permute-start(bf16[96,896]{1,0:T(8,128)(2,1)S(1)} %shard_map.346), channel_id=1, source_target_pairs={{0,8},{4,12},{8,0},{12,4},{16,24},{20,28},{24,16},{28,20},{1,9},{5... | collective-permute-start | bytes 516104 | tf_op jit(solution)/shard_map/ppermute | solution.py:52
  11.2 16.2 %collective-permute-start = (bf16[96,896]{1,0:T(8,128)(2,1)S(1)}, bf16[96,896]{1,0:T(8,128)(2,1)S(1)}, u32[]{:S(2)}, u32[]{:S(2)}) collective-permute-start(bf16[96,896]{1,0:T(8,128)(2,1)S(1)} %shard_map.345.refs_6_), channel_id=1, source_target_pairs={{0,8},{4,12},{8,0},{12,4},{16,24},{20,28},{24,16},{28,20},{1,9},{5... | collective-permute-start | bytes 516104 | tf_op jit(solution)/shard_map/ppermute | solution.py:52
  23.6 17.2 %collective-permute-start.10 = (bf16[96,896]{1,0:T(8,128)(2,1)S(1)}, bf16[96,896]{1,0:T(8,128)(2,1)S(1)}, u32[]{:S(2)}, u32[]{:S(2)}) collective-permute-start(bf16[96,896]{1,0:T(8,128)(2,1)S(1)} %shard_map.349.refs_7_), channel_id=1, source_target_pairs={{0,4},{4,0},{8,12},{12,8},{16,20},{20,16},{24,28},{28,24},{1,5},{5... | collective-permute-start | bytes 516104 | tf_op jit(solution)/shard_map/ppermute | solution.py:52
  24.0 16.8 %collective-permute-start.7 = (bf16[96,896]{1,0:T(8,128)(2,1)S(1)}, bf16[96,896]{1,0:T(8,128)(2,1)S(1)}, u32[]{:S(2)}, u32[]{:S(2)}) collective-permute-start(bf16[96,896]{1,0:T(8,128)(2,1)S(1)} %shard_map.349.refs_7_), channel_id=1, source_target_pairs={{0,16},{4,20},{8,24},{12,28},{16,0},{20,4},{24,8},{28,12},{1,17},{... | collective-permute-start | bytes 516104 | tf_op jit(solution)/shard_map/ppermute | solution.py:52
  27.4 13.5 %collective-permute-start.8 = (bf16[96,896]{1,0:T(8,128)(2,1)S(1)}, bf16[96,896]{1,0:T(8,128)(2,1)S(1)}, u32[]{:S(2)}, u32[]{:S(2)}) collective-permute-start(bf16[96,896]{1,0:T(8,128)(2,1)S(1)} %shard_map.349.refs_7_), channel_id=1, source_target_pairs={{0,24},{4,28},{8,16},{12,20},{16,8},{20,12},{24,0},{28,4},{1,25},{... | collective-permute-start | bytes 516104 | tf_op jit(solution)/shard_map/ppermute | solution.py:52
  29.0 12.2 %collective-permute-start.9 = (bf16[96,896]{1,0:T(8,128)(2,1)S(1)}, bf16[96,896]{1,0:T(8,128)(2,1)S(1)}, u32[]{:S(2)}, u32[]{:S(2)}) collective-permute-start(bf16[96,896]{1,0:T(8,128)(2,1)S(1)} %shard_map.349.refs_7_), channel_id=1, source_target_pairs={{0,8},{4,12},{8,0},{12,4},{16,24},{20,28},{24,16},{28,20},{1,9},{5... | collective-permute-start | bytes 516104 | tf_op jit(solution)/shard_map/ppermute | solution.py:52
  43.0 11.2 %collective-permute-start.12 = (bf16[256,768]{1,0:T(8,128)(2,1)S(1)}, bf16[256,768]{1,0:T(8,128)(2,1)S(1)}, u32[]{:S(2)}, u32[]{:S(2)}) collective-permute-start(bf16[256,768]{1,0:T(8,128)(2,1)S(1)} %shard_map.352.refs_3_), channel_id=1, source_target_pairs={{0,2},{1,3},{2,0},{3,1},{4,6},{5,7},{6,4},{7,5},{8,10},{9,11},{10,... | collective-permute-start | bytes 1179656 | tf_op jit(solution)/shard_map/ppermute | solution.py:52
  44.6 13.5 %collective-permute-start.15 = (bf16[3,96,896]{2,1,0:T(8,128)(2,1)S(1)}, bf16[3,96,896]{2,1,0:T(8,128)(2,1)S(1)}, u32[]{:S(2)}, u32[]{:S(2)}) collective-permute-start(bf16[3,96,896]{2,1,0:T(8,128)(2,1)S(1)} %shard_map.351.refs_2_.refs_8_), channel_id=1, source_target_pairs={{0,4},{4,0},{8,12},{12,8},{16,20},{20,16},{24,28},{28,24},{1,5},{5... | collective-permute-start | bytes 1548296 | tf_op jit(solution)/shard_map/ppermute | solution.py:52
  45.8 12.3 %collective-permute-start.13 = (bf16[256,768]{1,0:T(8,128)(2,1)S(1)}, bf16[256,768]{1,0:T(8,128)(2,1)S(1)}, u32[]{:S(2)}, u32[]{:S(2)}) collective-permute-start(bf16[256,768]{1,0:T(8,128)(2,1)S(1)} %shard_map.352.refs_3_), channel_id=1, source_target_pairs={{0,1},{1,0},{2,3},{3,2},{4,5},{5,4},{6,7},{7,6},{8,9},{9,8},{10,11... | collective-permute-start | bytes 1179656 | tf_op jit(solution)/shard_map/ppermute | solution.py:52
  79.5 17.9 %collective-permute-start.25 = (bf16[4,96,576]{2,1,0:T(8,128)(2,1)S(1)}, bf16[4,96,576]{2,1,0:T(8,128)(2,1)S(1)}, u32[]{:S(2)}, u32[]{:S(2)}) collective-permute-start(bf16[4,96,576]{2,1,0:T(8,128)(2,1)S(1)} %get-tuple-element.108), channel_id=1, source_target_pairs={{0,4},{4,0},{8,12},{12,8},{16,20},{20,16},{24,28},{28,24},{1,5},{5... | collective-permute-start | bytes 1327112 | tf_op jit(solution)/shard_map/ppermute | solution.py:52
  80.9 16.6 %collective-permute-start.19 = (bf16[256,768]{1,0:T(8,128)(2,1)S(1)}, bf16[256,768]{1,0:T(8,128)(2,1)S(1)}, u32[]{:S(2)}, u32[]{:S(2)}) collective-permute-start(bf16[256,768]{1,0:T(8,128)(2,1)S(1)} %shard_map.358.refs_2_), channel_id=1, source_target_pairs={{0,2},{1,3},{2,0},{3,1},{4,6},{5,7},{6,4},{7,5},{8,10},{9,11},{10,... | collective-permute-start | bytes 1179656 | tf_op jit(solution)/shard_map/ppermute | solution.py:52
  81.4 15.9 %collective-permute-start.29 = (bf16[192,288]{1,0:T(8,128)(2,1)S(1)}, bf16[192,288]{1,0:T(8,128)(2,1)S(1)}, u32[]{:S(2)}, u32[]{:S(2)}) collective-permute-start(bf16[192,288]{1,0:T(8,128)(2,1)S(1)} %get-tuple-element.118), channel_id=1, source_target_pairs={{0,8},{4,12},{8,0},{12,4},{16,24},{20,28},{24,16},{28,20},{1,9},{5... | collective-permute-start | bytes 331784 | tf_op jit(solution)/shard_map/ppermute | solution.py:52
  82.6 14.9 %collective-permute-start.30 = (bf16[192,288]{1,0:T(8,128)(2,1)S(1)}, bf16[192,288]{1,0:T(8,128)(2,1)S(1)}, u32[]{:S(2)}, u32[]{:S(2)}) collective-permute-start(bf16[192,288]{1,0:T(8,128)(2,1)S(1)} %get-tuple-element.119), channel_id=1, source_target_pairs={{0,16},{4,20},{8,24},{12,28},{16,0},{20,4},{24,8},{28,12},{1,17},{... | collective-permute-start | bytes 331784 | tf_op jit(solution)/shard_map/ppermute | solution.py:52
  84.8 12.7 %collective-permute-start.31 = (bf16[192,288]{1,0:T(8,128)(2,1)S(1)}, bf16[192,288]{1,0:T(8,128)(2,1)S(1)}, u32[]{:S(2)}, u32[]{:S(2)}) collective-permute-start(bf16[192,288]{1,0:T(8,128)(2,1)S(1)} %get-tuple-element.120), channel_id=1, source_target_pairs={{0,24},{4,28},{8,16},{12,20},{16,8},{20,12},{24,0},{28,4},{1,25},{... | collective-permute-start | bytes 331784 | tf_op jit(solution)/shard_map/ppermute | solution.py:52
  98.1 18.0 %collective-permute-start.24 = (bf16[4,96,768]{2,1,0:T(8,128)(2,1)S(1)}, bf16[4,96,768]{2,1,0:T(8,128)(2,1)S(1)}, u32[]{:S(2)}, u32[]{:S(2)}) collective-permute-start(bf16[4,96,768]{2,1,0:T(8,128)(2,1)S(1)} %get-tuple-element.106), channel_id=1, source_target_pairs={{0,4},{4,0},{8,12},{12,8},{16,20},{20,16},{24,28},{28,24},{1,5},{5... | collective-permute-start | bytes 1769480 | tf_op jit(solution)/shard_map/ppermute | solution.py:52
  100.3 15.7 %collective-permute-start.33 = (bf16[256,768]{1,0:T(8,128)(2,1)S(1)}, bf16[256,768]{1,0:T(8,128)(2,1)S(1)}, u32[]{:S(2)}, u32[]{:S(2)}) collective-permute-start(bf16[256,768]{1,0:T(8,128)(2,1)S(1)} %shard_map.364.refs_4_), channel_id=1, source_target_pairs={{0,2},{1,3},{2,0},{3,1},{4,6},{5,7},{6,4},{7,5},{8,10},{9,11},{10,... | collective-permute-start | bytes 1179656 | tf_op jit(solution)/shard_map/ppermute | solution.py:52
  103.7 12.3 %collective-permute-start.27 = (bf16[96,576]{1,0:T(8,128)(2,1)S(1)}, bf16[96,576]{1,0:T(8,128)(2,1)S(1)}, u32[]{:S(2)}, u32[]{:S(2)}) collective-permute-start(bf16[96,576]{1,0:T(8,128)(2,1)S(1)} %get-tuple-element.110), channel_id=1, source_target_pairs={{0,16},{4,20},{8,24},{12,28},{16,0},{20,4},{24,8},{28,12},{1,17},{... | collective-permute-start | bytes 331784 | tf_op jit(solution)/shard_map/ppermute | solution.py:52
  109.3 20.3 %collective-permute-start.34 = (bf16[256,768]{1,0:T(8,128)(2,1)S(1)}, bf16[256,768]{1,0:T(8,128)(2,1)S(1)}, u32[]{:S(2)}, u32[]{:S(2)}) collective-permute-start(bf16[256,768]{1,0:T(8,128)(2,1)S(1)} %shard_map.364.refs_4_), channel_id=1, source_target_pairs={{0,1},{1,0},{2,3},{3,2},{4,5},{5,4},{6,7},{7,6},{8,9},{9,8},{10,11... | collective-permute-start | bytes 1179656 | tf_op jit(solution)/shard_map/ppermute | solution.py:52
  116.1 13.6 %collective-permute-start.35 = (bf16[256,768]{1,0:T(8,128)(2,1)S(1)}, bf16[256,768]{1,0:T(8,128)(2,1)S(1)}, u32[]{:S(2)}, u32[]{:S(2)}) collective-permute-start(bf16[256,768]{1,0:T(8,128)(2,1)S(1)} %shard_map.365.refs_5_), channel_id=1, source_target_pairs={{0,1},{1,0},{2,3},{3,2},{4,5},{5,4},{6,7},{7,6},{8,9},{9,8},{10,11... | collective-permute-start | bytes 1179656 | tf_op jit(solution)/shard_map/ppermute | solution.py:52
  118.9 15.3 %collective-permute-start.36 = (bf16[96,768]{1,0:T(8,128)(2,1)S(1)}, bf16[96,768]{1,0:T(8,128)(2,1)S(1)}, u32[]{:S(2)}, u32[]{:S(2)}) collective-permute-start(bf16[96,768]{1,0:T(8,128)(2,1)S(1)} %get-tuple-element.122), channel_id=1, source_target_pairs={{0,8},{4,12},{8,0},{12,4},{16,24},{20,28},{24,16},{28,20},{1,9},{5... | collective-permute-start | bytes 442376 | tf_op jit(solution)/shard_map/ppermute | solution.py:52
  120.8 13.9 %collective-permute-start.37 = (bf16[96,768]{1,0:T(8,128)(2,1)S(1)}, bf16[96,768]{1,0:T(8,128)(2,1)S(1)}, u32[]{:S(2)}, u32[]{:S(2)}) collective-permute-start(bf16[96,768]{1,0:T(8,128)(2,1)S(1)} %get-tuple-element.123), channel_id=1, source_target_pairs={{0,16},{4,20},{8,24},{12,28},{16,0},{20,4},{24,8},{28,12},{1,17},{... | collective-permute-start | bytes 442376 | tf_op jit(solution)/shard_map/ppermute | solution.py:52
  122.2 12.6 %collective-permute-start.38 = (bf16[96,768]{1,0:T(8,128)(2,1)S(1)}, bf16[96,768]{1,0:T(8,128)(2,1)S(1)}, u32[]{:S(2)}, u32[]{:S(2)}) collective-permute-start(bf16[96,768]{1,0:T(8,128)(2,1)S(1)} %get-tuple-element.124), channel_id=1, source_target_pairs={{0,24},{4,28},{8,16},{12,20},{16,8},{20,12},{24,0},{28,4},{1,25},{... | collective-permute-start | bytes 442376 | tf_op jit(solution)/shard_map/ppermute | solution.py:52
  (38 other events, 265.7 us)

commit v4 on v3

--- a/solution.py
+++ b/solution.py
@@ -22,12 +22,12 @@
 F32 = jnp.float32
 
 
-def rope_tables(count, width):
+def rope_tables(count):
     half_dim = HEAD_DIM // 2
-    spot = (jnp.arange(width) % half_dim).astype(jnp.float32)
-    frequency = rope_base ** (-(spot * 2.0 / HEAD_DIM))
+    lane = jnp.arange(2 * HEAD_DIM)
+    frequency = rope_base ** (-((lane % half_dim).astype(jnp.float32) * 2.0 / HEAD_DIM))
     angles = jnp.arange(count, dtype=jnp.float32)[:, None] * frequency[None, :]
-    return (jnp.cos(angles), jnp.sin(angles))
+    return jnp.where(lane[None, :] < HEAD_DIM, jnp.cos(angles), jnp.sin(angles))
 
 
 def gelu_parts(inputs):
@@ -97,49 +97,6 @@
     return [parts[0]] + [swap(parts[m], "dp", 2 * m) for m in range(1, len(parts))], [got], [parts[0]]
 
 
-def far_kernel(where_ref, *refs):
-    terms, (own_ref, send_ref) = refs[:-2], refs[-2:]
-    rows = own_ref.shape[0]
-    odd = where_ref[0] & 1
-    for ref, at in ((own_ref, odd), (send_ref, 1 - odd)):
-        span = pl.ds(pl.multiple_of(at * rows, rows), rows)
-        total = terms[0][span, :].astype(F32)
-        for term in terms[1:]:
-            total = total + term[span, :].astype(F32)
-        ref[...] = total.astype(BF)
-
-
-def scatter_far_first(where, grads):
-    if len(grads) == 1:
-        pieces, got, _unused = scatter_start(where, grads)
-        return lambda deps: pieces, got
-    got = [swap(grads[m], "dp", 2 * m) for m in range(1, len(grads))]
-    rows, width = grads[0].shape
-
-    def finish(deps):
-        own, send = call(far_kernel, [((rows // 2, width), BF)] * 2, [where, grads[0], *got], deps=deps)
-        return [own, swap(send, "dp", 1)]
-
-    return finish, got
-
-
-def far_outs(depth, width):
-    count = lax.axis_size("dp")
-    if count != 8:
-        return [((depth, width), BF)]
-    return [((2 * depth // count, width), BF)] * (count // 2)
-
-
-def emit_far(where_ref, grad_scr, refs):
-    level = where_ref[0] >> 1
-    for m, ref in enumerate(refs):
-        if len(refs) == 1:
-            ref[...] = grad_scr[...]
-        else:
-            at = pl.multiple_of((level ^ m) * ref.shape[0], ref.shape[0])
-            ref[...] = grad_scr[pl.ds(at, ref.shape[0]), :]
-
-
 def grad_outs(depth, width):
     count = lax.axis_size("dp")
     if count != 8:
@@ -198,6 +155,12 @@
     return jnp.where(head_mask(values.shape[0], values.shape[1], head), values, jnp.zeros_like(values))
 
 
+def spread(table, width):
+    count = width // HEAD_DIM
+    cosine, sine = table[:, :HEAD_DIM], table[:, HEAD_DIM:]
+    return jnp.concatenate([cosine] * count, axis=1), jnp.concatenate([sine] * count, axis=1)
+
+
 def turn_matrix(width):
     half = HEAD_DIM // 2
     source = lax.broadcasted_iota(jnp.int32, (width, width), 0)
@@ -256,24 +219,34 @@
     )(*operands, *deps)
 
 
-def stream(kernel, outs, operands, scratch=(), smem=1, deps=(), vmem=40, near=(), far=()):
+def stream(kernel, outs, operands, scratch=(), smem=1, deps=(), vmem=40, near=(), far=(), here=(), stages=(), cost=None):
     count, total = len(operands), len(outs)
-    late = count - smem
-    room = [pltpu.VMEM(x.shape, x.dtype) for x in operands[smem:]]
+    moved = [i for i in range(smem, count) if i not in here]
+    late = len(moved)
+    room = [pltpu.VMEM(operands[i].shape, operands[i].dtype) for i in moved]
     room += [pltpu.VMEM(*out) for i, out in enumerate(outs) if i not in near]
     gone = total - len(near)
 
     def body(*refs):
-        given, results = refs[smem:count], refs[count + len(deps) : count + len(deps) + total]
+        given, results = refs[:count], refs[count + len(deps) : count + len(deps) + total]
         own = refs[count + len(deps) + total :]
         flags, own = own[-1], own[:-1]
         own, held, made = own[: -late - gone], own[-late - gone : -gone or None], list(own[len(own) - gone :])
         for i in sorted(near):
             made.insert(i, results[i])
-        copies = [pltpu.make_async_copy(given[i], held[i], flags.at[i]) for i in range(late)]
-        for copy in copies:
-            copy.start()
+        copies = [pltpu.make_async_copy(given[i], held[n], flags.at[n]) for n, i in enumerate(moved)]
         waiting = {id(ref): copy for ref, copy in zip(held, copies)}
+        inputs = list(given[smem:])
+        for n, i in enumerate(moved):
+            inputs[i - smem] = held[n]
+        queue = list(zip(moved, copies))
+
+        def launch():
+            first = True
+            while queue and (first or queue[0][0] not in stages):
+                queue.pop(0)[1].start()
+                first = False
+
         place = {id(ref): i for i, ref in enumerate(made) if i not in near}
         sent = []
         shipped = {}
@@ -281,8 +254,11 @@
         def ready(*wanted):
             for ref in wanted:
                 copy = waiting.pop(id(ref), None)
+                while any(copy is other for _unused, other in queue):
+                    launch()
                 if copy is not None:
                     copy.wait()
+            launch()
 
         def ship(ref, rows=None):
             i = place.get(id(ref))
@@ -295,7 +271,8 @@
             copy.start()
             sent.append(copy)
 
-        kernel(ready, ship, *refs[:smem], *held, *made, *own)
+        launch()
+        kernel(ready, ship, *refs[:smem], *inputs, *made, *own)
         ready(*held)
         for i, ref in enumerate(made):
             if i not in shipped:
@@ -308,10 +285,13 @@
     return pl.pallas_call(
         body,
         out_shape=[jax.ShapeDtypeStruct(*out) if i in near else pltpu.HBM(*out) for i, out in enumerate(outs)],
-        in_specs=[pl.BlockSpec(memory_space=pltpu.SMEM)] * smem + [anywhere] * (late + len(deps)),
+        in_specs=[pl.BlockSpec(memory_space=pltpu.SMEM)] * smem
+        + [pl.BlockSpec() if i in here else anywhere for i in range(smem, count)]
+        + [anywhere] * len(deps),
         out_specs=[pl.BlockSpec() if i in near else anywhere for i in range(total)],
         scratch_shapes=list(scratch) + room + [pltpu.SemaphoreType.DMA((late + 2 * total,))],
         compiler_params=pltpu.CompilerParams(vmem_limit_bytes=vmem * 1024 * 1024),
+        cost_estimate=None if cost is None else pl.CostEstimate(flops=cost, bytes_accessed=cost, transcendentals=0),
     )(*pinned, *deps)
 
 
@@ -358,7 +338,7 @@
     )(*pieces)
 
 
-CHUNK = 128
+CHUNK = 256
 
 
 def halves(core, length):
@@ -366,7 +346,7 @@
     return ((False, (1 - core) * half), (True, core * half))
 
 
-def attention_kernel(masks, count, width, ready, ship, where_ref, tok_ref, segc_ref, segr_ref, cos_ref, sin_ref, *rest):
+def attention_kernel(masks, count, width, ready, ship, where_ref, tok_ref, segc_ref, segr_ref, table_ref, *rest):
     pieces = rest[:count]
     n1_ref, q_ref, k_ref, v_ref, o_ref, ab_ref, gain_ref, mine_ref, theirs_ref, full_ref, w_scr, vm_scr = rest[count:]
     length = tok_ref.shape[0]
@@ -382,14 +362,14 @@
     for s in range(2):
         w_scr[3 + s] = dot(w_scr[s], turn).astype(BF)
     w_scr[5] = full_ref[:, 3 * width : 4 * width]
-    ready(tok_ref, cos_ref, sin_ref, segc_ref, segr_ref)
+    ready(tok_ref, table_ref, segc_ref, segr_ref)
 
     def project(i, _):
         rows = pl.ds(pl.multiple_of(i * CHUNK, CHUNK), CHUNK)
         hat, _unused = normalize(tok_ref[rows, :].astype(F32))
         normed = (hat * gain).astype(BF)
         n1_ref[rows, :] = normed
-        cosine, sine = cos_ref[rows, :], sin_ref[rows, :]
+        cosine, sine = spread(table_ref[rows, :], width)
         q_ref[rows, :] = (dot(normed, w_scr[0]) * cosine + dot(normed, w_scr[3]) * sine).astype(BF)
         k_ref[rows, :] = (dot(normed, w_scr[1]) * cosine + dot(normed, w_scr[4]) * sine).astype(BF)
         v_ref[rows, :] = dot(normed, w_scr[2]).astype(BF)
@@ -431,17 +411,18 @@
 
 def feed_kernel(masks, count, width, ready, ship, where_ref, tok_ref, cot_ref, a_ref, b_ref, c_ref, d_ref, *rest):
     pieces = rest[:count]
-    (h_ref, n2_ref, z_ref, du_ref, dv_ref, gain_ref, mine_ref, theirs_ref, full_ref, w_scr) = rest[count:]
+    (h_ref, n2_ref, z_ref, du_ref, dv_ref, gain_ref, mine_ref, theirs_ref, wd_ref, full_ref, w_scr) = rest[count:]
     length = tok_ref.shape[0]
     core = where_ref[1] & 1
     ready(*pieces)
     place_pieces(where_ref, pieces, masks, full_ref)
-    ship(full_ref)
     last = 3 * width // 128 * 128
     gain = column_as_row(full_ref[:, last:], 3 * width - last)
     gain_ref[...] = jnp.broadcast_to(gain, gain_ref.shape)
-    for s in range(3):
+    for s in range(2):
         w_scr[s] = full_ref[:, s * width : (s + 1) * width]
+    wd_ref[...] = full_ref[:, 2 * width : 3 * width]
+    ship(wd_ref)
     ready(tok_ref, cot_ref, a_ref, b_ref, c_ref, d_ref)
     for is_mine, first in halves(core, length):
         low, high = (a_ref, b_ref) if is_mine else (c_ref, d_ref)
@@ -458,7 +439,7 @@
             up, gate = dot(normed, w_scr[0]), dot(normed, w_scr[1])
             value, slope = gelu_parts(up)
             z_ref[rows, :] = (value * gate).astype(BF)
-            back = dot(cot_ref[rows, :], w_scr[2])
+            back = dot(cot_ref[rows, :], wd_ref[...])
             du, dv = (back * gate * slope).astype(BF), (back * value).astype(BF)
             du_ref[rows, :] = du
             dv_ref[rows, :] = dv
@@ -477,27 +458,21 @@
         ship(mine_ref if is_mine else theirs_ref)
 
 
-def feed_grad_kernel(width, split, ready, ship, where_ref, n2_ref, du_ref, dv_ref, cot_ref, z_ref, full_ref, mine_ref, theirs_ref, *rest):
-    grad_ref, down_ref, w_scr = rest[-3:]
+def feed_grad_kernel(width, ready, ship, where_ref, n2_ref, du_ref, dv_ref, cot_ref, z_ref, wd_ref, mine_ref, theirs_ref, *rest):
+    grad_ref = rest[-1]
     ready(n2_ref, du_ref)
     grad_ref[:, 0:width] = dot_tn(n2_ref[...], du_ref[...]).astype(BF)
     ready(dv_ref)
     grad_ref[:, width : 2 * width] = dot_tn(n2_ref[...], dv_ref[...]).astype(BF)
-    emit_grad(where_ref, grad_ref, rest[:split])
-    for ref in rest[:split]:
-        ship(ref)
     ready(cot_ref, z_ref)
-    down_ref[...] = dot_tn(cot_ref[...], z_ref[...]).astype(BF)
-    emit_far(where_ref, down_ref, rest[split:-3])
-    for ref in rest[split:-3]:
-        ship(ref)
-    ready(full_ref)
-    w_scr[...] = full_ref[:, 2 * width : 3 * width]
+    grad_ref[:, 2 * width : 3 * width] = dot_tn(cot_ref[...], z_ref[...]).astype(BF)
+    emit_grad(where_ref, grad_ref, rest[:-1])
+    ready(wd_ref)
     length = z_ref.shape[0]
     core = where_ref[1] & 1
     for is_mine, first in halves(core, length):
         rows = pl.ds(pl.multiple_of(first, length // 2), length // 2)
-        part = dot_nt(z_ref[rows, :], w_scr[...]).astype(BF)
+        part = dot_nt(z_ref[rows, :], wd_ref[...]).astype(BF)
         if is_mine:
             mine_ref[...] = part
         else:
@@ -508,7 +483,7 @@
 
 
 def back_kernel(width, ready, ship, where_ref, a_ref, b_ref, c_ref, d_ref, h_ref, cot_ref, gain_ref, full_ref, q_ref, k_ref, v_ref, o_ref, ab_ref,
-                n1_ref, cos_ref, sin_ref, dh_ref, mine_ref, theirs_ref, *rest):
+                n1_ref, table_ref, dh_ref, mine_ref, theirs_ref, *rest):
     grad_ref, low_scr, do_scr, w_scr, km_scr, qm_scr, dk_scr, dv_scr, dp_scr = rest[-9:]
     length = h_ref.shape[0]
     half = length // 2
@@ -546,7 +521,7 @@
         qm_scr[h, :, 0:width] = only_head(q_ref[...], h)
         qm_scr[h, :, 256 : 256 + width] = only_head(qt, h)
 
-    ready(cos_ref, sin_ref)
+    ready(table_ref)
     for i in range(length // SPAN):
         rows = pl.ds(i * SPAN, SPAN)
         grad_o = do_scr[rows, :]
@@ -566,14 +541,16 @@
             dq = term if dq is None else dq + term
             term = dot_tn(ds, qm_scr[h, rows, :])
             dk = term if dk is None else dk + term
-        dp_scr[0, rows, :] = (dq[:, :width] * cos_ref[rows, :] + dq[:, 256 : 256 + width] * sin_ref[rows, :]).astype(BF)
+        cosine, sine = spread(table_ref[rows, :], width)
+        dp_scr[0, rows, :] = (dq[:, :width] * cosine + dq[:, 256 : 256 + width] * sine).astype(BF)
         if i == 0:
             dk_scr[...] = dk
             dv_scr[...] = dv
         else:
             dk_scr[...] += dk
             dv_scr[...] += dv
-    dp_scr[1] = (dk_scr[:, :width] * cos_ref[...] + dk_scr[:, 256 : 256 + width] * sin_ref[...]).astype(BF)
+    cosine, sine = spread(table_ref[...], width)
+    dp_scr[1] = (dk_scr[:, :width] * cosine + dk_scr[:, 256 : 256 + width] * sine).astype(BF)
     dp_scr[2] = dv_scr[...].astype(BF)
     ready(n1_ref)
     for s in range(3):
@@ -721,9 +698,9 @@
     length, depth = tokens.shape
     half = length // 2
     where = jnp.stack([lax.axis_index("dp"), lax.axis_index("tensor")]).astype(jnp.int32)
-    cosine_table, sine_values = rope_tables(length, heads)
+    table = rope_tables(length)
     pieces_a, masks_a, pieces_b, masks_b, early, later = gather_pieces(
-        [cosine_table, sine_values],
+        [table],
         lambda deps: pack(w_qkv, w_out, gains, 0, deps), lambda deps: pack(w_in, w_down, gains, 1, deps)
     )
     wide_a, wide_b = pieces_a[0].shape[-1], pieces_b[0].shape[-1]
@@ -744,13 +721,14 @@
             ((half, depth), BF),
             ((depth, wide_a), BF),
         ],
-        [where, tokens, segments.reshape(length, 1), segments, cosine_table, sine_values, *pieces_a],
+        [where, tokens, segments.reshape(length, 1), segments, table, *pieces_a],
         [pltpu.VMEM((6, depth, heads), BF), pltpu.VMEM((repeat, length, heads), BF)],
         near=(7, 8),
         far=(1,),
+        here=range(5, 5 + len(pieces_a)),
     )
     terms = reduce_finish(reduce_start(mine, gate(theirs, early) if early else theirs, later))
-    middle, n2, z, du, dv2, gain_two, mine, theirs, full_b = stream(
+    middle, n2, z, du, dv2, gain_two, mine, theirs, wd = stream(
         lambda *refs: feed_kernel(masks_b, len(pieces_b), hidden, *refs),
         [
             ((length, depth), F32),
@@ -761,30 +739,28 @@
             ((8, depth), F32),
             ((half, depth), BF),
             ((half, depth), BF),
-            ((depth, wide_b), BF),
+            ((depth, hidden), BF),
         ],
         [where, tokens, cotangent, *terms, *pieces_b],
-        [pltpu.VMEM((3, depth, hidden), BF)],
+        [pltpu.VMEM((depth, wide_b), BF), pltpu.VMEM((2, depth, hidden), BF)],
         near=(6, 7),
         far=(1, 2),
+        here=range(3, 7 + len(pieces_b)),
     )
     chip = reduce_start(mine, theirs)
-    in_outs, down_outs = grad_outs(depth, 2 * hidden), far_outs(depth, hidden)
-    split = len(in_outs)
-    out_mine, out_theirs, *grads = stream(
-        lambda *refs: feed_grad_kernel(hidden, split, *refs),
-        [((half, depth), BF), ((half, depth), BF)] + in_outs + down_outs,
-        [where, n2, du, dv2, cotangent, z, full_b],
-        [pltpu.VMEM((depth, 2 * hidden), BF), pltpu.VMEM((depth, hidden), BF), pltpu.VMEM((depth, hidden), BF)],
+    feed_outs = grad_outs(depth, 3 * hidden)
+    out_mine, out_theirs, *grad_feed = stream(
+        lambda *refs: feed_grad_kernel(hidden, *refs),
+        [((half, depth), BF), ((half, depth), BF)] + feed_outs,
+        [where, n2, du, dv2, cotangent, z, wd],
+        [pltpu.VMEM((depth, 3 * hidden), BF)],
         deps=[chip],
-        near=range(2 + split + len(down_outs)),
+        near=range(2 + len(feed_outs)),
         far=range(1, 7),
     )
-    out_chip = reduce_start(out_mine, out_theirs)
     terms = reduce_finish(chip, [out_mine])
-    in_pieces, in_got, _unused = scatter_start(where, grads[:split])
-    down_finish, down_got = scatter_far_first(where, grads[split:])
-    out_chip = gate(out_chip, terms[1:2])
+    feed_pieces, feed_got, _unused = scatter_start(where, grad_feed)
+    out_chip = reduce_start(out_mine, out_theirs, terms[1:2])
     out_got = swap(out_chip, "tensor", 2)
     small = ((8, 128), F32)
     whole = ((length, depth), F32)
@@ -793,7 +769,7 @@
     dh, mine, theirs, *grad_attn = stream(
         lambda *refs: back_kernel(heads, *refs),
         [((length, depth), F32), ((half, depth), BF), ((half, depth), BF)] + attn_outs,
-        [where, *terms, middle, cotangent, gain_two, full_a, q, k, v, o, ab, n1, cosine_table, sine_values],
+        [where, *terms, middle, cotangent, gain_two, full_a, q, k, v, o, ab, n1, table],
         [
             pltpu.VMEM((depth, width), BF),
             pltpu.VMEM((length, depth), BF),
@@ -806,27 +782,28 @@
             pltpu.VMEM((3, length, heads), BF),
         ],
         near=range(1, 3 + len(attn_outs)),
-        far=range(5, 17),
-        vmem=44,
-    )
-    theirs = gate(theirs, [out_got] + in_got + down_got)
+        here=range(1, 16),
+        vmem=28,
+        cost=1,
+    )
+    chip = reduce_start(mine, gate(theirs, feed_got), [out_got])
+    attn_pieces, _unused, attn_pair = scatter_start(where, grad_attn, feed_pieces[1:])
+    out_chip, out_got = gate(out_chip, attn_pair), gate(out_got, attn_pair)
     out_terms = [out_chip, out_got, swap(out_chip, "tensor", 1), swap(out_got, "tensor", 1)]
-    attn_pieces, _unused, attn_pair = scatter_start(where, grad_attn, in_pieces[1:])
-    down_pieces = down_finish(attn_pair)
     output, sign = stream(
-        output_kernel, [whole, small], [where, middle, *out_terms], near=(1,), far=(1,), vmem=10, deps=attn_pair
+        output_kernel, [whole, small], [where, middle, *out_terms], near=(1,), far=(1,), here=range(2, 6), vmem=10, deps=attn_pair
     )
     signs = [sign]
-    terms = reduce_finish(reduce_start(mine, theirs, out_terms[2:]), in_pieces[1:])
+    terms = reduce_finish(chip, feed_pieces[1:])
     grad_tokens, sign = stream(
-        input_grad_kernel, [whole, small], [where, tokens, dh, gain_one, *terms], near=(1,), far=(1, 2), vmem=10
+        input_grad_kernel, [whole, small], [where, tokens, dh, gain_one, *terms], near=(1,), far=(1, 2), here=range(4, 8), vmem=10
     )
     signs.append(sign)
 
-    gain_sum_two = gain_call([0, hidden], 1, w_in, gains, in_pieces)
+    gain_sum_two = gain_call([0, hidden], 1, w_in, gains, feed_pieces)
     (leaf_in, leaf_down), sign = step_call(
-        [in_pieces, down_pieces],
-        [(False, [(0, 0, hidden), (0, hidden, hidden)]), (True, [(1, 0, hidden)])],
+        [feed_pieces],
+        [(False, [(0, 0, hidden), (0, hidden, hidden)]), (True, [(0, 2 * hidden, hidden)])],
         [(w_in, first_in, second_in), (w_down, first_down, second_down)],
     )
     gain_sum_one = gain_call([0, heads, 2 * heads], 0, w_qkv, gains, attn_pieces, signs + [sign])

time: 140 us -> 133 us (0.950)
  waiting for transfers between devices: 40.2 us -> 51.3 us
  Pallas kernels: 52.5 us -> 41.9 us
  starting transfers between devices: 42.6 us -> 36.1 us
    ppermute x43 -> x39, waiting for transfers between devices: 40.2 us -> 51.3 us  [swap(): return lax.ppermute(values, axis, [(i, i ^ mask) for i in range(count)])]
    pallas_call x8, Pallas kernels: 45.9 us -> 35.6 us  [stream(): pl.pallas_call(body, out_shape=[jax.ShapeDtypeStruct(*out) if i in near e...]
    ppermute x43 -> x39, starting transfers between devices: 42.6 us -> 36.1 us  [swap(): return lax.ppermute(values, axis, [(i, i ^ mask) for i in range(count)])]
    sin x1 -> x0, other arithmetic: 1.89 us -> none  [rope_tables(): return (jnp.cos(angles), jnp.sin(angles))]
    pallas_call x11 -> x10, Pallas kernels: 5.95 us -> 5.44 us  [call(): pl.pallas_call(body, out_shape=[jax.ShapeDtypeStruct(s, d) for s, d in ou...]
  transfers between devices with their start and end apart: 43 -> 39, of which waited for: 16 -> 15; matrix products, arithmetic and copies ran while one was open for 2% -> 1% of each run, Pallas kernels for 31% -> 26%
where the time goes in v4:
time: 133 us
  waiting for transfers between devices  51.3 us (39%)
  Pallas kernels  41.9 us (32%)
  starting transfers between devices  36.1 us (27%)
  other arithmetic  1.69 us (1%)
    ppermute x39, waiting for transfers between devices, swap(): return lax.ppermute(values, axis, [(i, i ^ mask) for i in range(count)])  51.3 us
    ppermute x39, starting transfers between devices, swap(): return lax.ppermute(values, axis, [(i, i ^ mask) for i in range(count)])  36.1 us
    pallas_call x8, Pallas kernels, stream(): pl.pallas_call(body, out_shape=[jax.ShapeDtypeStruct(*out) if i in near e...  35.6 us
    pallas_call x10, Pallas kernels, call(): pl.pallas_call(body, out_shape=[jax.ShapeDtypeStruct(s, d) for s, d in ou...  5.44 us
  transfers between devices with their start and end apart: 39, of which 15 were waited for; matrix products, arithmetic and copies ran while one was open for 1% of the time, Pallas kernels for 26%

profile of v4, /device:TPU:0, one launch (start us, length us, event | category | flops | bytes accessed | tf_op | source)
XLA Modules:
  0.0 132.5 jit_solution(12360996167048398922)
XLA Ops:
  1.9 3.0 %collective-permute-start.3 = (bf16[96,896]{1,0:T(8,128)(2,1)S(1)}, bf16[96,896]{1,0:T(8,128)(2,1)S(1)}, u32[]{:S(2)}, u32[]{:S(2)}) collective-permute-start(bf16[96,896]{1,0:T(8,128)(2,1)S(1)} %shard_map.345.refs_5_), channel_id=1, source_target_pairs={{0,4},{4,0},{8,12},{12,8},{16,20},{20,16},{24,28},{28,24},{1,5},{5... | collective-permute-start | bytes 516104 | tf_op jit(solution)/shard_map/ppermute | solution.py:52
  4.9 3.6 %collective-permute-start.2 = (bf16[96,896]{1,0:T(8,128)(2,1)S(1)}, bf16[96,896]{1,0:T(8,128)(2,1)S(1)}, u32[]{:S(2)}, u32[]{:S(2)}) collective-permute-start(bf16[96,896]{1,0:T(8,128)(2,1)S(1)} %shard_map.345.refs_5_), channel_id=1, source_target_pairs={{0,24},{4,28},{8,16},{12,20},{16,8},{20,12},{24,0},{28,4},{1,25},{... | collective-permute-start | bytes 516104 | tf_op jit(solution)/shard_map/ppermute | solution.py:52
  11.7 2.4 %collective-permute-done.2.refs_8_.refs_2_ = bf16[96,896]{1,0:T(8,128)(2,1)S(1)} collective-permute-done((bf16[96,896]{1,0:T(8,128)(2,1)S(1)}, bf16[96,896]{1,0:T(8,128)(2,1)S(1)}, u32[]{:S(2)}, u32[]{:S(2)}) %collective-permute-start.2) | collective-permute-done | bytes 172064 | tf_op jit(solution)/shard_map/ppermute | solution.py:52
  15.6 7.3 %collective-permute-done.1.refs_7_.refs_1_ = bf16[96,896]{1,0:T(8,128)(2,1)S(1)} collective-permute-done((bf16[96,896]{1,0:T(8,128)(2,1)S(1)}, bf16[96,896]{1,0:T(8,128)(2,1)S(1)}, u32[]{:S(2)}, u32[]{:S(2)}) %collective-permute-start.1) | collective-permute-done | bytes 172064 | tf_op jit(solution)/shard_map/ppermute | solution.py:52
  25.0 2.6 %collective-permute-start.8 = (bf16[96,896]{1,0:T(8,128)(2,1)S(1)}, bf16[96,896]{1,0:T(8,128)(2,1)S(1)}, u32[]{:S(2)}, u32[]{:S(2)}) collective-permute-start(bf16[96,896]{1,0:T(8,128)(2,1)S(1)} %shard_map.349.refs_7_), channel_id=1, source_target_pairs={{0,24},{4,28},{8,16},{12,20},{16,8},{20,12},{24,0},{28,4},{1,25},{... | collective-permute-start | bytes 516104 | tf_op jit(solution)/shard_map/ppermute | solution.py:52
  27.5 1.9 %collective-permute-start.7 = (bf16[96,896]{1,0:T(8,128)(2,1)S(1)}, bf16[96,896]{1,0:T(8,128)(2,1)S(1)}, u32[]{:S(2)}, u32[]{:S(2)}) collective-permute-start(bf16[96,896]{1,0:T(8,128)(2,1)S(1)} %shard_map.349.refs_7_), channel_id=1, source_target_pairs={{0,16},{4,20},{8,24},{12,28},{16,0},{20,4},{24,8},{28,12},{1,17},{... | collective-permute-start | bytes 516104 | tf_op jit(solution)/shard_map/ppermute | solution.py:52
  30.1 6.9 %shard_map.347 = (bf16[512,768]{1,0:T(8,128)(2,1)}, bf16[512,192]{1,0:T(8,128)(2,1)}, bf16[512,192]{1,0:T(8,128)(2,1)}, bf16[512,192]{1,0:T(8,128)(2,1)}, bf16[5...) custom-call(s32[2]{0:T(128)S(1)} %pad_add_fusion.refs_0_, ...), custom_call_target="tpu_custom_call" | custom-call | tf_op jit(solution)/shard_map/pallas_call | solution.py:285
  37.1 4.9 %collective-permute-done.7.refs_1_.refs_0_ = bf16[96,896]{1,0:T(8,128)(2,1)S(1)} collective-permute-done((bf16[96,896]{1,0:T(8,128)(2,1)S(1)}, bf16[96,896]{1,0:T(8,128)(2,1)S(1)}, u32[]{:S(2)}, u32[]{:S(2)}) %collective-permute-start.7) | collective-permute-done | bytes 172064 | tf_op jit(solution)/shard_map/ppermute | solution.py:52
  45.9 9.1 %collective-permute-done.12.refs_4_ = bf16[256,768]{1,0:T(8,128)(2,1)S(1)} collective-permute-done((bf16[256,768]{1,0:T(8,128)(2,1)S(1)}, bf16[256,768]{1,0:T(8,128)(2,1)S(1)}, u32[]{:S(2)}, u32[]{:S(2)}) %collective-permute-start.12) | collective-permute-done | bytes 393248 | tf_op jit(solution)/shard_map/ppermute | solution.py:52
  55.0 3.9 %collective-permute-done.15.refs_10_ = bf16[3,96,896]{2,1,0:T(8,128)(2,1)S(1)} collective-permute-done((bf16[3,96,896]{2,1,0:T(8,128)(2,1)S(1)}, bf16[3,96,896]{2,1,0:T(8,128)(2,1)S(1)}, u32[]{:S(2)}, u32[]{:S(2)}) %collective-permute-start.15) | collective-permute-done | bytes 516128 | tf_op jit(solution)/shard_map/ppermute | solution.py:52
  58.9 5.4 %shard_map.353 = (f32[512,768]{1,0:T(8,128)}, bf16[512,768]{1,0:T(8,128)(2,1)}, bf16[512,288]{1,0:T(8,128)(2,1)}, bf16[512,288]{1,0:T(8,128)(2,1)}, bf16[512,288...) custom-call(s32[2]{0:T(128)S(1)} %pad_add_fusion.refs_0_, ...), custom_call_target="tpu_custom_call" | custom-call | tf_op jit(solution)/shard_map/pallas_call | solution.py:285
  64.4 1.7 %collective-permute-done.16.refs_1_ = bf16[256,768]{1,0:T(8,128)(2,1)S(1)} collective-permute-done((bf16[256,768]{1,0:T(8,128)(2,1)S(1)}, bf16[256,768]{1,0:T(8,128)(2,1)S(1)}, u32[]{:S(2)}, u32[]{:S(2)}) %collective-permute-start.16) | collective-permute-done | bytes 393248 | tf_op jit(solution)/shard_map/ppermute | solution.py:52
  66.7 4.9 %shard_map.355 = (bf16[256,768]{1,0:T(8,128)(2,1)S(1)}, bf16[256,768]{1,0:T(8,128)(2,1)S(1)}, bf16[4,96,864]{2,1,0:T(8,128)(2,1)S(1)}, bf16[4,96,864]{2,1,0:T(8,128)(2,1)S(1)}) custom-call(s32[2]{0:T(128)S(1)} %pad_add_fusion.refs_0_, bf16[512,768]{1,0:T(8,128)(2,1)} %get-tuple-element.82.refs_1_, bf16[512,288]{1,0:T(8,128)(2,1)} %get-tuple-element.83.refs_2_, ...), custom_call_target="tpu_custom_call" | custom-call | tf_op jit(solution)/shard_map/pallas_call | solution.py:285
  72.9 4.5 %collective-permute-done.18.refs_0_ = bf16[256,768]{1,0:T(8,128)(2,1)S(1)} collective-permute-done((bf16[256,768]{1,0:T(8,128)(2,1)S(1)}, bf16[256,768]{1,0:T(8,128)(2,1)S(1)}, u32[]{:S(2)}, u32[]{:S(2)}) %collective-permute-start.18) | collective-permute-done | bytes 393248 | tf_op jit(solution)/shard_map/ppermute | solution.py:52
  79.2 8.3 %shard_map.358 = (f32[512,768]{1,0:T(8,128)}, bf16[256,768]{1,0:T(8,128)(2,1)S(1)}, bf16[256,768]{1,0:T(8,128)(2,1)S(1)}, bf16[4,96,768]{2,1,0:T(8,128)(2,1)S(1)}, bf16[4,96,768]{2,1,0:T(8,128)(2,1)S(1)}) custom-call(s32[2]{0:T(128)S(1)} %pad_add_fusion.refs_0_, bf16[256,768]{1,0:T(8,128)(2,1)S(1)} %shard_map.354.refs_7_.refs_1_, ...), custom_call_target="tpu_custom_call" | custom-call | flops 1 | bytes 1 | tf_op jit(solution)/shard_map/pallas_call | solution.py:285
  93.2 2.5 %collective-permute-start.24 = (bf16[96,864]{1,0:T(8,128)(2,1)S(1)}, bf16[96,864]{1,0:T(8,128)(2,1)S(1)}, u32[]{:S(2)}, u32[]{:S(2)}) collective-permute-start(bf16[96,864]{1,0:T(8,128)(2,1)S(1)} %get-tuple-element.104), channel_id=1, source_target_pairs={{0,16},{4,20},{8,24},{12,28},{16,0},{20,4},{24,8},{28,12},{1,17},{... | collective-permute-start | bytes 497672 | tf_op jit(solution)/shard_map/ppermute | solution.py:52
  95.7 1.9 %collective-permute-start.25 = (bf16[96,864]{1,0:T(8,128)(2,1)S(1)}, bf16[96,864]{1,0:T(8,128)(2,1)S(1)}, u32[]{:S(2)}, u32[]{:S(2)}) collective-permute-start(bf16[96,864]{1,0:T(8,128)(2,1)S(1)} %get-tuple-element.105), channel_id=1, source_target_pairs={{0,24},{4,28},{8,16},{12,20},{16,8},{20,12},{24,0},{28,4},{1,25},{... | collective-permute-start | bytes 497672 | tf_op jit(solution)/shard_map/ppermute | solution.py:52
  97.6 4.5 %collective-permute-done.23.refs_3_.refs_1_ = bf16[96,864]{1,0:T(8,128)(2,1)S(1)} collective-permute-done((bf16[96,864]{1,0:T(8,128)(2,1)S(1)}, bf16[96,864]{1,0:T(8,128)(2,1)S(1)}, u32[]{:S(2)}, u32[]{:S(2)}) %collective-permute-start.23) | collective-permute-done | bytes 165920 | tf_op jit(solution)/shard_map/ppermute | solution.py:52
  102.1 6.7 %collective-permute-done.24.refs_4_.refs_2_ = bf16[96,864]{1,0:T(8,128)(2,1)S(1)} collective-permute-done((bf16[96,864]{1,0:T(8,128)(2,1)S(1)}, bf16[96,864]{1,0:T(8,128)(2,1)S(1)}, u32[]{:S(2)}, u32[]{:S(2)}) %collective-permute-start.24) | collective-permute-done | bytes 165920 | tf_op jit(solution)/shard_map/ppermute | solution.py:52
  110.7 3.2 %collective-permute-start.33 = (bf16[96,768]{1,0:T(8,128)(2,1)S(1)}, bf16[96,768]{1,0:T(8,128)(2,1)S(1)}, u32[]{:S(2)}, u32[]{:S(2)}) collective-permute-start(bf16[96,768]{1,0:T(8,128)(2,1)S(1)} %get-tuple-element.113), channel_id=1, source_target_pairs={{0,8},{4,12},{8,0},{12,4},{16,24},{20,28},{24,16},{28,20},{1,9},{5... | collective-permute-start | bytes 442376 | tf_op jit(solution)/shard_map/ppermute | solution.py:52
  115.1 1.9 %collective-permute-start.35 = (bf16[96,768]{1,0:T(8,128)(2,1)S(1)}, bf16[96,768]{1,0:T(8,128)(2,1)S(1)}, u32[]{:S(2)}, u32[]{:S(2)}) collective-permute-start(bf16[96,768]{1,0:T(8,128)(2,1)S(1)} %get-tuple-element.115), channel_id=1, source_target_pairs={{0,24},{4,28},{8,16},{12,20},{16,8},{20,12},{24,0},{28,4},{1,25},{... | collective-permute-start | bytes 442376 | tf_op jit(solution)/shard_map/ppermute | solution.py:52
  117.2 1.7 %shard_map.369 = (f32[2,96,288]{2,1,0:T(8,128)}, f32[2,96,288]{2,1,0:T(8,128)}, f32[2,96,288]{2,1,0:T(8,128)}, f32[2,96,288]{2,1,0:T(8,128)}, f32[288,96]{1,0:T(...) custom-call(bf16[96,864]{1,0:T(8,128)(2,1)S(1)} %get-tuple-element.118.refs_0_.refs_2_, ...), custom_call_target="tpu_custom_call" | custom-call | tf_op jit(solution)/shard_map/pallas_call | solution.py:210
  118.9 3.3 %shard_map.363 = (f32[512,768]{1,0:T(8,128)}, f32[8,128]{1,0:T(8,128)S(1)}) custom-call(s32[2]{0:T(128)S(1)} %pad_add_fusion.refs_0_, f32[512,768]{1,0:T(8,128)} %get-tuple-element.81.refs_5_.refs_1_, bf16[256,768]{1,0:T(8,128)(2,1)S(1)} %shard_map.361.refs_2_, bf16[256,768]{1,0:T(8,128)(2,1)S(1)} %shard_map.362.refs_3_, ...), custom_call_target="tpu_custom_call" | custom-call | tf_op jit(solution)/shard_map/pallas_call | solution.py:285
  122.3 4.3 %shard_map.367 = (f32[512,768]{1,0:T(8,128)}, f32[8,128]{1,0:T(8,128)S(1)}) custom-call(s32[2]{0:T(128)S(1)} %pad_add_fusion.refs_0_, bf16[512,768]{1,0:T(8,128)(2,1)} %refs_1_.11, f32[512,768]{1,0:T(8,128)} %get-tuple-element.108.refs_2_, f32[8,768]{1,0:T(8,128)S(1)} %copy-done.22, bf16[256,768]{1,0:T(8,128)(2,1)S(1)} %shard_map.365.refs_4_, ...), custom_call_target="tpu_custom_call" | custom-call | tf_op jit(solution)/shard_map/pallas_call | solution.py:285
  (145 shorter events, 30.9 us)
Async XLA Ops:
  4.9 9.2 %collective-permute-start.2 = (bf16[96,896]{1,0:T(8,128)(2,1)S(1)}, bf16[96,896]{1,0:T(8,128)(2,1)S(1)}, u32[]{:S(2)}, u32[]{:S(2)}) collective-permute-start(bf16[96,896]{1,0:T(8,128)(2,1)S(1)} %shard_map.345.refs_5_), channel_id=1, source_target_pairs={{0,24},{4,28},{8,16},{12,20},{16,8},{20,12},{24,0},{28,4},{1,25},{... | collective-permute-start | bytes 516104 | tf_op jit(solution)/shard_map/ppermute | solution.py:52
  8.5 14.4 %collective-permute-start.1 = (bf16[96,896]{1,0:T(8,128)(2,1)S(1)}, bf16[96,896]{1,0:T(8,128)(2,1)S(1)}, u32[]{:S(2)}, u32[]{:S(2)}) collective-permute-start(bf16[96,896]{1,0:T(8,128)(2,1)S(1)} %shard_map.345.refs_5_), channel_id=1, source_target_pairs={{0,16},{4,20},{8,24},{12,28},{16,0},{20,4},{24,8},{28,12},{1,17},{... | collective-permute-start | bytes 516104 | tf_op jit(solution)/shard_map/ppermute | solution.py:52
  9.6 13.9 %collective-permute-start.4 = (bf16[96,896]{1,0:T(8,128)(2,1)S(1)}, bf16[96,896]{1,0:T(8,128)(2,1)S(1)}, u32[]{:S(2)}, u32[]{:S(2)}) collective-permute-start(bf16[96,896]{1,0:T(8,128)(2,1)S(1)} %shard_map.346), channel_id=1, source_target_pairs={{0,8},{4,12},{8,0},{12,4},{16,24},{20,28},{24,16},{28,20},{1,9},{5... | collective-permute-start | bytes 516104 | tf_op jit(solution)/shard_map/ppermute | solution.py:52
  11.2 13.8 %collective-permute-start = (bf16[96,896]{1,0:T(8,128)(2,1)S(1)}, bf16[96,896]{1,0:T(8,128)(2,1)S(1)}, u32[]{:S(2)}, u32[]{:S(2)}) collective-permute-start(bf16[96,896]{1,0:T(8,128)(2,1)S(1)} %shard_map.345.refs_5_), channel_id=1, source_target_pairs={{0,8},{4,12},{8,0},{12,4},{16,24},{20,28},{24,16},{28,20},{1,9},{5... | collective-permute-start | bytes 516104 | tf_op jit(solution)/shard_map/ppermute | solution.py:52
  14.1 13.5 %collective-permute-start.6 = (bf16[96,896]{1,0:T(8,128)(2,1)S(1)}, bf16[96,896]{1,0:T(8,128)(2,1)S(1)}, u32[]{:S(2)}, u32[]{:S(2)}) collective-permute-start(bf16[96,896]{1,0:T(8,128)(2,1)S(1)} %collective-permute-done.2.refs_8_.refs_2_), channel_id=1, source_target_pairs={{0,4},{4,0},{8,12},{12,8},{16,20},{20,16},{24,28},{28,24},{1,5},{5... | collective-permute-start | bytes 516104 | tf_op jit(solution)/shard_map/ppermute | solution.py:52
  23.5 13.6 %collective-permute-start.10 = (bf16[96,896]{1,0:T(8,128)(2,1)S(1)}, bf16[96,896]{1,0:T(8,128)(2,1)S(1)}, u32[]{:S(2)}, u32[]{:S(2)}) collective-permute-start(bf16[96,896]{1,0:T(8,128)(2,1)S(1)} %shard_map.349.refs_7_), channel_id=1, source_target_pairs={{0,4},{4,0},{8,12},{12,8},{16,20},{20,16},{24,28},{28,24},{1,5},{5... | collective-permute-start | bytes 516104 | tf_op jit(solution)/shard_map/ppermute | solution.py:52
  24.9 12.1 %collective-permute-start.9 = (bf16[96,896]{1,0:T(8,128)(2,1)S(1)}, bf16[96,896]{1,0:T(8,128)(2,1)S(1)}, u32[]{:S(2)}, u32[]{:S(2)}) collective-permute-start(bf16[96,896]{1,0:T(8,128)(2,1)S(1)} %shard_map.349.refs_7_), channel_id=1, source_target_pairs={{0,8},{4,12},{8,0},{12,4},{16,24},{20,28},{24,16},{28,20},{1,9},{5... | collective-permute-start | bytes 516104 | tf_op jit(solution)/shard_map/ppermute | solution.py:52
  25.0 12.1 %collective-permute-start.8 = (bf16[96,896]{1,0:T(8,128)(2,1)S(1)}, bf16[96,896]{1,0:T(8,128)(2,1)S(1)}, u32[]{:S(2)}, u32[]{:S(2)}) collective-permute-start(bf16[96,896]{1,0:T(8,128)(2,1)S(1)} %shard_map.349.refs_7_), channel_id=1, source_target_pairs={{0,24},{4,28},{8,16},{12,20},{16,8},{20,12},{24,0},{28,4},{1,25},{... | collective-permute-start | bytes 516104 | tf_op jit(solution)/shard_map/ppermute | solution.py:52
  27.5 14.4 %collective-permute-start.7 = (bf16[96,896]{1,0:T(8,128)(2,1)S(1)}, bf16[96,896]{1,0:T(8,128)(2,1)S(1)}, u32[]{:S(2)}, u32[]{:S(2)}) collective-permute-start(bf16[96,896]{1,0:T(8,128)(2,1)S(1)} %shard_map.349.refs_7_), channel_id=1, source_target_pairs={{0,16},{4,20},{8,24},{12,28},{16,0},{20,4},{24,8},{28,12},{1,17},{... | collective-permute-start | bytes 516104 | tf_op jit(solution)/shard_map/ppermute | solution.py:52
  43.8 11.2 %collective-permute-start.12 = (bf16[256,768]{1,0:T(8,128)(2,1)S(1)}, bf16[256,768]{1,0:T(8,128)(2,1)S(1)}, u32[]{:S(2)}, u32[]{:S(2)}) collective-permute-start(bf16[256,768]{1,0:T(8,128)(2,1)S(1)} %shard_map.352.refs_3_), channel_id=1, source_target_pairs={{0,2},{1,3},{2,0},{3,1},{4,6},{5,7},{6,4},{7,5},{8,10},{9,11},{10,... | collective-permute-start | bytes 1179656 | tf_op jit(solution)/shard_map/ppermute | solution.py:52
  45.4 13.5 %collective-permute-start.15 = (bf16[3,96,896]{2,1,0:T(8,128)(2,1)S(1)}, bf16[3,96,896]{2,1,0:T(8,128)(2,1)S(1)}, u32[]{:S(2)}, u32[]{:S(2)}) collective-permute-start(bf16[3,96,896]{2,1,0:T(8,128)(2,1)S(1)} %shard_map.351.refs_2_.refs_8_), channel_id=1, source_target_pairs={{0,4},{4,0},{8,12},{12,8},{16,20},{20,16},{24,28},{28,24},{1,5},{5... | collective-permute-start | bytes 1548296 | tf_op jit(solution)/shard_map/ppermute | solution.py:52
  45.9 13.0 %collective-permute-start.13 = (bf16[256,768]{1,0:T(8,128)(2,1)S(1)}, bf16[256,768]{1,0:T(8,128)(2,1)S(1)}, u32[]{:S(2)}, u32[]{:S(2)}) collective-permute-start(bf16[256,768]{1,0:T(8,128)(2,1)S(1)} %shard_map.352.refs_3_), channel_id=1, source_target_pairs={{0,1},{1,0},{2,3},{3,2},{4,5},{5,4},{6,7},{7,6},{8,9},{9,8},{10,11... | collective-permute-start | bytes 1179656 | tf_op jit(solution)/shard_map/ppermute | solution.py:52
  66.2 11.2 %collective-permute-start.18 = (bf16[256,768]{1,0:T(8,128)(2,1)S(1)}, bf16[256,768]{1,0:T(8,128)(2,1)S(1)}, u32[]{:S(2)}, u32[]{:S(2)}) collective-permute-start(bf16[256,768]{1,0:T(8,128)(2,1)S(1)} %shard_map.354.refs_7_.refs_1_), channel_id=1, source_target_pairs={{0,2},{1,3},{2,0},{3,1},{4,6},{5,7},{6,4},{7,5},{8,10},{9,11},{10,... | collective-permute-start | bytes 1179656 | tf_op jit(solution)/shard_map/ppermute | solution.py:52
  71.7 17.3 %collective-permute-start.22 = (bf16[4,96,864]{2,1,0:T(8,128)(2,1)S(1)}, bf16[4,96,864]{2,1,0:T(8,128)(2,1)S(1)}, u32[]{:S(2)}, u32[]{:S(2)}) collective-permute-start(bf16[4,96,864]{2,1,0:T(8,128)(2,1)S(1)} %get-tuple-element.102), channel_id=1, source_target_pairs={{0,4},{4,0},{8,12},{12,8},{16,20},{20,16},{24,28},{28,24},{1,5},{5... | collective-permute-start | bytes 1990664 | tf_op jit(solution)/shard_map/ppermute | solution.py:52
  77.5 12.1 %collective-permute-start.26 = (bf16[256,768]{1,0:T(8,128)(2,1)S(1)}, bf16[256,768]{1,0:T(8,128)(2,1)S(1)}, u32[]{:S(2)}, u32[]{:S(2)}) collective-permute-start(bf16[256,768]{1,0:T(8,128)(2,1)S(1)} %shard_map.357.refs_0_), channel_id=1, source_target_pairs={{0,2},{1,3},{2,0},{3,1},{4,6},{5,7},{6,4},{7,5},{8,10},{9,11},{10,... | collective-permute-start | bytes 1179656 | tf_op jit(solution)/shard_map/ppermute | solution.py:52
  89.0 19.8 %collective-permute-start.21 = (bf16[4,96,768]{2,1,0:T(8,128)(2,1)S(1)}, bf16[4,96,768]{2,1,0:T(8,128)(2,1)S(1)}, u32[]{:S(2)}, u32[]{:S(2)}) collective-permute-start(bf16[4,96,768]{2,1,0:T(8,128)(2,1)S(1)} %get-tuple-element.100), channel_id=1, source_target_pairs={{0,4},{4,0},{8,12},{12,8},{16,20},{20,16},{24,28},{28,24},{1,5},{5... | collective-permute-start | bytes 1769480 | tf_op jit(solution)/shard_map/ppermute | solution.py:52
  90.8 19.4 %collective-permute-start.30 = (bf16[256,768]{1,0:T(8,128)(2,1)S(1)}, bf16[256,768]{1,0:T(8,128)(2,1)S(1)}, u32[]{:S(2)}, u32[]{:S(2)}) collective-permute-start(bf16[256,768]{1,0:T(8,128)(2,1)S(1)} %shard_map.365.refs_4_), channel_id=1, source_target_pairs={{0,2},{1,3},{2,0},{3,1},{4,6},{5,7},{6,4},{7,5},{8,10},{9,11},{10,... | collective-permute-start | bytes 1179656 | tf_op jit(solution)/shard_map/ppermute | solution.py:52
  93.2 15.6 %collective-permute-start.24 = (bf16[96,864]{1,0:T(8,128)(2,1)S(1)}, bf16[96,864]{1,0:T(8,128)(2,1)S(1)}, u32[]{:S(2)}, u32[]{:S(2)}) collective-permute-start(bf16[96,864]{1,0:T(8,128)(2,1)S(1)} %get-tuple-element.104), channel_id=1, source_target_pairs={{0,16},{4,20},{8,24},{12,28},{16,0},{20,4},{24,8},{28,12},{1,17},{... | collective-permute-start | bytes 497672 | tf_op jit(solution)/shard_map/ppermute | solution.py:52
  95.7 13.1 %collective-permute-start.25 = (bf16[96,864]{1,0:T(8,128)(2,1)S(1)}, bf16[96,864]{1,0:T(8,128)(2,1)S(1)}, u32[]{:S(2)}, u32[]{:S(2)}) collective-permute-start(bf16[96,864]{1,0:T(8,128)(2,1)S(1)} %get-tuple-element.105), channel_id=1, source_target_pairs={{0,24},{4,28},{8,16},{12,20},{16,8},{20,12},{24,0},{28,4},{1,25},{... | collective-permute-start | bytes 497672 | tf_op jit(solution)/shard_map/ppermute | solution.py:52
  110.2 12.0 %collective-permute-start.31 = (bf16[256,768]{1,0:T(8,128)(2,1)S(1)}, bf16[256,768]{1,0:T(8,128)(2,1)S(1)}, u32[]{:S(2)}, u32[]{:S(2)}) collective-permute-start(bf16[256,768]{1,0:T(8,128)(2,1)S(1)} %shard_map.365.refs_4_), channel_id=1, source_target_pairs={{0,1},{1,0},{2,3},{3,2},{4,5},{5,4},{6,7},{7,6},{8,9},{9,8},{10,11... | collective-permute-start | bytes 1179656 | tf_op jit(solution)/shard_map/ppermute | solution.py:52
  110.3 11.9 %collective-permute-start.32 = (bf16[256,768]{1,0:T(8,128)(2,1)S(1)}, bf16[256,768]{1,0:T(8,128)(2,1)S(1)}, u32[]{:S(2)}, u32[]{:S(2)}) collective-permute-start(bf16[256,768]{1,0:T(8,128)(2,1)S(1)} %shard_map.366.refs_5_), channel_id=1, source_target_pairs={{0,1},{1,0},{2,3},{3,2},{4,5},{5,4},{6,7},{7,6},{8,9},{9,8},{10,11... | collective-permute-start | bytes 1179656 | tf_op jit(solution)/shard_map/ppermute | solution.py:52
  110.7 15.9 %collective-permute-start.33 = (bf16[96,768]{1,0:T(8,128)(2,1)S(1)}, bf16[96,768]{1,0:T(8,128)(2,1)S(1)}, u32[]{:S(2)}, u32[]{:S(2)}) collective-permute-start(bf16[96,768]{1,0:T(8,128)(2,1)S(1)} %get-tuple-element.113), channel_id=1, source_target_pairs={{0,8},{4,12},{8,0},{12,4},{16,24},{20,28},{24,16},{28,20},{1,9},{5... | collective-permute-start | bytes 442376 | tf_op jit(solution)/shard_map/ppermute | solution.py:52
  113.9 14.0 %collective-permute-start.34 = (bf16[96,768]{1,0:T(8,128)(2,1)S(1)}, bf16[96,768]{1,0:T(8,128)(2,1)S(1)}, u32[]{:S(2)}, u32[]{:S(2)}) collective-permute-start(bf16[96,768]{1,0:T(8,128)(2,1)S(1)} %get-tuple-element.114), channel_id=1, source_target_pairs={{0,16},{4,20},{8,24},{12,28},{16,0},{20,4},{24,8},{28,12},{1,17},{... | collective-permute-start | bytes 442376 | tf_op jit(solution)/shard_map/ppermute | solution.py:52
  115.1 12.8 %collective-permute-start.35 = (bf16[96,768]{1,0:T(8,128)(2,1)S(1)}, bf16[96,768]{1,0:T(8,128)(2,1)S(1)}, u32[]{:S(2)}, u32[]{:S(2)}) collective-permute-start(bf16[96,768]{1,0:T(8,128)(2,1)S(1)} %get-tuple-element.115), channel_id=1, source_target_pairs={{0,24},{4,28},{8,16},{12,20},{16,8},{20,12},{24,0},{28,4},{1,25},{... | collective-permute-start | bytes 442376 | tf_op jit(solution)/shard_map/ppermute | solution.py:52
  (42 other events, 313.2 us)

commit v5 on v4

--- a/solution.py
+++ b/solution.py
@@ -94,7 +94,8 @@
     keep, send = grads
     got = swap(send, "dp", 1)
     parts = call(pair_kernel, [(keep.shape[1:], BF)] * keep.shape[0], [where, keep, got], deps=deps)
-    return [parts[0]] + [swap(parts[m], "dp", 2 * m) for m in range(1, len(parts))], [got], [parts[0]]
+    came = [swap(parts[m], "dp", 2 * m) for m in reversed(range(1, len(parts)))]
+    return [parts[0]] + came, [got], [parts[0]]
 
 
 def grad_outs(depth, width):
@@ -482,17 +483,28 @@
 SPAN = 256
 
 
-def back_kernel(width, ready, ship, where_ref, a_ref, b_ref, c_ref, d_ref, h_ref, cot_ref, gain_ref, full_ref, q_ref, k_ref, v_ref, o_ref, ab_ref,
+def ahead_kernel(width, ready, ship, where_ref, full_ref, q_ref, k_ref, w_ref, km_ref, qm_ref):
+    ready(q_ref, k_ref)
+    turn = turn_matrix(width)
+    for given, out_ref in ((k_ref, km_ref), (q_ref, qm_ref)):
+        turned = (-dot(given[...], turn)).astype(BF)
+        for h in range(width // HEAD_DIM):
+            out_ref[h, :, 0:width] = only_head(given[...], h)
+            out_ref[h, :, 256 : 256 + width] = only_head(turned, h)
+    ready(full_ref)
+    for s in range(4):
+        w_ref[s] = full_ref[:, s * width : (s + 1) * width]
+
+
+def back_kernel(width, ready, ship, where_ref, a_ref, b_ref, c_ref, d_ref, h_ref, cot_ref, gain_ref, w_scr, km_scr, qm_scr, v_ref, o_ref, ab_ref,
                 n1_ref, table_ref, dh_ref, mine_ref, theirs_ref, *rest):
-    grad_ref, low_scr, do_scr, w_scr, km_scr, qm_scr, dk_scr, dv_scr, dp_scr = rest[-9:]
+    grad_ref, low_scr, do_scr, dk_scr, dv_scr, dp_scr = rest[-6:]
     length = h_ref.shape[0]
     half = length // 2
     heads = width // HEAD_DIM
     core = where_ref[1] & 1
-    ready(gain_ref, full_ref, a_ref, b_ref, c_ref, d_ref, h_ref, cot_ref)
+    ready(gain_ref, w_scr, a_ref, b_ref, c_ref, d_ref, h_ref, cot_ref)
     gain = gain_ref[0:1, :]
-    for s in range(4):
-        w_scr[s] = full_ref[:, s * width : (s + 1) * width]
     for is_mine, first in halves(core, length):
         low, high = (a_ref, b_ref) if is_mine else (c_ref, d_ref)
 
@@ -511,16 +523,7 @@
 
         lax.fori_loop(0, half // CHUNK, step, 0)
     ship(dh_ref)
-    turn = turn_matrix(width)
-    ready(q_ref, k_ref, v_ref, o_ref, ab_ref)
-    kt = (-dot(k_ref[...], turn)).astype(BF)
-    qt = (-dot(q_ref[...], turn)).astype(BF)
-    for h in range(heads):
-        km_scr[h, :, 0:width] = only_head(k_ref[...], h)
-        km_scr[h, :, 256 : 256 + width] = only_head(kt, h)
-        qm_scr[h, :, 0:width] = only_head(q_ref[...], h)
-        qm_scr[h, :, 256 : 256 + width] = only_head(qt, h)
-
+    ready(km_scr, qm_scr, v_ref, o_ref, ab_ref)
     ready(table_ref)
     for i in range(length // SPAN):
         rows = pl.ds(i * SPAN, SPAN)
@@ -556,8 +559,8 @@
     for s in range(3):
         grad_ref[:, s * width : (s + 1) * width] = dot_tn(n1_ref[...], dp_scr[s]).astype(BF)
     grad_ref[:, 3 * width :] = dot_tn(low_scr[...], o_ref[...]).astype(BF)
-    emit_grad(where_ref, grad_ref, rest[:-9])
-    for ref in rest[:-9]:
+    emit_grad(where_ref, grad_ref, rest[:-6])
+    for ref in rest[:-6]:
         ship(ref)
     for is_mine, first in halves(core, length):
         out = mine_ref if is_mine else theirs_ref
@@ -743,7 +746,7 @@
         ],
         [where, tokens, cotangent, *terms, *pieces_b],
         [pltpu.VMEM((depth, wide_b), BF), pltpu.VMEM((2, depth, hidden), BF)],
-        near=(6, 7),
+        near=(1, 2, 3, 4, 6, 7, 8),
         far=(1, 2),
         here=range(3, 7 + len(pieces_b)),
     )
@@ -756,9 +759,19 @@
         [pltpu.VMEM((depth, 3 * hidden), BF)],
         deps=[chip],
         near=range(2 + len(feed_outs)),
-        far=range(1, 7),
-    )
-    terms = reduce_finish(chip, [out_mine])
+        far=(4,),
+        here=(1, 2, 3, 5, 6),
+    )
+    weights, keys, queries = stream(
+        lambda *refs: ahead_kernel(heads, *refs),
+        [((4, depth, heads), BF), ((repeat, length, 512), BF), ((repeat, length, 512), BF)],
+        [where, full_a, q, k],
+        deps=[chip, out_mine],
+        near=(0, 1, 2),
+        far=(1, 2, 3),
+        vmem=16,
+    )
+    terms = reduce_finish(chip, [out_mine, keys])
     feed_pieces, feed_got, _unused = scatter_start(where, grad_feed)
     out_chip = reduce_start(out_mine, out_theirs, terms[1:2])
     out_got = swap(out_chip, "tensor", 2)
@@ -769,14 +782,11 @@
     dh, mine, theirs, *grad_attn = stream(
         lambda *refs: back_kernel(heads, *refs),
         [((length, depth), F32), ((half, depth), BF), ((half, depth), BF)] + attn_outs,
-        [where, *terms, middle, cotangent, gain_two, full_a, q, k, v, o, ab, n1, table],
+        [where, *terms, middle, cotangent, gain_two, weights, keys, queries, v, o, ab, n1, table],
         [
             pltpu.VMEM((depth, width), BF),
             pltpu.VMEM((length, depth), BF),
             pltpu.VMEM((length, heads), BF),
-            pltpu.VMEM((4, depth, heads), BF),
-            pltpu.VMEM((repeat, length, 512), BF),
-            pltpu.VMEM((repeat, length, 512), BF),
             pltpu.VMEM((length, 512), F32),
             pltpu.VMEM((length, heads), F32),
             pltpu.VMEM((3, length, heads), BF),
@@ -787,11 +797,11 @@
         cost=1,
     )
     chip = reduce_start(mine, gate(theirs, feed_got), [out_got])
-    attn_pieces, _unused, attn_pair = scatter_start(where, grad_attn, feed_pieces[1:])
-    out_chip, out_got = gate(out_chip, attn_pair), gate(out_got, attn_pair)
+    attn_pieces, _unused, _unused = scatter_start(where, grad_attn, feed_pieces[1:])
+    out_chip, out_got = gate(out_chip, feed_pieces[-1:]), gate(out_got, feed_pieces[-1:])
     out_terms = [out_chip, out_got, swap(out_chip, "tensor", 1), swap(out_got, "tensor", 1)]
     output, sign = stream(
-        output_kernel, [whole, small], [where, middle, *out_terms], near=(1,), far=(1,), here=range(2, 6), vmem=10, deps=attn_pair
+        output_kernel, [whole, small], [where, middle, *out_terms], near=(1,), far=(1,), here=range(2, 6), vmem=10
     )
     signs = [sign]
     terms = reduce_finish(chip, feed_pieces[1:])

time: 133 us -> 131 us (0.985)
  waiting for transfers between devices: 51.3 us -> 46.4 us
  Pallas kernels: 41.9 us -> 43.5 us
    ppermute x39, waiting for transfers between devices: 51.3 us -> 46.4 us  [swap(): return lax.ppermute(values, axis, [(i, i ^ mask) for i in range(count)])]
    pallas_call x8 -> x9, Pallas kernels: 35.6 us -> 37.1 us  [stream(): pl.pallas_call(body, out_shape=[jax.ShapeDtypeStruct(*out) if i in near e...]
  transfers between devices with their start and end apart: 39 -> 39, of which waited for: 15 -> 17; matrix products, arithmetic and copies ran while one was open for 1% -> 1% of each run, Pallas kernels for 26% -> 27%
where the time goes in v5:
time: 131 us; the launch traced here: 130 us
  waiting for transfers between devices  46.4 us (35%)
  Pallas kernels  43.5 us (33%)
  starting transfers between devices  37.1 us (28%)
  other arithmetic  1.69 us (1%)
    ppermute x39, waiting for transfers between devices, swap(): return lax.ppermute(values, axis, [(i, i ^ mask) for i in range(count)])  46.4 us
    pallas_call x9, Pallas kernels, stream(): pl.pallas_call(body, out_shape=[jax.ShapeDtypeStruct(*out) if i in near e...  37.1 us
    ppermute x39, starting transfers between devices, swap(): return lax.ppermute(values, axis, [(i, i ^ mask) for i in range(count)])  37.1 us
    pallas_call x10, Pallas kernels, call(): pl.pallas_call(body, out_shape=[jax.ShapeDtypeStruct(s, d) for s, d in ou...  5.43 us
  transfers between devices with their start and end apart: 39, of which 17 were waited for; matrix products, arithmetic and copies ran while one was open for 1% of the time, Pallas kernels for 27%

profile of v5, /device:TPU:0, one launch (start us, length us, event | category | flops | bytes accessed | tf_op | source)
XLA Modules:
  0.0 130.3 jit_solution(2498303433930751741)
XLA Ops:
  1.9 4.1 %collective-permute-start.1 = (bf16[96,896]{1,0:T(8,128)(2,1)S(1)}, bf16[96,896]{1,0:T(8,128)(2,1)S(1)}, u32[]{:S(2)}, u32[]{:S(2)}) collective-permute-start(bf16[96,896]{1,0:T(8,128)(2,1)S(1)} %shard_map.345.refs_5_), channel_id=1, source_target_pairs={{0,16},{4,20},{8,24},{12,28},{16,0},{20,4},{24,8},{28,12},{1,17},{... | collective-permute-start | bytes 516104 | tf_op jit(solution)/shard_map/ppermute | solution.py:52
  9.8 3.1 %collective-permute-done.3.refs_9_ = bf16[96,896]{1,0:T(8,128)(2,1)S(1)} collective-permute-done((bf16[96,896]{1,0:T(8,128)(2,1)S(1)}, bf16[96,896]{1,0:T(8,128)(2,1)S(1)}, u32[]{:S(2)}, u32[]{:S(2)}) %collective-permute-start.3) | collective-permute-done | bytes 172064 | tf_op jit(solution)/shard_map/ppermute | solution.py:52
  15.0 3.6 %collective-permute-done.1.refs_7_.refs_1_ = bf16[96,896]{1,0:T(8,128)(2,1)S(1)} collective-permute-done((bf16[96,896]{1,0:T(8,128)(2,1)S(1)}, bf16[96,896]{1,0:T(8,128)(2,1)S(1)}, u32[]{:S(2)}, u32[]{:S(2)}) %collective-permute-start.1) | collective-permute-done | bytes 172064 | tf_op jit(solution)/shard_map/ppermute | solution.py:52
  18.6 1.8 %collective-permute-start.5 = (bf16[96,896]{1,0:T(8,128)(2,1)S(1)}, bf16[96,896]{1,0:T(8,128)(2,1)S(1)}, u32[]{:S(2)}, u32[]{:S(2)}) collective-permute-start(bf16[96,896]{1,0:T(8,128)(2,1)S(1)} %collective-permute-done.1.refs_7_.refs_1_), channel_id=1, source_target_pairs={{0,4},{4,0},{8,12},{12,8},{16,20},{20,16},{24,28},{28,24},{1,5},{5... | collective-permute-start | bytes 516104 | tf_op jit(solution)/shard_map/ppermute | solution.py:52
  22.0 3.6 %collective-permute-start.7 = (bf16[96,896]{1,0:T(8,128)(2,1)S(1)}, bf16[96,896]{1,0:T(8,128)(2,1)S(1)}, u32[]{:S(2)}, u32[]{:S(2)}) collective-permute-start(bf16[96,896]{1,0:T(8,128)(2,1)S(1)} %shard_map.349.refs_7_), channel_id=1, source_target_pairs={{0,16},{4,20},{8,24},{12,28},{16,0},{20,4},{24,8},{28,12},{1,17},{... | collective-permute-start | bytes 516104 | tf_op jit(solution)/shard_map/ppermute | solution.py:52
  27.6 6.9 %shard_map.347 = (bf16[512,768]{1,0:T(8,128)(2,1)}, bf16[512,192]{1,0:T(8,128)(2,1)}, bf16[512,192]{1,0:T(8,128)(2,1)}, bf16[512,192]{1,0:T(8,128)(2,1)}, bf16[5...) custom-call(s32[2]{0:T(128)S(1)} %pad_add_fusion.refs_0_, ...), custom_call_target="tpu_custom_call" | custom-call | tf_op jit(solution)/shard_map/pallas_call | solution.py:286
  34.5 3.1 %collective-permute-done.7.refs_1_.refs_0_ = bf16[96,896]{1,0:T(8,128)(2,1)S(1)} collective-permute-done((bf16[96,896]{1,0:T(8,128)(2,1)S(1)}, bf16[96,896]{1,0:T(8,128)(2,1)S(1)}, u32[]{:S(2)}, u32[]{:S(2)}) %collective-permute-start.7) | collective-permute-done | bytes 172064 | tf_op jit(solution)/shard_map/ppermute | solution.py:52
  43.0 8.6 %collective-permute-done.12.refs_4_ = bf16[256,768]{1,0:T(8,128)(2,1)S(1)} collective-permute-done((bf16[256,768]{1,0:T(8,128)(2,1)S(1)}, bf16[256,768]{1,0:T(8,128)(2,1)S(1)}, u32[]{:S(2)}, u32[]{:S(2)}) %collective-permute-start.12) | collective-permute-done | bytes 393248 | tf_op jit(solution)/shard_map/ppermute | solution.py:52
  51.7 3.9 %collective-permute-done.15.refs_10_ = bf16[3,96,896]{2,1,0:T(8,128)(2,1)S(1)} collective-permute-done((bf16[3,96,896]{2,1,0:T(8,128)(2,1)S(1)}, bf16[3,96,896]{2,1,0:T(8,128)(2,1)S(1)}, u32[]{:S(2)}, u32[]{:S(2)}) %collective-permute-start.15) | collective-permute-done | bytes 516128 | tf_op jit(solution)/shard_map/ppermute | solution.py:52
  55.6 6.1 %shard_map.353 = (f32[512,768]{1,0:T(8,128)}, bf16[512,768]{1,0:T(8,128)(2,1)S(1)}, bf16[512,288]{1,0:T(8,128)(2,1)S(1)}, bf16[512,288]{1,0:T(8,128)(2,1)S(1)}, ...) custom-call(s32[2]{0:T(128)S(1)} %pad_add_fusion.refs_0_, ...), custom_call_target="tpu_custom_call" | custom-call | tf_op jit(solution)/shard_map/pallas_call | solution.py:286
  61.8 1.7 %collective-permute-done.16.refs_1_ = bf16[256,768]{1,0:T(8,128)(2,1)S(1)} collective-permute-done((bf16[256,768]{1,0:T(8,128)(2,1)S(1)}, bf16[256,768]{1,0:T(8,128)(2,1)S(1)}, u32[]{:S(2)}, u32[]{:S(2)}) %collective-permute-start.16) | collective-permute-done | bytes 393248 | tf_op jit(solution)/shard_map/ppermute | solution.py:52
  64.2 3.1 %shard_map.355 = (bf16[256,768]{1,0:T(8,128)(2,1)S(1)}, bf16[256,768]{1,0:T(8,128)(2,1)S(1)}, bf16[4,96,864]{2,1,0:T(8,128)(2,1)S(1)}, bf16[4,96,864]{2,1,0:T(8,128)(2,1)S(1)}) custom-call(s32[2]{0:T(128)S(1)} %pad_add_fusion.refs_0_, bf16[512,768]{1,0:T(8,128)(2,1)S(1)} %get-tuple-element.85.refs_1_, bf16[512,288]{1,0:T(8,128)(2,1)S(1)} %get-tuple-element.86.refs_2_, ...), custom_call_target="tpu_custom_call" | custom-call | tf_op jit(solution)/shard_map/pallas_call | solution.py:286
  68.9 2.8 %shard_map.356 = (bf16[4,768,192]{2,1,0:T(8,128)(2,1)S(1)}, bf16[3,512,512]{2,1,0:T(8,128)(2,1)S(1)}, bf16[3,512,512]{2,1,0:T(8,128)(2,1)S(1)}) custom-call(s32[2]{0:T(128)S(1)} %pad_add_fusion.refs_0_, bf16[768,896]{1,0:T(8,128)(2,1)} %get-tuple-element.94.refs_1_, bf16[512,192]{1,0:T(8,128)(2,1)} %get-tuple-element.95.refs_2_, ...), custom_call_target="tpu_custom_call" | custom-call | tf_op jit(solution)/shard_map/pallas_call | solution.py:286
  71.7 3.1 %collective-permute-done.18.refs_0_ = bf16[256,768]{1,0:T(8,128)(2,1)S(1)} collective-permute-done((bf16[256,768]{1,0:T(8,128)(2,1)S(1)}, bf16[256,768]{1,0:T(8,128)(2,1)S(1)}, u32[]{:S(2)}, u32[]{:S(2)}) %collective-permute-start.18) | collective-permute-done | bytes 393248 | tf_op jit(solution)/shard_map/ppermute | solution.py:52
  76.9 8.1 %shard_map.363 = (f32[512,768]{1,0:T(8,128)}, bf16[256,768]{1,0:T(8,128)(2,1)S(1)}, bf16[256,768]{1,0:T(8,128)(2,1)S(1)}, bf16[4,96,768]{2,1,0:T(8,128)(2,1)S(1)}, bf16[4,96,768]{2,1,0:T(8,128)(2,1)S(1)}) custom-call(s32[2]{0:T(128)S(1)} %pad_add_fusion.refs_0_, bf16[256,768]{1,0:T(8,128)(2,1)S(1)} %shard_map.354.refs_7_.refs_4_.refs_1_, ...), custom_call_target="tpu_custom_call" | custom-call | flops 1 | bytes 1 | tf_op jit(solution)/shard_map/pallas_call | solution.py:286
  89.7 2.6 %collective-permute-start.20 = (bf16[96,864]{1,0:T(8,128)(2,1)S(1)}, bf16[96,864]{1,0:T(8,128)(2,1)S(1)}, u32[]{:S(2)}, u32[]{:S(2)}) collective-permute-start(bf16[96,864]{1,0:T(8,128)(2,1)S(1)} %get-tuple-element.100), channel_id=1, source_target_pairs={{0,8},{4,12},{8,0},{12,4},{16,24},{20,28},{24,16},{28,20},{1,9},{5... | collective-permute-start | bytes 497672 | tf_op jit(solution)/shard_map/ppermute | solution.py:52
  92.3 3.2 %collective-permute-start.28 = (bf16[96,864]{1,0:T(8,128)(2,1)S(1)}, bf16[96,864]{1,0:T(8,128)(2,1)S(1)}, u32[]{:S(2)}, u32[]{:S(2)}) collective-permute-start(bf16[96,864]{1,0:T(8,128)(2,1)S(1)} %get-tuple-element.113), channel_id=1, source_target_pairs={{0,24},{4,28},{8,16},{12,20},{16,8},{20,12},{24,0},{28,4},{1,25},{... | collective-permute-start | bytes 497672 | tf_op jit(solution)/shard_map/ppermute | solution.py:52
  96.4 8.2 %collective-permute-done.28.refs_1_.refs_3_ = bf16[96,864]{1,0:T(8,128)(2,1)S(1)} collective-permute-done((bf16[96,864]{1,0:T(8,128)(2,1)S(1)}, bf16[96,864]{1,0:T(8,128)(2,1)S(1)}, u32[]{:S(2)}, u32[]{:S(2)}) %collective-permute-start.28) | collective-permute-done | bytes 165920 | tf_op jit(solution)/shard_map/ppermute | solution.py:52
  104.6 4.7 %collective-permute-done.29.refs_2_.refs_4_ = bf16[96,864]{1,0:T(8,128)(2,1)S(1)} collective-permute-done((bf16[96,864]{1,0:T(8,128)(2,1)S(1)}, bf16[96,864]{1,0:T(8,128)(2,1)S(1)}, u32[]{:S(2)}, u32[]{:S(2)}) %collective-permute-start.29) | collective-permute-done | bytes 165920 | tf_op jit(solution)/shard_map/ppermute | solution.py:52
  110.6 2.7 %collective-permute-start.33 = (bf16[96,768]{1,0:T(8,128)(2,1)S(1)}, bf16[96,768]{1,0:T(8,128)(2,1)S(1)}, u32[]{:S(2)}, u32[]{:S(2)}) collective-permute-start(bf16[96,768]{1,0:T(8,128)(2,1)S(1)} %get-tuple-element.119), channel_id=1, source_target_pairs={{0,24},{4,28},{8,16},{12,20},{16,8},{20,12},{24,0},{28,4},{1,25},{... | collective-permute-start | bytes 442376 | tf_op jit(solution)/shard_map/ppermute | solution.py:52
  113.4 1.7 %collective-permute-start.35 = (bf16[96,768]{1,0:T(8,128)(2,1)S(1)}, bf16[96,768]{1,0:T(8,128)(2,1)S(1)}, u32[]{:S(2)}, u32[]{:S(2)}) collective-permute-start(bf16[96,768]{1,0:T(8,128)(2,1)S(1)} %get-tuple-element.121), channel_id=1, source_target_pairs={{0,8},{4,12},{8,0},{12,4},{16,24},{20,28},{24,16},{28,20},{1,9},{5... | collective-permute-start | bytes 442376 | tf_op jit(solution)/shard_map/ppermute | solution.py:52
  115.4 1.7 %shard_map.370 = (f32[2,96,288]{2,1,0:T(8,128)}, f32[2,96,288]{2,1,0:T(8,128)}, f32[2,96,288]{2,1,0:T(8,128)}, f32[2,96,288]{2,1,0:T(8,128)}, f32[288,96]{1,0:T(...) custom-call(bf16[96,864]{1,0:T(8,128)(2,1)S(1)} %get-tuple-element.124.refs_0_.refs_2_, ...), custom_call_target="tpu_custom_call" | custom-call | tf_op jit(solution)/shard_map/pallas_call | solution.py:211
  117.1 3.3 %shard_map.362 = (f32[512,768]{1,0:T(8,128)}, f32[8,128]{1,0:T(8,128)S(1)}) custom-call(s32[2]{0:T(128)S(1)} %pad_add_fusion.refs_0_, f32[512,768]{1,0:T(8,128)} %get-tuple-element.84.refs_1_.refs_5_, bf16[256,768]{1,0:T(8,128)(2,1)S(1)} %shard_map.360.refs_2_, bf16[256,768]{1,0:T(8,128)(2,1)S(1)} %shard_map.361.refs_3_, ...), custom_call_target="tpu_custom_call" | custom-call | tf_op jit(solution)/shard_map/pallas_call | solution.py:286
  120.4 4.3 %shard_map.367 = (f32[512,768]{1,0:T(8,128)}, f32[8,128]{1,0:T(8,128)S(1)}) custom-call(s32[2]{0:T(128)S(1)} %pad_add_fusion.refs_0_, bf16[512,768]{1,0:T(8,128)(2,1)} %refs_1_.11, f32[512,768]{1,0:T(8,128)} %get-tuple-element.109.refs_2_, f32[8,768]{1,0:T(8,128)S(1)} %copy-done.19, bf16[256,768]{1,0:T(8,128)(2,1)S(1)} %shard_map.365.refs_4_, ...), custom_call_target="tpu_custom_call" | custom-call | tf_op jit(solution)/shard_map/pallas_call | solution.py:286
  (140 shorter events, 33.0 us)
Async XLA Ops:
  1.9 16.7 %collective-permute-start.1 = (bf16[96,896]{1,0:T(8,128)(2,1)S(1)}, bf16[96,896]{1,0:T(8,128)(2,1)S(1)}, u32[]{:S(2)}, u32[]{:S(2)}) collective-permute-start(bf16[96,896]{1,0:T(8,128)(2,1)S(1)} %shard_map.345.refs_5_), channel_id=1, source_target_pairs={{0,16},{4,20},{8,24},{12,28},{16,0},{20,4},{24,8},{28,12},{1,17},{... | collective-permute-start | bytes 516104 | tf_op jit(solution)/shard_map/ppermute | solution.py:52
  6.0 15.7 %collective-permute-start.2 = (bf16[96,896]{1,0:T(8,128)(2,1)S(1)}, bf16[96,896]{1,0:T(8,128)(2,1)S(1)}, u32[]{:S(2)}, u32[]{:S(2)}) collective-permute-start(bf16[96,896]{1,0:T(8,128)(2,1)S(1)} %shard_map.345.refs_5_), channel_id=1, source_target_pairs={{0,24},{4,28},{8,16},{12,20},{16,8},{20,12},{24,0},{28,4},{1,25},{... | collective-permute-start | bytes 516104 | tf_op jit(solution)/shard_map/ppermute | solution.py:52
  13.0 9.0 %collective-permute-start.4 = (bf16[96,896]{1,0:T(8,128)(2,1)S(1)}, bf16[96,896]{1,0:T(8,128)(2,1)S(1)}, u32[]{:S(2)}, u32[]{:S(2)}) collective-permute-start(bf16[96,896]{1,0:T(8,128)(2,1)S(1)} %shard_map.346), channel_id=1, source_target_pairs={{0,8},{4,12},{8,0},{12,4},{16,24},{20,28},{24,16},{28,20},{1,9},{5... | collective-permute-start | bytes 516104 | tf_op jit(solution)/shard_map/ppermute | solution.py:52
  13.5 12.6 %collective-permute-start = (bf16[96,896]{1,0:T(8,128)(2,1)S(1)}, bf16[96,896]{1,0:T(8,128)(2,1)S(1)}, u32[]{:S(2)}, u32[]{:S(2)}) collective-permute-start(bf16[96,896]{1,0:T(8,128)(2,1)S(1)} %shard_map.345.refs_5_), channel_id=1, source_target_pairs={{0,8},{4,12},{8,0},{12,4},{16,24},{20,28},{24,16},{28,20},{1,9},{5... | collective-permute-start | bytes 516104 | tf_op jit(solution)/shard_map/ppermute | solution.py:52
  22.0 15.6 %collective-permute-start.7 = (bf16[96,896]{1,0:T(8,128)(2,1)S(1)}, bf16[96,896]{1,0:T(8,128)(2,1)S(1)}, u32[]{:S(2)}, u32[]{:S(2)}) collective-permute-start(bf16[96,896]{1,0:T(8,128)(2,1)S(1)} %shard_map.349.refs_7_), channel_id=1, source_target_pairs={{0,16},{4,20},{8,24},{12,28},{16,0},{20,4},{24,8},{28,12},{1,17},{... | collective-permute-start | bytes 516104 | tf_op jit(solution)/shard_map/ppermute | solution.py:52
  25.6 12.0 %collective-permute-start.8 = (bf16[96,896]{1,0:T(8,128)(2,1)S(1)}, bf16[96,896]{1,0:T(8,128)(2,1)S(1)}, u32[]{:S(2)}, u32[]{:S(2)}) collective-permute-start(bf16[96,896]{1,0:T(8,128)(2,1)S(1)} %shard_map.349.refs_7_), channel_id=1, source_target_pairs={{0,24},{4,28},{8,16},{12,20},{16,8},{20,12},{24,0},{28,4},{1,25},{... | collective-permute-start | bytes 516104 | tf_op jit(solution)/shard_map/ppermute | solution.py:52
  26.1 12.6 %collective-permute-start.9 = (bf16[96,896]{1,0:T(8,128)(2,1)S(1)}, bf16[96,896]{1,0:T(8,128)(2,1)S(1)}, u32[]{:S(2)}, u32[]{:S(2)}) collective-permute-start(bf16[96,896]{1,0:T(8,128)(2,1)S(1)} %shard_map.349.refs_7_), channel_id=1, source_target_pairs={{0,8},{4,12},{8,0},{12,4},{16,24},{20,28},{24,16},{28,20},{1,9},{5... | collective-permute-start | bytes 516104 | tf_op jit(solution)/shard_map/ppermute | solution.py:52
  26.2 12.4 %collective-permute-start.10 = (bf16[96,896]{1,0:T(8,128)(2,1)S(1)}, bf16[96,896]{1,0:T(8,128)(2,1)S(1)}, u32[]{:S(2)}, u32[]{:S(2)}) collective-permute-start(bf16[96,896]{1,0:T(8,128)(2,1)S(1)} %shard_map.349.refs_7_), channel_id=1, source_target_pairs={{0,4},{4,0},{8,12},{12,8},{16,20},{20,16},{24,28},{28,24},{1,5},{5... | collective-permute-start | bytes 516104 | tf_op jit(solution)/shard_map/ppermute | solution.py:52
  40.5 11.2 %collective-permute-start.12 = (bf16[256,768]{1,0:T(8,128)(2,1)S(1)}, bf16[256,768]{1,0:T(8,128)(2,1)S(1)}, u32[]{:S(2)}, u32[]{:S(2)}) collective-permute-start(bf16[256,768]{1,0:T(8,128)(2,1)S(1)} %shard_map.352.refs_3_), channel_id=1, source_target_pairs={{0,2},{1,3},{2,0},{3,1},{4,6},{5,7},{6,4},{7,5},{8,10},{9,11},{10,... | collective-permute-start | bytes 1179656 | tf_op jit(solution)/shard_map/ppermute | solution.py:52
  42.0 13.5 %collective-permute-start.15 = (bf16[3,96,896]{2,1,0:T(8,128)(2,1)S(1)}, bf16[3,96,896]{2,1,0:T(8,128)(2,1)S(1)}, u32[]{:S(2)}, u32[]{:S(2)}) collective-permute-start(bf16[3,96,896]{2,1,0:T(8,128)(2,1)S(1)} %shard_map.351.refs_2_.refs_8_), channel_id=1, source_target_pairs={{0,4},{4,0},{8,12},{12,8},{16,20},{20,16},{24,28},{28,24},{1,5},{5... | collective-permute-start | bytes 1548296 | tf_op jit(solution)/shard_map/ppermute | solution.py:52
  43.0 12.5 %collective-permute-start.13 = (bf16[256,768]{1,0:T(8,128)(2,1)S(1)}, bf16[256,768]{1,0:T(8,128)(2,1)S(1)}, u32[]{:S(2)}, u32[]{:S(2)}) collective-permute-start(bf16[256,768]{1,0:T(8,128)(2,1)S(1)} %shard_map.352.refs_3_), channel_id=1, source_target_pairs={{0,1},{1,0},{2,3},{3,2},{4,5},{5,4},{6,7},{7,6},{8,9},{9,8},{10,11... | collective-permute-start | bytes 1179656 | tf_op jit(solution)/shard_map/ppermute | solution.py:52
  63.6 11.2 %collective-permute-start.18 = (bf16[256,768]{1,0:T(8,128)(2,1)S(1)}, bf16[256,768]{1,0:T(8,128)(2,1)S(1)}, u32[]{:S(2)}, u32[]{:S(2)}) collective-permute-start(bf16[256,768]{1,0:T(8,128)(2,1)S(1)} %shard_map.354.refs_7_.refs_4_.refs_1_), channel_id=1, source_target_pairs={{0,2},{1,3},{2,0},{3,1},{4,6},{5,7},{6,4},{7,5},{8,10},{9,11},{10,... | collective-permute-start | bytes 1179656 | tf_op jit(solution)/shard_map/ppermute | solution.py:52
  67.3 17.8 %collective-permute-start.19 = (bf16[4,96,864]{2,1,0:T(8,128)(2,1)S(1)}, bf16[4,96,864]{2,1,0:T(8,128)(2,1)S(1)}, u32[]{:S(2)}, u32[]{:S(2)}) collective-permute-start(bf16[4,96,864]{2,1,0:T(8,128)(2,1)S(1)} %get-tuple-element.99), channel_id=1, source_target_pairs={{0,4},{4,0},{8,12},{12,8},{16,20},{20,16},{24,28},{28,24},{1,5},{5... | collective-permute-start | bytes 1990664 | tf_op jit(solution)/shard_map/ppermute | solution.py:52
  75.0 11.6 %collective-permute-start.21 = (bf16[256,768]{1,0:T(8,128)(2,1)S(1)}, bf16[256,768]{1,0:T(8,128)(2,1)S(1)}, u32[]{:S(2)}, u32[]{:S(2)}) collective-permute-start(bf16[256,768]{1,0:T(8,128)(2,1)S(1)} %shard_map.358.refs_0_), channel_id=1, source_target_pairs={{0,2},{1,3},{2,0},{3,1},{4,6},{5,7},{6,4},{7,5},{8,10},{9,11},{10,... | collective-permute-start | bytes 1179656 | tf_op jit(solution)/shard_map/ppermute | solution.py:52
  87.0 22.3 %collective-permute-start.27 = (bf16[256,768]{1,0:T(8,128)(2,1)S(1)}, bf16[256,768]{1,0:T(8,128)(2,1)S(1)}, u32[]{:S(2)}, u32[]{:S(2)}) collective-permute-start(bf16[256,768]{1,0:T(8,128)(2,1)S(1)} %shard_map.365.refs_4_), channel_id=1, source_target_pairs={{0,2},{1,3},{2,0},{3,1},{4,6},{5,7},{6,4},{7,5},{8,10},{9,11},{10,... | collective-permute-start | bytes 1179656 | tf_op jit(solution)/shard_map/ppermute | solution.py:52
  88.0 22.0 %collective-permute-start.32 = (bf16[4,96,768]{2,1,0:T(8,128)(2,1)S(1)}, bf16[4,96,768]{2,1,0:T(8,128)(2,1)S(1)}, u32[]{:S(2)}, u32[]{:S(2)}) collective-permute-start(bf16[4,96,768]{2,1,0:T(8,128)(2,1)S(1)} %get-tuple-element.117), channel_id=1, source_target_pairs={{0,4},{4,0},{8,12},{12,8},{16,20},{20,16},{24,28},{28,24},{1,5},{5... | collective-permute-start | bytes 1769480 | tf_op jit(solution)/shard_map/ppermute | solution.py:52
  92.3 12.3 %collective-permute-start.28 = (bf16[96,864]{1,0:T(8,128)(2,1)S(1)}, bf16[96,864]{1,0:T(8,128)(2,1)S(1)}, u32[]{:S(2)}, u32[]{:S(2)}) collective-permute-start(bf16[96,864]{1,0:T(8,128)(2,1)S(1)} %get-tuple-element.113), channel_id=1, source_target_pairs={{0,24},{4,28},{8,16},{12,20},{16,8},{20,12},{24,0},{28,4},{1,25},{... | collective-permute-start | bytes 497672 | tf_op jit(solution)/shard_map/ppermute | solution.py:52
  95.5 13.8 %collective-permute-start.29 = (bf16[96,864]{1,0:T(8,128)(2,1)S(1)}, bf16[96,864]{1,0:T(8,128)(2,1)S(1)}, u32[]{:S(2)}, u32[]{:S(2)}) collective-permute-start(bf16[96,864]{1,0:T(8,128)(2,1)S(1)} %get-tuple-element.114), channel_id=1, source_target_pairs={{0,16},{4,20},{8,24},{12,28},{16,0},{20,4},{24,8},{28,12},{1,17},{... | collective-permute-start | bytes 497672 | tf_op jit(solution)/shard_map/ppermute | solution.py:52
  96.4 16.9 %collective-permute-start.22 = (bf16[256,768]{1,0:T(8,128)(2,1)S(1)}, bf16[256,768]{1,0:T(8,128)(2,1)S(1)}, u32[]{:S(2)}, u32[]{:S(2)}) collective-permute-start(bf16[256,768]{1,0:T(8,128)(2,1)S(1)} %shard_map.360.refs_2_), channel_id=1, source_target_pairs={{0,1},{1,0},{2,3},{3,2},{4,5},{5,4},{6,7},{7,6},{8,9},{9,8},{10,11... | collective-permute-start | bytes 1179656 | tf_op jit(solution)/shard_map/ppermute | solution.py:52
  109.3 11.0 %collective-permute-start.30 = (bf16[256,768]{1,0:T(8,128)(2,1)S(1)}, bf16[256,768]{1,0:T(8,128)(2,1)S(1)}, u32[]{:S(2)}, u32[]{:S(2)}) collective-permute-start(bf16[256,768]{1,0:T(8,128)(2,1)S(1)} %shard_map.365.refs_4_), channel_id=1, source_target_pairs={{0,1},{1,0},{2,3},{3,2},{4,5},{5,4},{6,7},{7,6},{8,9},{9,8},{10,11... | collective-permute-start | bytes 1179656 | tf_op jit(solution)/shard_map/ppermute | solution.py:52
  109.4 10.9 %collective-permute-start.31 = (bf16[256,768]{1,0:T(8,128)(2,1)S(1)}, bf16[256,768]{1,0:T(8,128)(2,1)S(1)}, u32[]{:S(2)}, u32[]{:S(2)}) collective-permute-start(bf16[256,768]{1,0:T(8,128)(2,1)S(1)} %shard_map.366.refs_5_), channel_id=1, source_target_pairs={{0,1},{1,0},{2,3},{3,2},{4,5},{5,4},{6,7},{7,6},{8,9},{9,8},{10,11... | collective-permute-start | bytes 1179656 | tf_op jit(solution)/shard_map/ppermute | solution.py:52
  110.6 14.1 %collective-permute-start.33 = (bf16[96,768]{1,0:T(8,128)(2,1)S(1)}, bf16[96,768]{1,0:T(8,128)(2,1)S(1)}, u32[]{:S(2)}, u32[]{:S(2)}) collective-permute-start(bf16[96,768]{1,0:T(8,128)(2,1)S(1)} %get-tuple-element.119), channel_id=1, source_target_pairs={{0,24},{4,28},{8,16},{12,20},{16,8},{20,12},{24,0},{28,4},{1,25},{... | collective-permute-start | bytes 442376 | tf_op jit(solution)/shard_map/ppermute | solution.py:52
  113.4 11.9 %collective-permute-start.34 = (bf16[96,768]{1,0:T(8,128)(2,1)S(1)}, bf16[96,768]{1,0:T(8,128)(2,1)S(1)}, u32[]{:S(2)}, u32[]{:S(2)}) collective-permute-start(bf16[96,768]{1,0:T(8,128)(2,1)S(1)} %get-tuple-element.120), channel_id=1, source_target_pairs={{0,16},{4,20},{8,24},{12,28},{16,0},{20,4},{24,8},{28,12},{1,17},{... | collective-permute-start | bytes 442376 | tf_op jit(solution)/shard_map/ppermute | solution.py:52
  113.4 11.9 %collective-permute-start.35 = (bf16[96,768]{1,0:T(8,128)(2,1)S(1)}, bf16[96,768]{1,0:T(8,128)(2,1)S(1)}, u32[]{:S(2)}, u32[]{:S(2)}) collective-permute-start(bf16[96,768]{1,0:T(8,128)(2,1)S(1)} %get-tuple-element.121), channel_id=1, source_target_pairs={{0,8},{4,12},{8,0},{12,4},{16,24},{20,28},{24,16},{28,20},{1,9},{5... | collective-permute-start | bytes 442376 | tf_op jit(solution)/shard_map/ppermute | solution.py:52
  (39 other events, 242.9 us)

commit v6 on v5

--- a/solution.py
+++ b/solution.py
@@ -727,8 +727,7 @@
         [where, tokens, segments.reshape(length, 1), segments, table, *pieces_a],
         [pltpu.VMEM((6, depth, heads), BF), pltpu.VMEM((repeat, length, heads), BF)],
         near=(7, 8),
-        far=(1,),
-        here=range(5, 5 + len(pieces_a)),
+        here=range(1, 5 + len(pieces_a)),
     )
     terms = reduce_finish(reduce_start(mine, gate(theirs, early) if early else theirs, later))
     middle, n2, z, du, dv2, gain_two, mine, theirs, wd = stream(
@@ -747,8 +746,7 @@
         [where, tokens, cotangent, *terms, *pieces_b],
         [pltpu.VMEM((depth, wide_b), BF), pltpu.VMEM((2, depth, hidden), BF)],
         near=(1, 2, 3, 4, 6, 7, 8),
-        far=(1, 2),
-        here=range(3, 7 + len(pieces_b)),
+        here=range(1, 7 + len(pieces_b)),
     )
     chip = reduce_start(mine, theirs)
     feed_outs = grad_outs(depth, 3 * hidden)
@@ -801,12 +799,12 @@
     out_chip, out_got = gate(out_chip, feed_pieces[-1:]), gate(out_got, feed_pieces[-1:])
     out_terms = [out_chip, out_got, swap(out_chip, "tensor", 1), swap(out_got, "tensor", 1)]
     output, sign = stream(
-        output_kernel, [whole, small], [where, middle, *out_terms], near=(1,), far=(1,), here=range(2, 6), vmem=10
+        output_kernel, [whole, small], [where, middle, *out_terms], near=(1,), here=range(1, 6), vmem=10
     )
     signs = [sign]
     terms = reduce_finish(chip, feed_pieces[1:])
     grad_tokens, sign = stream(
-        input_grad_kernel, [whole, small], [where, tokens, dh, gain_one, *terms], near=(1,), far=(1, 2), here=range(4, 8), vmem=10
+        input_grad_kernel, [whole, small], [where, tokens, dh, gain_one, *terms], near=(1,), here=range(1, 8), vmem=10
     )
     signs.append(sign)
 

time: 131 us -> 129 us (0.985)
  Pallas kernels: 43.5 us -> 38.3 us
  waiting for transfers between devices: 46.4 us -> 49.9 us
    pallas_call x9, Pallas kernels: 37.1 us -> 31.9 us  [stream(): pl.pallas_call(body, out_shape=[jax.ShapeDtypeStruct(*out) if i in near e...]
    ppermute x39, waiting for transfers between devices: 46.4 us -> 49.9 us  [swap(): return lax.ppermute(values, axis, [(i, i ^ mask) for i in range(count)])]
  transfers between devices with their start and end apart: 39 -> 39, of which waited for: 17 -> 17; matrix products, arithmetic and copies ran while one was open for 1% -> 1% of each run, Pallas kernels for 27% -> 25%
where the time goes in v6:
time: 129 us
  waiting for transfers between devices  49.9 us (39%)
  Pallas kernels  38.3 us (30%)
  starting transfers between devices  37.1 us (29%)
  other arithmetic  1.69 us (1%)
    ppermute x39, waiting for transfers between devices, swap(): return lax.ppermute(values, axis, [(i, i ^ mask) for i in range(count)])  49.9 us
    ppermute x39, starting transfers between devices, swap(): return lax.ppermute(values, axis, [(i, i ^ mask) for i in range(count)])  37.1 us
    pallas_call x9, Pallas kernels, stream(): pl.pallas_call(body, out_shape=[jax.ShapeDtypeStruct(*out) if i in near e...  31.9 us
    pallas_call x10, Pallas kernels, call(): pl.pallas_call(body, out_shape=[jax.ShapeDtypeStruct(s, d) for s, d in ou...  5.43 us
  transfers between devices with their start and end apart: 39, of which 17 were waited for; matrix products, arithmetic and copies ran while one was open for 1% of the time, Pallas kernels for 25%

profile of v6, /device:TPU:0, one launch (start us, length us, event | category | flops | bytes accessed | tf_op | source)
XLA Modules:
  0.0 128.7 jit_solution(3430504143518806453)
XLA Ops:
  1.9 4.1 %collective-permute-start.1 = (bf16[96,896]{1,0:T(8,128)(2,1)S(1)}, bf16[96,896]{1,0:T(8,128)(2,1)S(1)}, u32[]{:S(2)}, u32[]{:S(2)}) collective-permute-start(bf16[96,896]{1,0:T(8,128)(2,1)S(1)} %shard_map.345.refs_5_), channel_id=1, source_target_pairs={{0,16},{4,20},{8,24},{12,28},{16,0},{20,4},{24,8},{28,12},{1,17},{... | collective-permute-start | bytes 516104 | tf_op jit(solution)/shard_map/ppermute | solution.py:52
  9.9 3.1 %collective-permute-done.3.refs_9_ = bf16[96,896]{1,0:T(8,128)(2,1)S(1)} collective-permute-done((bf16[96,896]{1,0:T(8,128)(2,1)S(1)}, bf16[96,896]{1,0:T(8,128)(2,1)S(1)}, u32[]{:S(2)}, u32[]{:S(2)}) %collective-permute-start.3) | collective-permute-done | bytes 172064 | tf_op jit(solution)/shard_map/ppermute | solution.py:52
  15.1 3.6 %collective-permute-done.1.refs_7_.refs_1_ = bf16[96,896]{1,0:T(8,128)(2,1)S(1)} collective-permute-done((bf16[96,896]{1,0:T(8,128)(2,1)S(1)}, bf16[96,896]{1,0:T(8,128)(2,1)S(1)}, u32[]{:S(2)}, u32[]{:S(2)}) %collective-permute-start.1) | collective-permute-done | bytes 172064 | tf_op jit(solution)/shard_map/ppermute | solution.py:52
  18.6 1.8 %collective-permute-start.5 = (bf16[96,896]{1,0:T(8,128)(2,1)S(1)}, bf16[96,896]{1,0:T(8,128)(2,1)S(1)}, u32[]{:S(2)}, u32[]{:S(2)}) collective-permute-start(bf16[96,896]{1,0:T(8,128)(2,1)S(1)} %collective-permute-done.1.refs_7_.refs_1_), channel_id=1, source_target_pairs={{0,4},{4,0},{8,12},{12,8},{16,20},{20,16},{24,28},{28,24},{1,5},{5... | collective-permute-start | bytes 516104 | tf_op jit(solution)/shard_map/ppermute | solution.py:52
  22.0 3.6 %collective-permute-start.7 = (bf16[96,896]{1,0:T(8,128)(2,1)S(1)}, bf16[96,896]{1,0:T(8,128)(2,1)S(1)}, u32[]{:S(2)}, u32[]{:S(2)}) collective-permute-start(bf16[96,896]{1,0:T(8,128)(2,1)S(1)} %shard_map.349.refs_7_), channel_id=1, source_target_pairs={{0,16},{4,20},{8,24},{12,28},{16,0},{20,4},{24,8},{28,12},{1,17},{... | collective-permute-start | bytes 516104 | tf_op jit(solution)/shard_map/ppermute | solution.py:52
  27.6 6.4 %shard_map.347 = (bf16[512,768]{1,0:T(8,128)(2,1)}, bf16[512,192]{1,0:T(8,128)(2,1)}, bf16[512,192]{1,0:T(8,128)(2,1)}, bf16[512,192]{1,0:T(8,128)(2,1)}, bf16[5...) custom-call(s32[2]{0:T(128)S(1)} %pad_add_fusion.refs_0_, ...), custom_call_target="tpu_custom_call" | custom-call | tf_op jit(solution)/shard_map/pallas_call | solution.py:286
  34.0 3.6 %collective-permute-done.7.refs_1_.refs_0_ = bf16[96,896]{1,0:T(8,128)(2,1)S(1)} collective-permute-done((bf16[96,896]{1,0:T(8,128)(2,1)S(1)}, bf16[96,896]{1,0:T(8,128)(2,1)S(1)}, u32[]{:S(2)}, u32[]{:S(2)}) %collective-permute-start.7) | collective-permute-done | bytes 172064 | tf_op jit(solution)/shard_map/ppermute | solution.py:52
  43.1 8.6 %collective-permute-done.12.refs_4_ = bf16[256,768]{1,0:T(8,128)(2,1)S(1)} collective-permute-done((bf16[256,768]{1,0:T(8,128)(2,1)S(1)}, bf16[256,768]{1,0:T(8,128)(2,1)S(1)}, u32[]{:S(2)}, u32[]{:S(2)}) %collective-permute-start.12) | collective-permute-done | bytes 393248 | tf_op jit(solution)/shard_map/ppermute | solution.py:52
  51.7 3.9 %collective-permute-done.15.refs_10_ = bf16[3,96,896]{2,1,0:T(8,128)(2,1)S(1)} collective-permute-done((bf16[3,96,896]{2,1,0:T(8,128)(2,1)S(1)}, bf16[3,96,896]{2,1,0:T(8,128)(2,1)S(1)}, u32[]{:S(2)}, u32[]{:S(2)}) %collective-permute-start.15) | collective-permute-done | bytes 516128 | tf_op jit(solution)/shard_map/ppermute | solution.py:52
  55.6 4.5 %shard_map.353 = (f32[512,768]{1,0:T(8,128)}, bf16[512,768]{1,0:T(8,128)(2,1)S(1)}, bf16[512,288]{1,0:T(8,128)(2,1)S(1)}, bf16[512,288]{1,0:T(8,128)(2,1)S(1)}, ...) custom-call(s32[2]{0:T(128)S(1)} %pad_add_fusion.refs_0_, ...), custom_call_target="tpu_custom_call" | custom-call | tf_op jit(solution)/shard_map/pallas_call | solution.py:286
  60.2 1.7 %collective-permute-done.16.refs_1_ = bf16[256,768]{1,0:T(8,128)(2,1)S(1)} collective-permute-done((bf16[256,768]{1,0:T(8,128)(2,1)S(1)}, bf16[256,768]{1,0:T(8,128)(2,1)S(1)}, u32[]{:S(2)}, u32[]{:S(2)}) %collective-permute-start.16) | collective-permute-done | bytes 393248 | tf_op jit(solution)/shard_map/ppermute | solution.py:52
  62.6 3.1 %shard_map.355 = (bf16[256,768]{1,0:T(8,128)(2,1)S(1)}, bf16[256,768]{1,0:T(8,128)(2,1)S(1)}, bf16[4,96,864]{2,1,0:T(8,128)(2,1)S(1)}, bf16[4,96,864]{2,1,0:T(8,128)(2,1)S(1)}) custom-call(s32[2]{0:T(128)S(1)} %pad_add_fusion.refs_0_, bf16[512,768]{1,0:T(8,128)(2,1)S(1)} %get-tuple-element.85.refs_1_, bf16[512,288]{1,0:T(8,128)(2,1)S(1)} %get-tuple-element.86.refs_2_, ...), custom_call_target="tpu_custom_call" | custom-call | tf_op jit(solution)/shard_map/pallas_call | solution.py:286
  67.3 2.8 %shard_map.356 = (bf16[4,768,192]{2,1,0:T(8,128)(2,1)S(1)}, bf16[3,512,512]{2,1,0:T(8,128)(2,1)S(1)}, bf16[3,512,512]{2,1,0:T(8,128)(2,1)S(1)}) custom-call(s32[2]{0:T(128)S(1)} %pad_add_fusion.refs_0_, bf16[768,896]{1,0:T(8,128)(2,1)} %get-tuple-element.94.refs_1_, bf16[512,192]{1,0:T(8,128)(2,1)} %get-tuple-element.95.refs_2_, ...), custom_call_target="tpu_custom_call" | custom-call | tf_op jit(solution)/shard_map/pallas_call | solution.py:286
  70.1 3.1 %collective-permute-done.18.refs_0_ = bf16[256,768]{1,0:T(8,128)(2,1)S(1)} collective-permute-done((bf16[256,768]{1,0:T(8,128)(2,1)S(1)}, bf16[256,768]{1,0:T(8,128)(2,1)S(1)}, u32[]{:S(2)}, u32[]{:S(2)}) %collective-permute-start.18) | collective-permute-done | bytes 393248 | tf_op jit(solution)/shard_map/ppermute | solution.py:52
  75.4 8.1 %shard_map.363 = (f32[512,768]{1,0:T(8,128)}, bf16[256,768]{1,0:T(8,128)(2,1)S(1)}, bf16[256,768]{1,0:T(8,128)(2,1)S(1)}, bf16[4,96,768]{2,1,0:T(8,128)(2,1)S(1)}, bf16[4,96,768]{2,1,0:T(8,128)(2,1)S(1)}) custom-call(s32[2]{0:T(128)S(1)} %pad_add_fusion.refs_0_, bf16[256,768]{1,0:T(8,128)(2,1)S(1)} %shard_map.354.refs_7_.refs_4_.refs_1_, ...), custom_call_target="tpu_custom_call" | custom-call | flops 1 | bytes 1 | tf_op jit(solution)/shard_map/pallas_call | solution.py:286
  88.1 2.6 %collective-permute-start.20 = (bf16[96,864]{1,0:T(8,128)(2,1)S(1)}, bf16[96,864]{1,0:T(8,128)(2,1)S(1)}, u32[]{:S(2)}, u32[]{:S(2)}) collective-permute-start(bf16[96,864]{1,0:T(8,128)(2,1)S(1)} %get-tuple-element.100), channel_id=1, source_target_pairs={{0,8},{4,12},{8,0},{12,4},{16,24},{20,28},{24,16},{28,20},{1,9},{5... | collective-permute-start | bytes 497672 | tf_op jit(solution)/shard_map/ppermute | solution.py:52
  90.7 3.3 %collective-permute-start.28 = (bf16[96,864]{1,0:T(8,128)(2,1)S(1)}, bf16[96,864]{1,0:T(8,128)(2,1)S(1)}, u32[]{:S(2)}, u32[]{:S(2)}) collective-permute-start(bf16[96,864]{1,0:T(8,128)(2,1)S(1)} %get-tuple-element.113), channel_id=1, source_target_pairs={{0,24},{4,28},{8,16},{12,20},{16,8},{20,12},{24,0},{28,4},{1,25},{... | collective-permute-start | bytes 497672 | tf_op jit(solution)/shard_map/ppermute | solution.py:52
  94.8 8.2 %collective-permute-done.28.refs_1_.refs_3_ = bf16[96,864]{1,0:T(8,128)(2,1)S(1)} collective-permute-done((bf16[96,864]{1,0:T(8,128)(2,1)S(1)}, bf16[96,864]{1,0:T(8,128)(2,1)S(1)}, u32[]{:S(2)}, u32[]{:S(2)}) %collective-permute-start.28) | collective-permute-done | bytes 165920 | tf_op jit(solution)/shard_map/ppermute | solution.py:52
  103.0 4.7 %collective-permute-done.29.refs_2_.refs_4_ = bf16[96,864]{1,0:T(8,128)(2,1)S(1)} collective-permute-done((bf16[96,864]{1,0:T(8,128)(2,1)S(1)}, bf16[96,864]{1,0:T(8,128)(2,1)S(1)}, u32[]{:S(2)}, u32[]{:S(2)}) %collective-permute-start.29) | collective-permute-done | bytes 165920 | tf_op jit(solution)/shard_map/ppermute | solution.py:52
  109.1 2.7 %collective-permute-start.33 = (bf16[96,768]{1,0:T(8,128)(2,1)S(1)}, bf16[96,768]{1,0:T(8,128)(2,1)S(1)}, u32[]{:S(2)}, u32[]{:S(2)}) collective-permute-start(bf16[96,768]{1,0:T(8,128)(2,1)S(1)} %get-tuple-element.119), channel_id=1, source_target_pairs={{0,24},{4,28},{8,16},{12,20},{16,8},{20,12},{24,0},{28,4},{1,25},{... | collective-permute-start | bytes 442376 | tf_op jit(solution)/shard_map/ppermute | solution.py:52
  111.8 1.7 %collective-permute-start.35 = (bf16[96,768]{1,0:T(8,128)(2,1)S(1)}, bf16[96,768]{1,0:T(8,128)(2,1)S(1)}, u32[]{:S(2)}, u32[]{:S(2)}) collective-permute-start(bf16[96,768]{1,0:T(8,128)(2,1)S(1)} %get-tuple-element.121), channel_id=1, source_target_pairs={{0,8},{4,12},{8,0},{12,4},{16,24},{20,28},{24,16},{28,20},{1,9},{5... | collective-permute-start | bytes 442376 | tf_op jit(solution)/shard_map/ppermute | solution.py:52
  115.5 1.8 %shard_map.362 = (f32[512,768]{1,0:T(8,128)}, f32[8,128]{1,0:T(8,128)S(1)}) custom-call(s32[2]{0:T(128)S(1)} %pad_add_fusion.refs_0_, f32[512,768]{1,0:T(8,128)S(1)} %copy-done.3, bf16[256,768]{1,0:T(8,128)(2,1)S(1)} %shard_map.360.refs_2_, bf16[256,768]{1,0:T(8,128)(2,1)S(1)} %shard_map.361.refs_3_, bf16[256,768]{1,0:T(8,128)(2,1)S(1)} %collective-permute-done.22.refs_4_, ...), custom_call_target="tpu_custom_call" | custom-call | tf_op jit(solution)/shard_map/pallas_call | solution.py:286
  117.4 2.7 %shard_map.367 = (f32[512,768]{1,0:T(8,128)}, f32[8,128]{1,0:T(8,128)S(1)}) custom-call(s32[2]{0:T(128)S(1)} %pad_add_fusion.refs_0_, bf16[512,768]{1,0:T(8,128)(2,1)S(1)} %copy-done, f32[512,768]{1,0:T(8,128)S(1)} %copy-done.6, f32[8,768]{1,0:T(8,128)S(1)} %copy-done.22, bf16[256,768]{1,0:T(8,128)(2,1)S(1)} %shard_map.365.refs_4_, ...), custom_call_target="tpu_custom_call" | custom-call | tf_op jit(solution)/shard_map/pallas_call | solution.py:286
  120.2 3.5 %collective-permute-done.34.refs_2_.refs_4_ = bf16[96,768]{1,0:T(8,128)(2,1)S(1)} collective-permute-done((bf16[96,768]{1,0:T(8,128)(2,1)S(1)}, bf16[96,768]{1,0:T(8,128)(2,1)S(1)}, u32[]{:S(2)}, u32[]{:S(2)}) %collective-permute-start.34) | collective-permute-done | bytes 147488 | tf_op jit(solution)/shard_map/ppermute | solution.py:52
  (146 shorter events, 34.2 us)
Async XLA Ops:
  1.9 16.7 %collective-permute-start.1 = (bf16[96,896]{1,0:T(8,128)(2,1)S(1)}, bf16[96,896]{1,0:T(8,128)(2,1)S(1)}, u32[]{:S(2)}, u32[]{:S(2)}) collective-permute-start(bf16[96,896]{1,0:T(8,128)(2,1)S(1)} %shard_map.345.refs_5_), channel_id=1, source_target_pairs={{0,16},{4,20},{8,24},{12,28},{16,0},{20,4},{24,8},{28,12},{1,17},{... | collective-permute-start | bytes 516104 | tf_op jit(solution)/shard_map/ppermute | solution.py:52
  6.0 15.7 %collective-permute-start.2 = (bf16[96,896]{1,0:T(8,128)(2,1)S(1)}, bf16[96,896]{1,0:T(8,128)(2,1)S(1)}, u32[]{:S(2)}, u32[]{:S(2)}) collective-permute-start(bf16[96,896]{1,0:T(8,128)(2,1)S(1)} %shard_map.345.refs_5_), channel_id=1, source_target_pairs={{0,24},{4,28},{8,16},{12,20},{16,8},{20,12},{24,0},{28,4},{1,25},{... | collective-permute-start | bytes 516104 | tf_op jit(solution)/shard_map/ppermute | solution.py:52
  13.0 9.0 %collective-permute-start.4 = (bf16[96,896]{1,0:T(8,128)(2,1)S(1)}, bf16[96,896]{1,0:T(8,128)(2,1)S(1)}, u32[]{:S(2)}, u32[]{:S(2)}) collective-permute-start(bf16[96,896]{1,0:T(8,128)(2,1)S(1)} %shard_map.346), channel_id=1, source_target_pairs={{0,8},{4,12},{8,0},{12,4},{16,24},{20,28},{24,16},{28,20},{1,9},{5... | collective-permute-start | bytes 516104 | tf_op jit(solution)/shard_map/ppermute | solution.py:52
  13.5 12.6 %collective-permute-start = (bf16[96,896]{1,0:T(8,128)(2,1)S(1)}, bf16[96,896]{1,0:T(8,128)(2,1)S(1)}, u32[]{:S(2)}, u32[]{:S(2)}) collective-permute-start(bf16[96,896]{1,0:T(8,128)(2,1)S(1)} %shard_map.345.refs_5_), channel_id=1, source_target_pairs={{0,8},{4,12},{8,0},{12,4},{16,24},{20,28},{24,16},{28,20},{1,9},{5... | collective-permute-start | bytes 516104 | tf_op jit(solution)/shard_map/ppermute | solution.py:52
  22.0 15.6 %collective-permute-start.7 = (bf16[96,896]{1,0:T(8,128)(2,1)S(1)}, bf16[96,896]{1,0:T(8,128)(2,1)S(1)}, u32[]{:S(2)}, u32[]{:S(2)}) collective-permute-start(bf16[96,896]{1,0:T(8,128)(2,1)S(1)} %shard_map.349.refs_7_), channel_id=1, source_target_pairs={{0,16},{4,20},{8,24},{12,28},{16,0},{20,4},{24,8},{28,12},{1,17},{... | collective-permute-start | bytes 516104 | tf_op jit(solution)/shard_map/ppermute | solution.py:52
  25.6 12.0 %collective-permute-start.8 = (bf16[96,896]{1,0:T(8,128)(2,1)S(1)}, bf16[96,896]{1,0:T(8,128)(2,1)S(1)}, u32[]{:S(2)}, u32[]{:S(2)}) collective-permute-start(bf16[96,896]{1,0:T(8,128)(2,1)S(1)} %shard_map.349.refs_7_), channel_id=1, source_target_pairs={{0,24},{4,28},{8,16},{12,20},{16,8},{20,12},{24,0},{28,4},{1,25},{... | collective-permute-start | bytes 516104 | tf_op jit(solution)/shard_map/ppermute | solution.py:52
  26.1 12.6 %collective-permute-start.9 = (bf16[96,896]{1,0:T(8,128)(2,1)S(1)}, bf16[96,896]{1,0:T(8,128)(2,1)S(1)}, u32[]{:S(2)}, u32[]{:S(2)}) collective-permute-start(bf16[96,896]{1,0:T(8,128)(2,1)S(1)} %shard_map.349.refs_7_), channel_id=1, source_target_pairs={{0,8},{4,12},{8,0},{12,4},{16,24},{20,28},{24,16},{28,20},{1,9},{5... | collective-permute-start | bytes 516104 | tf_op jit(solution)/shard_map/ppermute | solution.py:52
  26.2 12.4 %collective-permute-start.10 = (bf16[96,896]{1,0:T(8,128)(2,1)S(1)}, bf16[96,896]{1,0:T(8,128)(2,1)S(1)}, u32[]{:S(2)}, u32[]{:S(2)}) collective-permute-start(bf16[96,896]{1,0:T(8,128)(2,1)S(1)} %shard_map.349.refs_7_), channel_id=1, source_target_pairs={{0,4},{4,0},{8,12},{12,8},{16,20},{20,16},{24,28},{28,24},{1,5},{5... | collective-permute-start | bytes 516104 | tf_op jit(solution)/shard_map/ppermute | solution.py:52
  40.5 11.2 %collective-permute-start.12 = (bf16[256,768]{1,0:T(8,128)(2,1)S(1)}, bf16[256,768]{1,0:T(8,128)(2,1)S(1)}, u32[]{:S(2)}, u32[]{:S(2)}) collective-permute-start(bf16[256,768]{1,0:T(8,128)(2,1)S(1)} %shard_map.352.refs_3_), channel_id=1, source_target_pairs={{0,2},{1,3},{2,0},{3,1},{4,6},{5,7},{6,4},{7,5},{8,10},{9,11},{10,... | collective-permute-start | bytes 1179656 | tf_op jit(solution)/shard_map/ppermute | solution.py:52
  42.1 13.5 %collective-permute-start.15 = (bf16[3,96,896]{2,1,0:T(8,128)(2,1)S(1)}, bf16[3,96,896]{2,1,0:T(8,128)(2,1)S(1)}, u32[]{:S(2)}, u32[]{:S(2)}) collective-permute-start(bf16[3,96,896]{2,1,0:T(8,128)(2,1)S(1)} %shard_map.351.refs_2_.refs_8_), channel_id=1, source_target_pairs={{0,4},{4,0},{8,12},{12,8},{16,20},{20,16},{24,28},{28,24},{1,5},{5... | collective-permute-start | bytes 1548296 | tf_op jit(solution)/shard_map/ppermute | solution.py:52
  43.1 12.5 %collective-permute-start.13 = (bf16[256,768]{1,0:T(8,128)(2,1)S(1)}, bf16[256,768]{1,0:T(8,128)(2,1)S(1)}, u32[]{:S(2)}, u32[]{:S(2)}) collective-permute-start(bf16[256,768]{1,0:T(8,128)(2,1)S(1)} %shard_map.352.refs_3_), channel_id=1, source_target_pairs={{0,1},{1,0},{2,3},{3,2},{4,5},{5,4},{6,7},{7,6},{8,9},{9,8},{10,11... | collective-permute-start | bytes 1179656 | tf_op jit(solution)/shard_map/ppermute | solution.py:52
  62.0 11.2 %collective-permute-start.18 = (bf16[256,768]{1,0:T(8,128)(2,1)S(1)}, bf16[256,768]{1,0:T(8,128)(2,1)S(1)}, u32[]{:S(2)}, u32[]{:S(2)}) collective-permute-start(bf16[256,768]{1,0:T(8,128)(2,1)S(1)} %shard_map.354.refs_7_.refs_4_.refs_1_), channel_id=1, source_target_pairs={{0,2},{1,3},{2,0},{3,1},{4,6},{5,7},{6,4},{7,5},{8,10},{9,11},{10,... | collective-permute-start | bytes 1179656 | tf_op jit(solution)/shard_map/ppermute | solution.py:52
  65.7 17.8 %collective-permute-start.19 = (bf16[4,96,864]{2,1,0:T(8,128)(2,1)S(1)}, bf16[4,96,864]{2,1,0:T(8,128)(2,1)S(1)}, u32[]{:S(2)}, u32[]{:S(2)}) collective-permute-start(bf16[4,96,864]{2,1,0:T(8,128)(2,1)S(1)} %get-tuple-element.99), channel_id=1, source_target_pairs={{0,4},{4,0},{8,12},{12,8},{16,20},{20,16},{24,28},{28,24},{1,5},{5... | collective-permute-start | bytes 1990664 | tf_op jit(solution)/shard_map/ppermute | solution.py:52
  73.4 11.6 %collective-permute-start.21 = (bf16[256,768]{1,0:T(8,128)(2,1)S(1)}, bf16[256,768]{1,0:T(8,128)(2,1)S(1)}, u32[]{:S(2)}, u32[]{:S(2)}) collective-permute-start(bf16[256,768]{1,0:T(8,128)(2,1)S(1)} %shard_map.358.refs_0_), channel_id=1, source_target_pairs={{0,2},{1,3},{2,0},{3,1},{4,6},{5,7},{6,4},{7,5},{8,10},{9,11},{10,... | collective-permute-start | bytes 1179656 | tf_op jit(solution)/shard_map/ppermute | solution.py:52
  85.4 22.4 %collective-permute-start.27 = (bf16[256,768]{1,0:T(8,128)(2,1)S(1)}, bf16[256,768]{1,0:T(8,128)(2,1)S(1)}, u32[]{:S(2)}, u32[]{:S(2)}) collective-permute-start(bf16[256,768]{1,0:T(8,128)(2,1)S(1)} %shard_map.365.refs_4_), channel_id=1, source_target_pairs={{0,2},{1,3},{2,0},{3,1},{4,6},{5,7},{6,4},{7,5},{8,10},{9,11},{10,... | collective-permute-start | bytes 1179656 | tf_op jit(solution)/shard_map/ppermute | solution.py:52
  86.4 22.0 %collective-permute-start.32 = (bf16[4,96,768]{2,1,0:T(8,128)(2,1)S(1)}, bf16[4,96,768]{2,1,0:T(8,128)(2,1)S(1)}, u32[]{:S(2)}, u32[]{:S(2)}) collective-permute-start(bf16[4,96,768]{2,1,0:T(8,128)(2,1)S(1)} %get-tuple-element.117), channel_id=1, source_target_pairs={{0,4},{4,0},{8,12},{12,8},{16,20},{20,16},{24,28},{28,24},{1,5},{5... | collective-permute-start | bytes 1769480 | tf_op jit(solution)/shard_map/ppermute | solution.py:52
  90.7 12.3 %collective-permute-start.28 = (bf16[96,864]{1,0:T(8,128)(2,1)S(1)}, bf16[96,864]{1,0:T(8,128)(2,1)S(1)}, u32[]{:S(2)}, u32[]{:S(2)}) collective-permute-start(bf16[96,864]{1,0:T(8,128)(2,1)S(1)} %get-tuple-element.113), channel_id=1, source_target_pairs={{0,24},{4,28},{8,16},{12,20},{16,8},{20,12},{24,0},{28,4},{1,25},{... | collective-permute-start | bytes 497672 | tf_op jit(solution)/shard_map/ppermute | solution.py:52
  94.0 13.8 %collective-permute-start.29 = (bf16[96,864]{1,0:T(8,128)(2,1)S(1)}, bf16[96,864]{1,0:T(8,128)(2,1)S(1)}, u32[]{:S(2)}, u32[]{:S(2)}) collective-permute-start(bf16[96,864]{1,0:T(8,128)(2,1)S(1)} %get-tuple-element.114), channel_id=1, source_target_pairs={{0,16},{4,20},{8,24},{12,28},{16,0},{20,4},{24,8},{28,12},{1,17},{... | collective-permute-start | bytes 497672 | tf_op jit(solution)/shard_map/ppermute | solution.py:52
  94.8 16.9 %collective-permute-start.22 = (bf16[256,768]{1,0:T(8,128)(2,1)S(1)}, bf16[256,768]{1,0:T(8,128)(2,1)S(1)}, u32[]{:S(2)}, u32[]{:S(2)}) collective-permute-start(bf16[256,768]{1,0:T(8,128)(2,1)S(1)} %shard_map.360.refs_2_), channel_id=1, source_target_pairs={{0,1},{1,0},{2,3},{3,2},{4,5},{5,4},{6,7},{7,6},{8,9},{9,8},{10,11... | collective-permute-start | bytes 1179656 | tf_op jit(solution)/shard_map/ppermute | solution.py:52
  107.8 9.6 %collective-permute-start.30 = (bf16[256,768]{1,0:T(8,128)(2,1)S(1)}, bf16[256,768]{1,0:T(8,128)(2,1)S(1)}, u32[]{:S(2)}, u32[]{:S(2)}) collective-permute-start(bf16[256,768]{1,0:T(8,128)(2,1)S(1)} %shard_map.365.refs_4_), channel_id=1, source_target_pairs={{0,1},{1,0},{2,3},{3,2},{4,5},{5,4},{6,7},{7,6},{8,9},{9,8},{10,11... | collective-permute-start | bytes 1179656 | tf_op jit(solution)/shard_map/ppermute | solution.py:52
  107.8 9.5 %collective-permute-start.31 = (bf16[256,768]{1,0:T(8,128)(2,1)S(1)}, bf16[256,768]{1,0:T(8,128)(2,1)S(1)}, u32[]{:S(2)}, u32[]{:S(2)}) collective-permute-start(bf16[256,768]{1,0:T(8,128)(2,1)S(1)} %shard_map.366.refs_5_), channel_id=1, source_target_pairs={{0,1},{1,0},{2,3},{3,2},{4,5},{5,4},{6,7},{7,6},{8,9},{9,8},{10,11... | collective-permute-start | bytes 1179656 | tf_op jit(solution)/shard_map/ppermute | solution.py:52
  109.1 11.1 %collective-permute-start.33 = (bf16[96,768]{1,0:T(8,128)(2,1)S(1)}, bf16[96,768]{1,0:T(8,128)(2,1)S(1)}, u32[]{:S(2)}, u32[]{:S(2)}) collective-permute-start(bf16[96,768]{1,0:T(8,128)(2,1)S(1)} %get-tuple-element.119), channel_id=1, source_target_pairs={{0,24},{4,28},{8,16},{12,20},{16,8},{20,12},{24,0},{28,4},{1,25},{... | collective-permute-start | bytes 442376 | tf_op jit(solution)/shard_map/ppermute | solution.py:52
  111.8 11.9 %collective-permute-start.34 = (bf16[96,768]{1,0:T(8,128)(2,1)S(1)}, bf16[96,768]{1,0:T(8,128)(2,1)S(1)}, u32[]{:S(2)}, u32[]{:S(2)}) collective-permute-start(bf16[96,768]{1,0:T(8,128)(2,1)S(1)} %get-tuple-element.120), channel_id=1, source_target_pairs={{0,16},{4,20},{8,24},{12,28},{16,0},{20,4},{24,8},{28,12},{1,17},{... | collective-permute-start | bytes 442376 | tf_op jit(solution)/shard_map/ppermute | solution.py:52
  111.8 11.9 %collective-permute-start.35 = (bf16[96,768]{1,0:T(8,128)(2,1)S(1)}, bf16[96,768]{1,0:T(8,128)(2,1)S(1)}, u32[]{:S(2)}, u32[]{:S(2)}) collective-permute-start(bf16[96,768]{1,0:T(8,128)(2,1)S(1)} %get-tuple-element.121), channel_id=1, source_target_pairs={{0,8},{4,12},{8,0},{12,4},{16,24},{20,28},{24,16},{28,20},{1,9},{5... | collective-permute-start | bytes 442376 | tf_op jit(solution)/shard_map/ppermute | solution.py:52
  (42 other events, 300.6 us)
